TPU v7x, 128 devices: a whole 4x4x4 slice. The times are simulated.
128 devices in a mesh: seq: 16 (over x_hi, y, core), blk: 8 (over x_lo, z).
Axes of the slice: x: 4 (x_hi: 2, x_lo: 2; x = x_hi * 2 + x_lo), y: 4, z: 4, core: 2. Of those that a mesh axis runs over, the one named last changes fastest.
Arguments:
- tokens: bfloat16 [16384, 1536], P(('seq', 'blk')), may hold values from -6 to 6
- boundary: int32 [16384], P(('seq', 'blk')), may hold values from 0 to 1, as said below
- heads_in: bfloat16 [1536, 3, 1536], P(None, None, 'blk')
- heads_out: bfloat16 [1536, 1536], P('blk'), may hold values from -0.15625 to 0.15625
- gate_up: bfloat16 [1536, 2, 4096], P(None, None, 'blk'), may hold values from -0.15625 to 0.15625
- down_weight: bfloat16 [4096, 1536], P('blk'), may hold values from -0.09375 to 0.09375
- widen: bfloat16 [1536, 4096], P(None, 'blk'), may hold values from -0.15625 to 0.15625
- heads_in_two: bfloat16 [4096, 3, 4096], P(None, None, 'blk')
- heads_out_two: bfloat16 [4096, 4096], P('blk'), may hold values from -0.09375 to 0.09375
Outputs:
- level_one: bfloat16 [16384, 1536], P(('seq', 'blk'))
- level_two: bfloat16 [8192, 4096], P('seq', 'blk')
Inputs may be any that keep to these rules, and one draw needn't show every extreme that they name: `boundary`: each aligned block of 1024 consecutive rows holds between 256 and 512 ones, and some block holds exactly 512.
All inputs are finite; a program needn't handle non-finite values.
Results may differ from a plain program's by a relative error of at most 0.04.
Values may be sent and summed in bfloat16 or wider, within the bound.
No kernel may reach another device: no remote copies, remote signals or barrier semaphores. Data moves between devices by JAX's collectives and lax.ppermute only.
A program may use at most 128 MiB of HBM per device.

v0:
```python
import jax
import jax.numpy as jnp
from jax import lax
from jax.experimental import pallas as pl
from jax.experimental.pallas import tpu as pltpu
from jax.sharding import PartitionSpec as P

D1 = 1536
H1 = 24
D2 = 4096
H2 = 32
WIN = 512
EXT = 16
SENT = 128 + EXT
BF16 = jnp.bfloat16
F32 = jnp.float32
MASKED = -1e30
SCORE_FACTOR = 128 ** (-0.5) * 1.4426950408889634

PLACES = ((0, 0), (1, 0), (0, 1), (0, 3), (0, 2), (1, 2), (1, 1), (1, 3))


def flip_x(value):
    return lax.ppermute(value, "blk", [(i, i ^ 4) for i in range(8)])


def turn_z(value, steps):
    return lax.ppermute(value, "blk", [(i, (i & 4) | ((i + steps) & 3)) for i in range(8)])


def gather_blk(own):
    across = flip_x(own)
    behind = turn_z(own, 1)
    ahead = turn_z(own, 3)
    first = jnp.concatenate([own, across], axis=0)
    second = jnp.concatenate([ahead, behind], axis=0)
    opposite = turn_z(first, 2)
    diagonal = flip_x(second)
    near = jnp.concatenate([first, second], axis=0)
    far = jnp.concatenate([opposite, diagonal], axis=0)
    return near, far


def reduce_first(far):
    count = far.shape[0] // 4
    return turn_z(far[: 2 * count], 2), flip_x(far[2 * count :])


def reduce_second(near, opposite, diagonal):
    count = near.shape[0] // 4

    def plus(block, other):
        return near[block * count : (block + 1) * count].astype(F32) + other.astype(F32)

    across = flip_x(plus(1, opposite[count:]).astype(BF16))
    behind = turn_z(plus(2, diagonal[:count]).astype(BF16), 1)
    ahead = turn_z(plus(3, diagonal[count:]).astype(BF16), 3)
    return (
        plus(0, opposite[:count])
        + across.astype(F32)
        + behind.astype(F32)
        + ahead.astype(F32)
    )


def reduce_blk(near, far):
    return reduce_second(near, *reduce_first(far))


def normalize(values):
    floats = values.astype(F32)
    return floats * lax.rsqrt(jnp.mean(floats * floats, axis=-1, keepdims=True) + 1e-06)


def dot(left, right):
    return jnp.dot(left, right, preferred_element_type=F32)


def dot_t(left, right):
    return lax.dot_general(left, right, (((1,), (1,)), ((), ())), preferred_element_type=F32)


def window_kernel(blocks, info, qkv, halo, before, out):
    rows, width, size, stride = 128, D1 // 8, D1 // H1, SENT
    key_count = WIN + rows
    i = lax.broadcasted_iota(jnp.int32, (rows, key_count), 0)
    j = lax.broadcasted_iota(jnp.int32, (rows, key_count), 1)
    band = (j > i) & (j <= i + WIN)
    seq_position = info[8]
    if before is not None:
        out[...] = before[...]
    for n in blocks:
        place = info[n]
        keys, values = [], []
        for k in range(n - 4, n + 1):
            if k >= 0:
                start = pl.multiple_of(info[k] * stride, 16)
                block = qkv[pl.ds(start, rows), :]
                keys.append(block[:, :width])
                values.append(block[:, width : 2 * width])
            else:
                block = halo[(k + 4) * rows : (k + 5) * rows, :]
                keys.append(block[:, :width])
                values.append(block[:, width:])
        keys = jnp.concatenate(keys, axis=0)
        values = jnp.concatenate(values, axis=0)
        queries = qkv[pl.ds(pl.multiple_of(place * stride, 16), rows), 2 * width :]
        allowed = band
        if n < 4:
            allowed = band & (j + ((n - 4) * rows + seq_position * 1024) >= 0)
        parts = []
        for h in range(width // size):
            cut = slice(h * size, (h + 1) * size)
            scores = lax.dot_general(
                queries[:, cut], keys[:, cut], (((1,), (1,)), ((), ())),
                preferred_element_type=F32,
            ) * size ** (-0.5)
            scores = jnp.where(allowed, scores, MASKED)
            largest = jnp.max(scores, axis=-1, keepdims=True)
            weights = jnp.exp(scores - largest)
            total = jnp.sum(weights, axis=-1, keepdims=True)
            parts.append(dot(weights.astype(BF16), values[:, cut]) / total)
        out[pl.ds(pl.multiple_of(place * rows, 16), rows), :] = jnp.concatenate(
            parts, axis=1
        ).astype(BF16)


def window_attend(info, qkv, halo=None, before=None):
    if halo is None:
        def kernel(info, qkv, out):
            window_kernel(range(4, 8), info, qkv, None, None, out)

        operands = (info, qkv)
    else:
        def kernel(info, qkv, halo, before, out):
            window_kernel(range(4), info, qkv, halo, before, out)

        operands = (info, qkv, halo, before)
    vmem = pl.BlockSpec(memory_space=pltpu.VMEM)
    return pl.pallas_call(
        kernel,
        out_shape=jax.ShapeDtypeStruct((1024, D1 // 8), BF16),
        in_specs=[pl.BlockSpec(memory_space=pltpu.SMEM)] + [vmem] * (len(operands) - 1),
        out_specs=vmem,
        compiler_params=pltpu.CompilerParams(vmem_limit_bytes=32 * 2**20),
        cost_estimate=pl.CostEstimate(
            flops=12 * 128 * 640 * 256, bytes_accessed=2 * 2**20, transcendentals=12 * 128 * 640
        ),
        name="window_late" if halo is None else "window_early",
    )(*operands)


def prepare_kernel(tokens, marks, out):
    floats = tokens[...].astype(F32)
    scale = lax.rsqrt(jnp.mean(floats * floats, axis=-1, keepdims=True) + 1e-06)
    out[:128, :] = (floats * scale).astype(BF16)
    out[128:, :] = jnp.zeros((EXT, D1), BF16)
    out[128:, :128] = jnp.broadcast_to(marks[...].astype(F32), (EXT, 128)).astype(BF16)


def prepare(tokens, marks):
    return pl.pallas_call(
        prepare_kernel,
        out_shape=jax.ShapeDtypeStruct((SENT, D1), BF16),
        in_specs=[pl.BlockSpec(memory_space=pltpu.VMEM)] * 2,
        out_specs=pl.BlockSpec(memory_space=pltpu.VMEM),
        name="prepare",
    )(tokens, marks)


def near_kernel(rows, weights, out):
    out[:, :384] = dot_t(rows[...], weights[192:, :]).astype(BF16)
    out[:, 384:] = dot_t(rows[...], weights[:192, :]).astype(BF16)


def far_kernel(info, near, rows, weights, out, edge):
    half = 4 * SENT
    out[:half, :] = near[...]
    out[half:, :384] = dot_t(rows[...], weights[192:, :]).astype(BF16)
    for k in range(4):
        start = pl.multiple_of(info[4 + k] * SENT, 16)
        edge[k * 128 : (k + 1) * 128, :] = out[pl.ds(start, 128), :384]
    out[half:, 384:] = dot_t(rows[...], weights[:192, :]).astype(BF16)


def project_one(rows, weights, info=None, near=None):
    vmem = pl.BlockSpec(memory_space=pltpu.VMEM)
    cost = pl.CostEstimate(flops=2 * 576 * 576 * D1, bytes_accessed=5 * 2**20, transcendentals=0)
    params = pltpu.CompilerParams(vmem_limit_bytes=24 * 2**20)
    if near is None:
        return pl.pallas_call(
            near_kernel,
            out_shape=jax.ShapeDtypeStruct((4 * SENT, 576), BF16),
            in_specs=[vmem] * 2,
            out_specs=vmem,
            compiler_params=params,
            cost_estimate=cost,
            name="project_near",
        )(rows, weights)
    return pl.pallas_call(
        far_kernel,
        out_shape=(
            jax.ShapeDtypeStruct((8 * SENT, 576), BF16), jax.ShapeDtypeStruct((WIN, 384), BF16)
        ),
        in_specs=[pl.BlockSpec(memory_space=pltpu.SMEM)] + [vmem] * 3,
        out_specs=(vmem, vmem),
        compiler_params=params,
        cost_estimate=cost,
        name="project_far",
    )(info, near, rows, weights)


def mlp_kernel(rows, gate, up, down, out):
    def some(step, _):
        cut = pl.ds(pl.multiple_of(step * 256, 256), 256)
        block = rows[cut, :]
        gated = dot(block, gate[...])
        hidden = gated / (1.0 + jnp.exp(-gated)) * dot(block, up[...])
        out[cut, :] = dot(hidden.astype(BF16), down[...]).astype(BF16)
        return 0

    lax.fori_loop(0, rows.shape[0] // 256, some, 0)


def mlp(rows, gate, up, down):
    return pl.pallas_call(
        mlp_kernel,
        out_shape=jax.ShapeDtypeStruct(rows.shape, BF16),
        in_specs=[pl.BlockSpec(memory_space=pltpu.VMEM)] * 4,
        out_specs=pl.BlockSpec(memory_space=pltpu.VMEM),
        compiler_params=pltpu.CompilerParams(vmem_limit_bytes=32 * 2**20),
        cost_estimate=pl.CostEstimate(
            flops=2 * 512 * 1536 * 1536, bytes_accessed=8 * 2**20, transcendentals=512 * 512
        ),
        name="mlp",
    )(rows, gate, up, down)


def project_kernel(info, pooled, *refs):
    pieces, (weights, valid, chunks, pairs, wide_own, total, squares) = refs[:16], refs[16:]
    step = pl.program_id(0)
    y = info[8]

    @pl.when(step == 0)
    def _():
        total[...] = jnp.zeros_like(total)
        squares[...] = jnp.zeros_like(squares)

    wide = jnp.zeros((512, 512), F32)
    for k in range(4):
        rows = jnp.concatenate([piece[...] for piece in pieces[4 * k : 4 * k + 4]], axis=0)
        wide += dot(pooled[:, k * 384 : (k + 1) * 384], rows)
    wide = wide.astype(BF16)
    floats = wide.astype(F32)
    squares[...] += jnp.broadcast_to(
        jnp.sum(floats * floats, axis=-1, keepdims=True), squares.shape
    )
    for i in range(3):
        total[:, i * 512 : (i + 1) * 512] += dot(wide, weights[i])

    @pl.when(step == 0)
    def _():
        for p in range(8):
            start = pl.multiple_of(info[p] * 64, 64)
            wide_own[pl.ds(start, 64), :] = wide[p * 64 : (p + 1) * 64]

    @pl.when(step == 7)
    def _():
        scale = lax.rsqrt(squares[...] / D2 + 1e-06)
        for k in range(4):
            head = (y + k) & 3
            for i in range(3):
                cut = slice(i * 128, (i + 1) * 128)
                lanes = pl.ds(pl.multiple_of(i * 512 + head * 128, 128), 128)
                part = total[:, lanes] * (scale * SCORE_FACTOR if i == 0 else scale)
                part = part.astype(BF16)
                for p in range(8):
                    start = pl.multiple_of(info[p] * 64, 64)
                    chunks[k, pl.ds(start, 64), cut] = part[p * 64 : (p + 1) * 64]
                    if i > 0:
                        pairs[k, pl.ds(start, 64), (i - 1) * 128 : i * 128] = part[p * 64 : (p + 1) * 64]
                chunks[k, 512:, cut] = valid[...]
                if i > 0:
                    pairs[k, 512:, (i - 1) * 128 : i * 128] = valid[...]


def project_two(info, pooled, pieces, weights, valid):
    return pl.pallas_call(
        project_kernel,
        out_shape=(
            jax.ShapeDtypeStruct((4, 512 + EXT, 384), BF16),
            jax.ShapeDtypeStruct((4, 512 + EXT, 256), BF16),
            jax.ShapeDtypeStruct((512, 512), BF16),
        ),
        grid_spec=pltpu.PrefetchScalarGridSpec(
            num_scalar_prefetch=1,
            grid=(8,),
            in_specs=[
                pl.BlockSpec((512, D1), lambda s, info: (0, 0)),
                *[pl.BlockSpec((96, 512), lambda s, info, h=h: (8 * h + s, 0)) for _ in range(8) for h in range(2)],
                pl.BlockSpec((3, 512, 512), lambda s, info: (0, info[s], 0)),
                pl.BlockSpec((EXT, 128), lambda s, info: (0, 0)),
            ],
            out_specs=(
                pl.BlockSpec((4, 512 + EXT, 384), lambda s, info: (0, 0, 0)),
                pl.BlockSpec((4, 512 + EXT, 256), lambda s, info: (0, 0, 0)),
                pl.BlockSpec((512, 512), lambda s, info: (0, 0)),
            ),
            scratch_shapes=[pltpu.VMEM((512, 1536), F32), pltpu.VMEM((512, 128), F32)],
        ),
        compiler_params=pltpu.CompilerParams(vmem_limit_bytes=40 * 2**20),
        cost_estimate=pl.CostEstimate(
            flops=4 * 512 * 4096 * 1536, bytes_accessed=28 * 2**20, transcendentals=512
        ),
        name="project_two",
    )(info, pooled, *[piece for piece in pieces for _ in range(2)], weights, valid)


def causal_kernel(own_part, info, queries, kv, start, start_stats, out, out_stats, keys, values, even, odd):
    half, core, y = info[0], info[1], info[2]
    slot = pl.program_id(0)
    own_pair = (y + slot) & 3

    @pl.when(slot == 0)
    def _():
        def prepare(block, _):
            count = jnp.sum(kv[block, 512 : 512 + EXT, :128].astype(F32))
            row = lax.broadcasted_iota(jnp.int32, (512, 128), 0).astype(F32)
            lane = lax.broadcasted_iota(jnp.int32, (512, 128), 1)
            keys[block, :, :128] = kv[block, :512, :128]
            keys[block, :, 128:] = jnp.where((lane == 0) & (row >= count), MASKED, 0.0).astype(BF16)
            values[block] = kv[block, :512, 128:].T
            return 0

        lax.fori_loop(0, 8, prepare, 0)

    lane = lax.broadcasted_iota(jnp.int32, (512, 128), 1)
    query = jnp.concatenate([queries[0], jnp.where(lane == 0, 1.0, 0.0).astype(BF16)], axis=1)

    def block_of(pair, which):
        return (which ^ core) * 4 + ((pair - y) & 3)

    def scores_of(pair, which):
        return lax.dot_general(
            keys[block_of(pair, which)], query, (((1,), (1,)), ((), ())), preferred_element_type=F32
        )

    def absorb(scores, pair, which, carry, edge):
        largest, total, sums = carry
        if edge:
            key = lax.broadcasted_iota(jnp.int32, scores.shape, 0) + which * 512
            own = lax.broadcasted_iota(jnp.int32, scores.shape, 1) + core * 512
            scores = jnp.where(key <= own, scores, MASKED)
        new_largest = jnp.maximum(largest, jnp.max(scores, axis=0, keepdims=True))
        decay = jnp.exp2(largest - new_largest)
        weights = jnp.exp2(scores - new_largest)
        total = total * decay + jnp.sum(weights, axis=0, keepdims=True)
        sums = sums * decay + dot(values[block_of(pair, which)], weights.astype(BF16))
        return new_largest, total, sums

    even[...] = scores_of(0, 0)

    def both(pair, carry, edge=False):
        odd[...] = scores_of(pair, 1)
        carry = absorb(even[...], pair, 0, carry, edge)
        if not edge:
            even[...] = scores_of((pair + 1) & 3, 0)
        return absorb(odd[...], pair, 1, carry, edge)

    if own_part:
        carry = (
            jnp.full((1, 512), MASKED, F32), jnp.zeros((1, 512), F32), jnp.zeros((128, 512), F32)
        )
        carry = lax.fori_loop(0, own_pair, both, carry)
        largest, total, sums = both(own_pair, carry, True)
        out[0] = sums
        out_stats[0] = jnp.concatenate([largest, total, jnp.zeros((6, 512), F32)], axis=0)
    else:
        carry = (start_stats[0, 0:1], start_stats[0, 1:2], start[0])
        _, total, sums = lax.fori_loop(0, half * 4, both, carry)
        out[0] = (sums / total).T.astype(BF16)


def causal_attend(own_part, info, queries, kv, start=None):
    def by_slot(*shape):
        return pl.BlockSpec((1, *shape), lambda s, info: (s, 0, 0))

    sums_shape = jax.ShapeDtypeStruct((4, 128, 512), F32)
    stats_shape = jax.ShapeDtypeStruct((4, 8, 512), F32)
    in_specs = [by_slot(512, 128), pl.BlockSpec((8, 512 + EXT, 256), lambda s, info: (0, 0, 0))]
    operands = [queries, kv]
    if own_part:
        def kernel(info, queries, kv, out, out_stats, *scratch):
            causal_kernel(True, info, queries, kv, None, None, out, out_stats, *scratch)

        out_shape = (sums_shape, stats_shape)
        out_specs = (by_slot(128, 512), by_slot(8, 512))
        tiles = 18
    else:
        def kernel(info, queries, kv, start, start_stats, out, *scratch):
            causal_kernel(False, info, queries, kv, start, start_stats, out, None, *scratch)

        out_shape = jax.ShapeDtypeStruct((4, 512, 128), BF16)
        out_specs = by_slot(512, 128)
        in_specs += [by_slot(128, 512), by_slot(8, 512)]
        operands += list(start)
        tiles = 32
    return pl.pallas_call(
        kernel,
        out_shape=out_shape,
        grid_spec=pltpu.PrefetchScalarGridSpec(
            num_scalar_prefetch=1,
            grid=(4,),
            in_specs=in_specs,
            out_specs=out_specs,
            scratch_shapes=[
                pltpu.VMEM((8, 512, 256), BF16),
                pltpu.VMEM((8, 128, 512), BF16),
                pltpu.VMEM((512, 512), F32),
                pltpu.VMEM((512, 512), F32),
            ],
        ),
        compiler_params=pltpu.CompilerParams(vmem_limit_bytes=40 * 2**20),
        cost_estimate=pl.CostEstimate(
            flops=tiles * 512 * 512 * 512, bytes_accessed=4 * 2**20, transcendentals=tiles * 2**18
        ),
        name="causal_own" if own_part else "causal_first_half",
    )(info, *operands)


def turn_y(value, steps, first=0):
    return lax.ppermute(
        value, "seq", [(i, (i & 9) | ((i + 2 * steps) & 6)) for i in range(first, 16)]
    )


def flip_seq(value, bit):
    return lax.ppermute(value, "seq", [(i, i ^ bit) for i in range(16)])


def per_device(
    tokens, boundary, heads_in, heads_out, gate_up, down_weight, widen, heads_in_two, heads_out_two
):
    seq_position = lax.axis_index("seq")
    me = lax.axis_index("blk")
    rows = tokens.shape[0]
    capacity = 512
    width = D1 // 8
    block_of = jnp.stack([((me ^ (4 * x)) & 4) | ((me + z) & 3) for x, z in PLACES])
    numbers = jnp.arange(8, dtype=jnp.int32)
    place_of = jnp.sum(
        jnp.where(block_of[None, :] == numbers[:, None], numbers[None, :], 0), axis=1
    )

    def later(number, value):
        return number + (value[0, 0].astype(F32) * 0.0).astype(number.dtype)

    heads_in_flat = heads_in.transpose(1, 2, 0).reshape(3 * width, D1)
    gate_flat, up_flat = lax.optimization_barrier((gate_up[:, 0, :], gate_up[:, 1, :]))
    core, y, half = seq_position & 1, (seq_position >> 1) & 3, seq_position >> 3
    piece = lax.dynamic_slice(widen, (seq_position * 96, 0), (96, 512))

    near, far = gather_blk(prepare(tokens, boundary[None, :]))
    piece_here = jnp.concatenate(gather_blk(piece), axis=0)
    piece_across = flip_seq(piece_here, 8)
    marks = jnp.concatenate(
        [part.reshape(4, SENT, D1)[:, rows, :rows] for part in (near, far)], axis=0
    )
    info = later(jnp.concatenate([place_of, seq_position[None]]).astype(jnp.int32), gate_flat)
    qkv, edge = project_one(far, heads_in_flat, info, project_one(near, heads_in_flat))
    halo = lax.ppermute(edge, "seq", [(i, i + 1) for i in range(15)])
    attended = window_attend(info, qkv, halo, window_attend(info, qkv))
    attn_near = dot(attended[: 4 * rows], heads_out).astype(BF16)
    attn_far = dot(attended[4 * rows :], heads_out).astype(BF16)
    piece_pair = later(
        jnp.concatenate([piece_here, piece_across, jnp.zeros((EXT, 512), BF16)], axis=0), attended
    )
    pieces = [piece_pair, turn_y(piece_pair, 3), turn_y(piece_pair, 2), turn_y(piece_pair, 1)]
    mid_stream = (tokens.astype(F32) + reduce_blk(attn_near, attn_far)).astype(BF16)

    normed_mid = normalize(mid_stream).astype(BF16)

    near, far = gather_blk(normed_mid)
    mlp_near = mlp(near, gate_flat, up_flat, down_weight)
    mlp_far = mlp(far, gate_flat, up_flat, down_weight)
    marks = marks.astype(F32)
    counts = jnp.sum(marks, axis=1)
    before = jnp.sum(
        jnp.where(block_of[None, :] < block_of[:, None], counts[None, :], 0.0), axis=1
    )
    steps = jnp.arange(rows)
    running = dot(marks.astype(BF16), (steps[:, None] <= steps[None, :]).astype(BF16))
    slots = jnp.where(marks > 0.5, before[:, None] + running - 1.0, -1.0).astype(jnp.int32)
    span_count = jnp.sum(counts).astype(jnp.int32)
    targets = (block_of[:, None] * 64 + jnp.arange(64)[None, :]).reshape(capacity, 1)
    selector = (slots.reshape(1, 8 * rows) == targets).astype(BF16)
    placed = (
        dot(selector[:, : 4 * rows], mlp_near)
        + dot(selector[:, 4 * rows :], mlp_far)
        + dot(selector[:, :rows], mid_stream)
    ).astype(BF16)
    pooled_own = reduce_blk(placed[:256], placed[256:]).astype(BF16)
    unread = later(jnp.zeros((EXT, 512), BF16), pooled_own)
    pieces[1:] = [lax.dynamic_update_slice(part, unread, (1536, 0)) for part in pieces[1:]]
    pieces = [part for own in pieces for part in (own, flip_seq(own, 1))]
    pooled_own = jnp.concatenate(
        [
            lax.dynamic_slice(
                pooled_own, (0, 96 * ((half ^ h) * 8 + ((y + k) & 3) * 2 + (core ^ c))), (64, 96)
            )
            for k in range(4)
            for c in range(2)
            for h in range(2)
        ],
        axis=1,
    )
    pooled = jnp.concatenate(gather_blk(pooled_own), axis=0)

    far = later(mlp_far, pooled)
    opposite, diagonal = reduce_first(far)
    level_one = (mid_stream.astype(F32) + reduce_second(mlp_near, opposite, diagonal)).astype(BF16)

    validity = (jnp.arange(capacity, dtype=jnp.int32) < span_count).astype(F32)
    valid_rows = jnp.pad(
        validity.reshape(4, 128).astype(BF16), ((0, EXT - 4), (0, 0))
    )
    info_one = jnp.concatenate([block_of, y[None]]).astype(jnp.int32)
    chunks, pairs, wide_cols = project_two(
        info_one, pooled, pieces, heads_in_two.transpose(1, 0, 2), valid_rows
    )
    from_behind = turn_y(chunks[1], 1)
    from_ahead = turn_y(chunks[3], 3)
    from_opposite = turn_y(chunks[2], 2)
    first = lax.ppermute(pairs, "seq", [(i, i + 8) for i in range(8)])
    mine = jnp.stack([chunks[0], from_ahead, from_opposite, from_behind])
    queries, own_kv = mine[:, :capacity, :128], mine[:, :, 128:]
    own_pair = jnp.concatenate([own_kv, flip_seq(own_kv, 1)], axis=0)
    first_kv = jnp.stack(
        [first[0], turn_y(first[3], 3, 8), turn_y(first[2], 2, 8), turn_y(first[1], 1, 8)]
    )
    info_two = jnp.stack([half, core, y]).astype(jnp.int32)
    running = causal_attend(True, later(info_two, opposite), queries, own_pair)
    unread = jnp.broadcast_to(running[1][0:1, 2:3, :128], (1, EXT, 128)).astype(BF16)
    first_kv = lax.dynamic_update_slice(first_kv, unread, (0, capacity, 128))
    first_pair = jnp.concatenate([first_kv, flip_seq(first_kv, 1)], axis=0)
    mixed = causal_attend(False, later(info_two, level_one), queries, first_pair, running)
    back = [mixed[0], turn_y(mixed[3], 3), turn_y(mixed[2], 2), turn_y(mixed[1], 1)]
    heads = jnp.concatenate([back[0], back[1], back[2], back[3]] * 2, axis=1)
    attended_two = lax.dynamic_slice(heads, (0, ((4 - y) & 3) * 128), (capacity, 512))

    def columns(place):
        part = lax.dynamic_slice(heads_out_two, (0, block_of[place] * 512), (512, 512))
        return dot(attended_two, part).astype(BF16)

    out_far = jnp.concatenate([columns(place) for place in range(4, 8)], axis=0)
    out_near = jnp.concatenate([columns(place) for place in range(4)], axis=0)
    level_two = (
        (wide_cols.astype(F32) + reduce_blk(out_near, out_far)) * validity[:, None]
    ).astype(BF16)
    return (level_one, level_two)


def solution(mesh):
    placed = (
        P(("seq", "blk"), None),
        P(("seq", "blk")),
        P(None, None, "blk"),
        P("blk", None),
        P(None, None, "blk"),
        P("blk", None),
        P(None, "blk"),
        P(None, None, "blk"),
        P("blk", None),
    )
    return jax.shard_map(
        per_device,
        mesh=mesh,
        in_specs=placed,
        out_specs=(P(("seq", "blk"), None), P("seq", "blk")),
        check_vma=False,
    )
```

profile of v0, /device:TPU:6, one launch (start us, length us, event | category | flops | bytes accessed | tf_op | source)
XLA Modules:
  0.0 436.3 jit_solution(7302073473934096941)
XLA Ops:
  12.3 7.9 %fusion.59 = (bf16[1536,1,512]{2,1,0:T(2,128)(2,1)S(1)}, bf16[1536,1,512]{2,1,0:T(2,128)(2,1)S(1)}) fusion(bf16[1536,2,512]{2,1,0:T(2,128)(2,1)} %param.13), kind=kLoop, calls=%fused_computation.192 | loop fusion | bytes 6291456 | tf_op jit(solution)/shard_map/slice | solution.py:459
  32.1 15.1 %collective-permute-done.3 = bf16[288,1536]{1,0:T(8,128)(2,1)S(1)} collective-permute-done((bf16[288,1536]{1,0:T(8,128)(2,1)S(1)}, bf16[288,1536]{1,0:T(8,128)(2,1)S(1)}, u32[]{:S(2)}, u32[]{:S(2)}) %collective-permute-start.3) | collective-permute-done | bytes 884768 | tf_op jit(solution)/shard_map/ppermute | solution.py:28
  60.0 4.7 %window_late.1.before = bf16[1024,192]{1,0:T(8,128)(2,1)S(1)} custom-call(s32[9]{0:T(128)S(1)} %add_add_fusion.info, bf16[1152,576]{1,0:T(8,128)(2,1)S(1)} %copy-done.4), custom_call_target="tpu_custom_call" | custom-call | flops 251658240 | bytes 2097152 | tf_op jit(solution)/shard_map/window_late/pallas_call | solution.py:140
  66.5 4.8 %window_early.1 = bf16[1024,192]{1,0:T(8,128)(2,1)S(1)} custom-call(s32[9]{0:T(128)S(1)} %add_add_fusion.info, bf16[1152,576]{1,0:T(8,128)(2,1)S(1)} %copy-done.4, bf16[512,384]{1,0:T(8,128)(2,1)S(1)} %copy-done.11, bf16[1024,192]{1,0:T(8,128)(2,1)S(1)} %window_late.1.before), custom_call_target="tpu_custom_call" | custom-call | flops 251658240 | bytes 2097152 | tf_op jit(solution)/shard_map/window_early/pallas_call | solution.py:140
  78.3 14.1 %collective-permute-done.8 = bf16[256,1536]{1,0:T(8,128)(2,1)S(1)} collective-permute-done((bf16[256,1536]{1,0:T(8,128)(2,1)S(1)}, bf16[256,1536]{1,0:T(8,128)(2,1)S(1)}, u32[]{:S(2)}, u32[]{:S(2)}) %collective-permute-start.8) | collective-permute-done | bytes 786464 | tf_op jit(solution)/shard_map/ppermute | solution.py:24
  95.4 3.0 collective-permute-start.10
  99.3 9.4 %collective-permute-done.36 = bf16[768,512]{1,0:T(8,128)(2,1)S(1)} collective-permute-done((bf16[768,512]{1,0:T(8,128)(2,1)S(1)}, bf16[768,512]{1,0:T(8,128)(2,1)S(1)}, u32[]{:S(2)}, u32[]{:S(2)}) %collective-permute-start.36) | collective-permute-done | bytes 786464 | tf_op jit(solution)/shard_map/ppermute | solution.py:438
  110.4 7.3 %collective-permute-done.7 = bf16[128,1536]{1,0:T(8,128)(2,1)S(1)} collective-permute-done((bf16[128,1536]{1,0:T(8,128)(2,1)S(1)}, bf16[128,1536]{1,0:T(8,128)(2,1)S(1)}, u32[]{:S(2)}, u32[]{:S(2)}) %collective-permute-start.7) | collective-permute-done | bytes 393248 | tf_op jit(solution)/shard_map/ppermute | solution.py:24
  124.6 6.0 %collective-permute-done.13 = bf16[128,1536]{1,0:T(8,128)(2,1)S(1)} collective-permute-done((bf16[128,1536]{1,0:T(8,128)(2,1)S(1)}, bf16[128,1536]{1,0:T(8,128)(2,1)S(1)}, u32[]{:S(2)}, u32[]{:S(2)}) %collective-permute-start.13) | collective-permute-done | bytes 393248 | tf_op jit(solution)/shard_map/ppermute | solution.py:28
  137.8 3.0 mlp.2
  140.8 8.9 %collective-permute-done.15 = bf16[256,1536]{1,0:T(8,128)(2,1)S(1)} collective-permute-done((bf16[256,1536]{1,0:T(8,128)(2,1)S(1)}, bf16[256,1536]{1,0:T(8,128)(2,1)S(1)}, u32[]{:S(2)}, u32[]{:S(2)}) %collective-permute-start.15) | collective-permute-done | bytes 786464 | tf_op jit(solution)/shard_map/ppermute | solution.py:24
  152.4 3.0 mlp.3
  161.2 3.6 collective-permute-start.40
  185.8 13.2 %collective-permute-done.38 = bf16[1552,512]{1,0:T(8,128)(2,1)} collective-permute-done((bf16[1552,512]{1,0:T(8,128)(2,1)S(1)}, bf16[1552,512]{1,0:T(8,128)(2,1)}, u32[]{:S(2)}, u32[]{:S(2)}) %collective-permute-start.38) | collective-permute-done | bytes 1589280 | tf_op jit(solution)/shard_map/ppermute | solution.py:432
  203.0 27.9 %collective-permute-done.42 = bf16[1552,512]{1,0:T(8,128)(2,1)} collective-permute-done((bf16[1552,512]{1,0:T(8,128)(2,1)S(1)}, bf16[1552,512]{1,0:T(8,128)(2,1)}, u32[]{:S(2)}, u32[]{:S(2)}) %collective-permute-start.42) | collective-permute-done | bytes 1589280 | tf_op jit(solution)/shard_map/ppermute | solution.py:432
  233.3 6.9 %collective-permute-done.28 = bf16[64,1536]{1,0:T(8,128)(2,1)S(1)} collective-permute-done((bf16[64,1536]{1,0:T(8,128)(2,1)S(1)}, bf16[64,1536]{1,0:T(8,128)(2,1)S(1)}, u32[]{:S(2)}, u32[]{:S(2)}) %collective-permute-start.28) | collective-permute-done | bytes 196640 | tf_op jit(solution)/shard_map/ppermute | solution.py:28
  240.6 11.4 %collective-permute-done.29 = bf16[128,1536]{1,0:T(8,128)(2,1)S(1)} collective-permute-done((bf16[128,1536]{1,0:T(8,128)(2,1)S(1)}, bf16[128,1536]{1,0:T(8,128)(2,1)S(1)}, u32[]{:S(2)}, u32[]{:S(2)}) %collective-permute-start.29) | collective-permute-done | bytes 393248 | tf_op jit(solution)/shard_map/ppermute | solution.py:28
  253.4 8.0 %collective-permute-done.30 = bf16[128,1536]{1,0:T(8,128)(2,1)S(1)} collective-permute-done((bf16[128,1536]{1,0:T(8,128)(2,1)S(1)}, bf16[128,1536]{1,0:T(8,128)(2,1)S(1)}, u32[]{:S(2)}, u32[]{:S(2)}) %collective-permute-start.30) | collective-permute-done | bytes 393248 | tf_op jit(solution)/shard_map/ppermute | solution.py:24
  262.6 22.2 %project_two.1 = (bf16[4,528,384]{2,1,0:T(8,128)(2,1)}, bf16[4,528,256]{2,1,0:T(8,128)(2,1)S(1)}, bf16[512,512]{1,0:T(8,128)(2,1)S(1)}) custom-call(s32[9]{0:T(128)S(1)} %concatenate.93.info, bf16[512,1536]{1,0:T(8,128)(2,1)S(1)} %constant_dynamic-update-slice_fusion.2.pooled, bf16[1552,512]{1,0:T(8,128)(2,1)S(1)} %broadcast_add_fusion.refs_0_.refs_1_, ...), custom_call_target="tpu_custom_call" | custom-call | flops 12884901888 | bytes 29360128 | tf_op jit(solution)/shard_map/project_two/pallas_call | solution.py:288
  287.7 4.4 %collective-permute-start.46 = (bf16[528,384]{1,0:T(8,128)(2,1)S(1)}, bf16[528,384]{1,0:T(8,128)(2,1)S(1)}, u32[]{:S(2)}, u32[]{:S(2)}) collective-permute-start(bf16[528,384]{1,0:T(8,128)(2,1)S(1)} %get-tuple-element.37), channel_id=1, source_target_pairs={{0,16},{8,24},{16,32},{24,40},{32,48},{40,56},{48,0},{56,8},{64,80... | collective-permute-start | bytes 1216520 | tf_op jit(solution)/shard_map/ppermute | solution.py:432
  296.2 5.9 %collective-permute-done.46 = bf16[528,384]{1,0:T(8,128)(2,1)S(1)} collective-permute-done((bf16[528,384]{1,0:T(8,128)(2,1)S(1)}, bf16[528,384]{1,0:T(8,128)(2,1)S(1)}, u32[]{:S(2)}, u32[]{:S(2)}) %collective-permute-start.46) | collective-permute-done | bytes 405536 | tf_op jit(solution)/shard_map/ppermute | solution.py:432
  305.0 5.0 %collective-permute-done.45 = bf16[528,384]{1,0:T(8,128)(2,1)S(1)} collective-permute-done((bf16[528,384]{1,0:T(8,128)(2,1)S(1)}, bf16[528,384]{1,0:T(8,128)(2,1)S(1)}, u32[]{:S(2)}, u32[]{:S(2)}) %collective-permute-start.45) | collective-permute-done | bytes 405536 | tf_op jit(solution)/shard_map/ppermute | solution.py:432
  311.3 6.5 %collective-permute-done.47 = bf16[4,528,256]{2,1,0:T(8,128)(2,1)S(1)} collective-permute-done((bf16[4,528,256]{2,1,0:T(8,128)(2,1)S(1)}, bf16[4,528,256]{2,1,0:T(8,128)(2,1)S(1)}, u32[]{:S(2)}, u32[]{:S(2)}) %collective-permute-start.47) | collective-permute-done | bytes 1081376 | tf_op jit(solution)/shard_map/ppermute | solution.py:534
  317.9 3.5 collective-permute-start.50
  321.4 5.6 %collective-permute-start.49 = (bf16[528,256]{1,0:T(8,128)(2,1)S(1)}, bf16[528,256]{1,0:T(8,128)(2,1)S(1)}, u32[]{:S(2)}, u32[]{:S(2)}) collective-permute-start(bf16[528,256]{1,0:T(8,128)(2,1)S(1)} %get-tuple-element.51), channel_id=1, source_target_pairs={{64,96},{72,104},{80,112},{88,120},{96,64},{104,72},{112,80},{120,... | collective-permute-start | bytes 811016 | tf_op jit(solution)/shard_map/ppermute | solution.py:432
  336.7 11.4 %causal_own.1 = (f32[4,128,512]{2,1,0:T(8,128)S(1)}, f32[4,8,512]{2,1,0:T(8,128)S(1)}) custom-call(s32[3]{0:T(128)S(1)} %get-tuple-element.22.info, bf16[4,512,128]{2,1,0:T(8,128)(2,1)S(1)} %pad_maximum_fusion.15.queries, bf16[8,528,256]{2,1,0:T(8,128)(2,1)S(1)} %pad_maximum_fusion.kv), custom_call_target="tpu_custom_call" | custom-call | flops 2415919104 | bytes 4194304 | tf_op jit(solution)/shard_map/causal_own/pallas_call | solution.py:408
  353.6 16.8 %causal_first_half.1 = bf16[4,512,128]{2,1,0:T(8,128)(2,1)S(1)} custom-call(s32[3]{0:T(128)S(1)} %broadcast_add_fusion.3.info, bf16[4,512,128]{2,1,0:T(8,128)(2,1)S(1)} %pad_maximum_fusion.15.queries, bf16[8,528,256]{2,1,0:T(8,128)(2,1)S(1)} %pad_maximum_fusion.1.kv, f32[4,128,512]{2,1,0:T(8,128)S(1)} %get-tuple-element.19.start, ...), custom_call_target="tpu_custom_call" | custom-call | flops 4294967296 | bytes 4194304 | tf_op jit(solution)/shard_map/causal_first_half/pallas_call | solution.py:408
  373.4 3.4 collective-permute-done.53
  392.2 19.2 %collective-permute-done.58 = bf16[1024,512]{1,0:T(8,128)(2,1)} collective-permute-done((bf16[1024,512]{1,0:T(8,128)(2,1)}, bf16[1024,512]{1,0:T(8,128)(2,1)}, u32[]{:S(2)}, u32[]{:S(2)}) %collective-permute-start.58) | collective-permute-done | bytes 1048608 | tf_op jit(solution)/shard_map/ppermute | solution.py:24
  421.1 5.0 %collective-permute-done.60 = bf16[512,512]{1,0:T(8,128)(2,1)S(1)} collective-permute-done((bf16[512,512]{1,0:T(8,128)(2,1)S(1)}, bf16[512,512]{1,0:T(8,128)(2,1)S(1)}, u32[]{:S(2)}, u32[]{:S(2)}) %collective-permute-start.60) | collective-permute-done | bytes 524320 | tf_op jit(solution)/shard_map/ppermute | solution.py:28
  426.1 4.0 collective-permute-done.59
  432.8 3.1 multiply_convert_fusion
  (253 shorter events, 155.6 us)
Async XLA Ops:
  2.6 22.2 %collective-permute-start.2 = (bf16[144,1536]{1,0:T(8,128)(2,1)}, bf16[144,1536]{1,0:T(8,128)(2,1)S(1)}, u32[]{:S(2)}, u32[]{:S(2)}) collective-permute-start(bf16[144,1536]{1,0:T(8,128)(2,1)} %prepare.1), channel_id=1, source_target_pairs={{0,1},{1,2},{2,3},{3,0},{4,5},{5,6},{6,7},{7,4},{8,9},{9,10},{10,1... | collective-permute-start | bytes 1327112 | tf_op jit(solution)/shard_map/ppermute | solution.py:28
  4.6 22.2 %collective-permute-start.1 = (bf16[144,1536]{1,0:T(8,128)(2,1)}, bf16[144,1536]{1,0:T(8,128)(2,1)}, u32[]{:S(2)}, u32[]{:S(2)}) collective-permute-start(bf16[144,1536]{1,0:T(8,128)(2,1)} %prepare.1), channel_id=1, source_target_pairs={{0,3},{1,0},{2,1},{3,2},{4,7},{5,4},{6,5},{7,6},{8,11},{9,8},{10,9... | collective-permute-start | bytes 1327112 | tf_op jit(solution)/shard_map/ppermute | solution.py:28
  9.1 44.3 %collective-permute-start.31 = (bf16[96,512]{1,0:T(8,128)(2,1)S(1)}, bf16[96,512]{1,0:T(8,128)(2,1)}, u32[]{:S(2)}, u32[]{:S(2)}) collective-permute-start(bf16[96,512]{1,0:T(8,128)(2,1)S(1)} %get-tuple-element.25), channel_id=1, source_target_pairs={{0,4},{1,5},{2,6},{3,7},{4,0},{5,1},{6,2},{7,3},{8,12},{9,13},{10,... | collective-permute-start | bytes 294920 | tf_op jit(solution)/shard_map/ppermute | solution.py:24
  10.3 46.1 %collective-permute-start.32 = (bf16[96,512]{1,0:T(8,128)(2,1)S(1)}, bf16[96,512]{1,0:T(8,128)(2,1)S(1)}, u32[]{:S(2)}, u32[]{:S(2)}) collective-permute-start(bf16[96,512]{1,0:T(8,128)(2,1)S(1)} %get-tuple-element.25), channel_id=1, source_target_pairs={{0,3},{1,0},{2,1},{3,2},{4,7},{5,4},{6,5},{7,6},{8,11},{9,8},{10,9... | collective-permute-start | bytes 294920 | tf_op jit(solution)/shard_map/ppermute | solution.py:28
  23.7 32.7 %collective-permute-start.33 = (bf16[96,512]{1,0:T(8,128)(2,1)S(1)}, bf16[96,512]{1,0:T(8,128)(2,1)}, u32[]{:S(2)}, u32[]{:S(2)}) collective-permute-start(bf16[96,512]{1,0:T(8,128)(2,1)S(1)} %get-tuple-element.25), channel_id=1, source_target_pairs={{0,1},{1,2},{2,3},{3,0},{4,5},{5,6},{6,7},{7,4},{8,9},{9,10},{10,1... | collective-permute-start | bytes 294920 | tf_op jit(solution)/shard_map/ppermute | solution.py:28
  24.9 22.4 %collective-permute-start.3 = (bf16[288,1536]{1,0:T(8,128)(2,1)S(1)}, bf16[288,1536]{1,0:T(8,128)(2,1)S(1)}, u32[]{:S(2)}, u32[]{:S(2)}) collective-permute-start(bf16[288,1536]{1,0:T(8,128)(2,1)S(1)} %pad_maximum_fusion.11), channel_id=1, source_target_pairs={{0,2},{1,3},{2,0},{3,1},{4,6},{5,7},{6,4},{7,5},{8,10},{9,11},{10,... | collective-permute-start | bytes 2654216 | tf_op jit(solution)/shard_map/ppermute | solution.py:28
  27.9 19.5 %collective-permute-start.4 = (bf16[288,1536]{1,0:T(8,128)(2,1)S(1)}, bf16[288,1536]{1,0:T(8,128)(2,1)S(1)}, u32[]{:S(2)}, u32[]{:S(2)}) collective-permute-start(bf16[288,1536]{1,0:T(8,128)(2,1)S(1)} %pad_maximum_fusion.12), channel_id=1, source_target_pairs={{0,4},{1,5},{2,6},{3,7},{4,0},{5,1},{6,2},{7,3},{8,12},{9,13},{10,... | collective-permute-start | bytes 2654216 | tf_op jit(solution)/shard_map/ppermute | solution.py:24
  54.3 22.7 %collective-permute-start.34 = (bf16[192,512]{1,0:T(8,128)(2,1)S(1)}, bf16[192,512]{1,0:T(8,128)(2,1)S(1)}, u32[]{:S(2)}, u32[]{:S(2)}) collective-permute-start(bf16[192,512]{1,0:T(8,128)(2,1)S(1)} %pad_maximum_fusion.18), channel_id=1, source_target_pairs={{0,2},{1,3},{2,0},{3,1},{4,6},{5,7},{6,4},{7,5},{8,10},{9,11},{10,... | collective-permute-start | bytes 589832 | tf_op jit(solution)/shard_map/ppermute | solution.py:28
  57.3 19.8 %collective-permute-start.35 = (bf16[192,512]{1,0:T(8,128)(2,1)S(1)}, bf16[192,512]{1,0:T(8,128)(2,1)S(1)}, u32[]{:S(2)}, u32[]{:S(2)}) collective-permute-start(bf16[192,512]{1,0:T(8,128)(2,1)S(1)} %pad_maximum_fusion.19), channel_id=1, source_target_pairs={{0,4},{1,5},{2,6},{3,7},{4,0},{5,1},{6,2},{7,3},{8,12},{9,13},{10,... | collective-permute-start | bytes 589832 | tf_op jit(solution)/shard_map/ppermute | solution.py:24
  72.0 20.3 %collective-permute-start.8 = (bf16[256,1536]{1,0:T(8,128)(2,1)S(1)}, bf16[256,1536]{1,0:T(8,128)(2,1)S(1)}, u32[]{:S(2)}, u32[]{:S(2)}) collective-permute-start(bf16[256,1536]{1,0:T(8,128)(2,1)S(1)} %get-tuple-element.48), channel_id=1, source_target_pairs={{0,4},{1,5},{2,6},{3,7},{4,0},{5,1},{6,2},{7,3},{8,12},{9,13},{10,... | collective-permute-start | bytes 2359304 | tf_op jit(solution)/shard_map/ppermute | solution.py:24
  73.3 21.8 %collective-permute-start.6 = (bf16[256,1536]{1,0:T(8,128)(2,1)S(1)}, bf16[256,1536]{1,0:T(8,128)(2,1)S(1)}, u32[]{:S(2)}, u32[]{:S(2)}) collective-permute-start(bf16[256,1536]{1,0:T(8,128)(2,1)S(1)} %get-tuple-element.47), channel_id=1, source_target_pairs={{0,2},{1,3},{2,0},{3,1},{4,6},{5,7},{6,4},{7,5},{8,10},{9,11},{10,... | collective-permute-start | bytes 2359304 | tf_op jit(solution)/shard_map/ppermute | solution.py:28
  77.1 31.6 %collective-permute-start.36 = (bf16[768,512]{1,0:T(8,128)(2,1)S(1)}, bf16[768,512]{1,0:T(8,128)(2,1)S(1)}, u32[]{:S(2)}, u32[]{:S(2)}) collective-permute-start(bf16[768,512]{1,0:T(8,128)(2,1)S(1)} %get-tuple-element.58), channel_id=1, source_target_pairs={{0,64},{8,72},{16,80},{24,88},{32,96},{40,104},{48,112},{56,120},{... | collective-permute-start | bytes 2359304 | tf_op jit(solution)/shard_map/ppermute | solution.py:438
  98.4 19.2 %collective-permute-start.7 = (bf16[128,1536]{1,0:T(8,128)(2,1)S(1)}, bf16[128,1536]{1,0:T(8,128)(2,1)S(1)}, u32[]{:S(2)}, u32[]{:S(2)}) collective-permute-start(bf16[128,1536]{1,0:T(8,128)(2,1)S(1)} %get-tuple-element.46), channel_id=1, source_target_pairs={{0,4},{1,5},{2,6},{3,7},{4,0},{5,1},{6,2},{7,3},{8,12},{9,13},{10,... | collective-permute-start | bytes 1179656 | tf_op jit(solution)/shard_map/ppermute | solution.py:24
  130.7 19.0 %collective-permute-start.15 = (bf16[256,1536]{1,0:T(8,128)(2,1)S(1)}, bf16[256,1536]{1,0:T(8,128)(2,1)S(1)}, u32[]{:S(2)}, u32[]{:S(2)}) collective-permute-start(bf16[256,1536]{1,0:T(8,128)(2,1)S(1)} %pad_maximum_fusion.14), channel_id=1, source_target_pairs={{0,4},{1,5},{2,6},{3,7},{4,0},{5,1},{6,2},{7,3},{8,12},{9,13},{10,... | collective-permute-start | bytes 2359304 | tf_op jit(solution)/shard_map/ppermute | solution.py:24
  132.6 19.7 %collective-permute-start.14 = (bf16[256,1536]{1,0:T(8,128)(2,1)S(1)}, bf16[256,1536]{1,0:T(8,128)(2,1)S(1)}, u32[]{:S(2)}, u32[]{:S(2)}) collective-permute-start(bf16[256,1536]{1,0:T(8,128)(2,1)S(1)} %pad_maximum_fusion.13), channel_id=1, source_target_pairs={{0,2},{1,3},{2,0},{3,1},{4,6},{5,7},{6,4},{7,5},{8,10},{9,11},{10,... | collective-permute-start | bytes 2359304 | tf_op jit(solution)/shard_map/ppermute | solution.py:28
  161.2 37.9 %collective-permute-start.38 = (bf16[1552,512]{1,0:T(8,128)(2,1)S(1)}, bf16[1552,512]{1,0:T(8,128)(2,1)}, u32[]{:S(2)}, u32[]{:S(2)}) collective-permute-start(bf16[1552,512]{1,0:T(8,128)(2,1)S(1)} %broadcast_add_fusion.refs_0_.refs_1_), channel_id=1, source_target_pairs={{0,48},{8,56},{16,0},{24,8},{32,16},{40,24},{48,32},{56,40},{64,11... | collective-permute-start | bytes 4767752 | tf_op jit(solution)/shard_map/ppermute | solution.py:432
  161.2 39.6 %collective-permute-start.40 = (bf16[1552,512]{1,0:T(8,128)(2,1)S(1)}, bf16[1552,512]{1,0:T(8,128)(2,1)}, u32[]{:S(2)}, u32[]{:S(2)}) collective-permute-start(bf16[1552,512]{1,0:T(8,128)(2,1)S(1)} %broadcast_add_fusion.refs_0_.refs_1_), channel_id=1, source_target_pairs={{0,32},{8,40},{16,48},{24,56},{32,0},{40,8},{48,16},{56,24},{64,96... | collective-permute-start | bytes 4767752 | tf_op jit(solution)/shard_map/ppermute | solution.py:432
  175.7 55.1 %collective-permute-start.42 = (bf16[1552,512]{1,0:T(8,128)(2,1)S(1)}, bf16[1552,512]{1,0:T(8,128)(2,1)}, u32[]{:S(2)}, u32[]{:S(2)}) collective-permute-start(bf16[1552,512]{1,0:T(8,128)(2,1)S(1)} %broadcast_add_fusion.refs_0_.refs_1_), channel_id=1, source_target_pairs={{0,16},{8,24},{16,32},{24,40},{32,48},{40,56},{48,0},{56,8},{64,80... | collective-permute-start | bytes 4767752 | tf_op jit(solution)/shard_map/ppermute | solution.py:432
  179.4 82.0 %collective-permute-start.37 = (bf16[1552,512]{1,0:T(8,128)(2,1)S(1)}, bf16[1552,512]{1,0:T(8,128)(2,1)}, u32[]{:S(2)}, u32[]{:S(2)}) collective-permute-start(bf16[1552,512]{1,0:T(8,128)(2,1)S(1)} %broadcast_add_fusion.refs_0_.refs_1_), channel_id=1, source_target_pairs={{0,8},{8,0},{16,24},{24,16},{32,40},{40,32},{48,56},{56,48},{64,72... | collective-permute-start | bytes 4767752 | tf_op jit(solution)/shard_map/ppermute | solution.py:438
  183.9 47.6 %collective-permute-start.26 = (bf16[64,1536]{1,0:T(8,128)(2,1)S(1)}, bf16[64,1536]{1,0:T(8,128)(2,1)S(1)}, u32[]{:S(2)}, u32[]{:S(2)}) collective-permute-start(bf16[64,1536]{1,0:T(8,128)(2,1)S(1)} %concatenate.94), channel_id=1, source_target_pairs={{0,4},{1,5},{2,6},{3,7},{4,0},{5,1},{6,2},{7,3},{8,12},{9,13},{10,... | collective-permute-start | bytes 589832 | tf_op jit(solution)/shard_map/ppermute | solution.py:24
  199.0 33.1 %collective-permute-start.27 = (bf16[64,1536]{1,0:T(8,128)(2,1)S(1)}, bf16[64,1536]{1,0:T(8,128)(2,1)S(1)}, u32[]{:S(2)}, u32[]{:S(2)}) collective-permute-start(bf16[64,1536]{1,0:T(8,128)(2,1)S(1)} %concatenate.94), channel_id=1, source_target_pairs={{0,3},{1,0},{2,1},{3,2},{4,7},{5,4},{6,5},{7,6},{8,11},{9,8},{10,9... | collective-permute-start | bytes 589832 | tf_op jit(solution)/shard_map/ppermute | solution.py:28
  200.8 60.6 %collective-permute-start.39 = (bf16[1552,512]{1,0:T(8,128)(2,1)}, bf16[1552,512]{1,0:T(8,128)(2,1)S(1)}, u32[]{:S(2)}, u32[]{:S(2)}) collective-permute-start(bf16[1552,512]{1,0:T(8,128)(2,1)} %broadcast_dynamic-update-slice_fusion.2.refs_4_.refs_5_), channel_id=1, source_target_pairs={{0,8},{8,0},{16,24},{24,16},{32,40},{40,32},{48,56},{56,48},{64,72... | collective-permute-start | bytes 4767752 | tf_op jit(solution)/shard_map/ppermute | solution.py:438
  230.9 30.6 %collective-permute-start.41 = (bf16[1552,512]{1,0:T(8,128)(2,1)}, bf16[1552,512]{1,0:T(8,128)(2,1)S(1)}, u32[]{:S(2)}, u32[]{:S(2)}) collective-permute-start(bf16[1552,512]{1,0:T(8,128)(2,1)} %broadcast_dynamic-update-slice_fusion.1.refs_8_.refs_9_), channel_id=1, source_target_pairs={{0,8},{8,0},{16,24},{24,16},{32,40},{40,32},{48,56},{56,48},{64,72... | collective-permute-start | bytes 4767752 | tf_op jit(solution)/shard_map/ppermute | solution.py:438
  231.5 29.9 %collective-permute-start.43 = (bf16[1552,512]{1,0:T(8,128)(2,1)}, bf16[1552,512]{1,0:T(8,128)(2,1)S(1)}, u32[]{:S(2)}, u32[]{:S(2)}) collective-permute-start(bf16[1552,512]{1,0:T(8,128)(2,1)} %broadcast_dynamic-update-slice_fusion.refs_12_.refs_13_), channel_id=1, source_target_pairs={{0,8},{8,0},{16,24},{24,16},{32,40},{40,32},{48,56},{56,48},{64,72... | collective-permute-start | bytes 4767752 | tf_op jit(solution)/shard_map/ppermute | solution.py:438
  284.9 32.9 %collective-permute-start.47 = (bf16[4,528,256]{2,1,0:T(8,128)(2,1)S(1)}, bf16[4,528,256]{2,1,0:T(8,128)(2,1)S(1)}, u32[]{:S(2)}, u32[]{:S(2)}) collective-permute-start(bf16[4,528,256]{2,1,0:T(8,128)(2,1)S(1)} %get-tuple-element.17), channel_id=1, source_target_pairs={{0,64},{8,72},{16,80},{24,88},{32,96},{40,104},{48,112},{56,120},{... | collective-permute-start | bytes 3244040 | tf_op jit(solution)/shard_map/ppermute | solution.py:534
  292.2 34.8 %collective-permute-start.23 = (bf16[256,1536]{1,0:T(8,128)(2,1)S(1)}, bf16[256,1536]{1,0:T(8,128)(2,1)S(1)}, u32[]{:S(2)}, u32[]{:S(2)}) collective-permute-start(bf16[256,1536]{1,0:T(8,128)(2,1)S(1)} %get-tuple-element.42), channel_id=1, source_target_pairs={{0,4},{1,5},{2,6},{3,7},{4,0},{5,1},{6,2},{7,3},{8,12},{9,13},{10,... | collective-permute-start | bytes 2359304 | tf_op jit(solution)/shard_map/ppermute | solution.py:24
  293.4 35.5 %collective-permute-start.21 = (bf16[256,1536]{1,0:T(8,128)(2,1)S(1)}, bf16[256,1536]{1,0:T(8,128)(2,1)S(1)}, u32[]{:S(2)}, u32[]{:S(2)}) collective-permute-start(bf16[256,1536]{1,0:T(8,128)(2,1)S(1)} %get-tuple-element.41), channel_id=1, source_target_pairs={{0,2},{1,3},{2,0},{3,1},{4,6},{5,7},{6,4},{7,5},{8,10},{9,11},{10,... | collective-permute-start | bytes 2359304 | tf_op jit(solution)/shard_map/ppermute | solution.py:28
  311.2 25.3 %collective-permute-start.51 = (bf16[4,528,256]{2,1,0:T(8,128)(2,1)S(1)}, bf16[4,528,256]{2,1,0:T(8,128)(2,1)S(1)}, u32[]{:S(2)}, u32[]{:S(2)}) collective-permute-start(bf16[4,528,256]{2,1,0:T(8,128)(2,1)S(1)} %pad_maximum_fusion.5), channel_id=1, source_target_pairs={{0,8},{8,0},{16,24},{24,16},{32,40},{40,32},{48,56},{56,48},{64,72... | collective-permute-start | bytes 3244040 | tf_op jit(solution)/shard_map/ppermute | solution.py:438
  330.2 18.5 %collective-permute-start.25 = (bf16[128,1536]{1,0:T(8,128)(2,1)}, bf16[128,1536]{1,0:T(8,128)(2,1)}, u32[]{:S(2)}, u32[]{:S(2)}) collective-permute-start(bf16[128,1536]{1,0:T(8,128)(2,1)} %get-tuple-element.31), channel_id=1, source_target_pairs={{0,3},{1,0},{2,1},{3,2},{4,7},{5,4},{6,5},{7,6},{8,11},{9,8},{10,9... | collective-permute-start | bytes 1179656 | tf_op jit(solution)/shard_map/ppermute | solution.py:28
  331.7 17.1 %collective-permute-start.24 = (bf16[128,1536]{1,0:T(8,128)(2,1)}, bf16[128,1536]{1,0:T(8,128)(2,1)}, u32[]{:S(2)}, u32[]{:S(2)}) collective-permute-start(bf16[128,1536]{1,0:T(8,128)(2,1)} %get-tuple-element.30), channel_id=1, source_target_pairs={{0,1},{1,2},{2,3},{3,0},{4,5},{5,6},{6,7},{7,4},{8,9},{9,10},{10,1... | collective-permute-start | bytes 1179656 | tf_op jit(solution)/shard_map/ppermute | solution.py:28
  386.0 25.4 %collective-permute-start.58 = (bf16[1024,512]{1,0:T(8,128)(2,1)}, bf16[1024,512]{1,0:T(8,128)(2,1)}, u32[]{:S(2)}, u32[]{:S(2)}) collective-permute-start(bf16[1024,512]{1,0:T(8,128)(2,1)} %pad_maximum_fusion.10), channel_id=1, source_target_pairs={{0,4},{1,5},{2,6},{3,7},{4,0},{5,1},{6,2},{7,3},{8,12},{9,13},{10,... | collective-permute-start | bytes 3145736 | tf_op jit(solution)/shard_map/ppermute | solution.py:24
  390.5 27.0 %collective-permute-start.56 = (bf16[1024,512]{1,0:T(8,128)(2,1)}, bf16[1024,512]{1,0:T(8,128)(2,1)}, u32[]{:S(2)}, u32[]{:S(2)}) collective-permute-start(bf16[1024,512]{1,0:T(8,128)(2,1)} %pad_maximum_fusion.9), channel_id=1, source_target_pairs={{0,2},{1,3},{2,0},{3,1},{4,6},{5,7},{6,4},{7,5},{8,10},{9,11},{10,... | collective-permute-start | bytes 3145736 | tf_op jit(solution)/shard_map/ppermute | solution.py:28
  (53 other events, 491.5 us)
where the time goes:
time: 444 us; the launch traced here: 436 us
  waiting for transfers between devices  201 us (45%)
  starting transfers between devices  85.1 us (19%)
  Pallas kernels  72.2 us (16%)
  local copies, waits for them, and re-layouts  31.8 us (7%)
  other arithmetic  20.5 us (5%)
  matrix products  19.3 us (4%)
  between operations  6.54 us (1%)
    ppermute x12, waiting for transfers between devices, turn_y(): lax.ppermute(value, 'seq', [(i, i & 9 | i + 2 * steps & 6) for i in range...  62.8 us
    ppermute x16, waiting for transfers between devices, flip_x(): return lax.ppermute(value, 'blk', [(i, i ^ 4) for i in range(8)])  62.2 us
    ppermute x24, waiting for transfers between devices, turn_z(): lax.ppermute(value, 'blk', [(i, i & 4 | i + steps & 3) for i in range(8)])  60 us
    ppermute x24, starting transfers between devices, turn_z(): lax.ppermute(value, 'blk', [(i, i & 4 | i + steps & 3) for i in range(8)])  34.4 us
    ppermute x12, starting transfers between devices, turn_y(): lax.ppermute(value, 'seq', [(i, i & 9 | i + 2 * steps & 6) for i in range...  28.8 us
    pallas_call x2, Pallas kernels, causal_attend(): pl.pallas_call(kernel, out_shape=out_shape, grid_spec=pltpu.PrefetchScala...  28.2 us
    pallas_call x1, Pallas kernels, project_two(): pl.pallas_call(project_kernel, out_shape=(jax.ShapeDtypeStruct((4, 512 +...  22.2 us
    dot_general x14, matrix products, dot(): return jnp.dot(left, right, preferred_element_type=F32)  19.3 us
  transfers between devices with their start and end apart: 61, of which 31 were waited for; matrix products, arithmetic and copies ran while one was open for 12% of the time, Pallas kernels for 6%

commit v1 on v0

--- a/solution.py
+++ b/solution.py
@@ -237,7 +237,7 @@
 
 
 def project_kernel(info, pooled, *refs):
-    pieces, (weights, valid, chunks, pairs, wide_own, total, squares) = refs[:16], refs[16:]
+    pieces, (weights, valid, chunks, pairs, wide_own, total, squares) = refs[:8], refs[8:]
     step = pl.program_id(0)
     y = info[8]
 
@@ -246,11 +246,7 @@
         total[...] = jnp.zeros_like(total)
         squares[...] = jnp.zeros_like(squares)
 
-    wide = jnp.zeros((512, 512), F32)
-    for k in range(4):
-        rows = jnp.concatenate([piece[...] for piece in pieces[4 * k : 4 * k + 4]], axis=0)
-        wide += dot(pooled[:, k * 384 : (k + 1) * 384], rows)
-    wide = wide.astype(BF16)
+    wide = dot(pooled[...], jnp.concatenate([piece[...] for piece in pieces], axis=0)).astype(BF16)
     floats = wide.astype(F32)
     squares[...] += jnp.broadcast_to(
         jnp.sum(floats * floats, axis=-1, keepdims=True), squares.shape
@@ -297,7 +293,7 @@
             grid=(8,),
             in_specs=[
                 pl.BlockSpec((512, D1), lambda s, info: (0, 0)),
-                *[pl.BlockSpec((96, 512), lambda s, info, h=h: (8 * h + s, 0)) for _ in range(8) for h in range(2)],
+                *[pl.BlockSpec((192, 512), lambda s, info: (s, 0)) for _ in range(8)],
                 pl.BlockSpec((3, 512, 512), lambda s, info: (0, info[s], 0)),
                 pl.BlockSpec((EXT, 128), lambda s, info: (0, 0)),
             ],
@@ -313,10 +309,10 @@
             flops=4 * 512 * 4096 * 1536, bytes_accessed=28 * 2**20, transcendentals=512
         ),
         name="project_two",
-    )(info, pooled, *[piece for piece in pieces for _ in range(2)], weights, valid)
-
-
-def causal_kernel(own_part, info, queries, kv, start, start_stats, out, out_stats, keys, values, even, odd):
+    )(info, pooled, *pieces, weights, valid)
+
+
+def causal_kernel(own_part, info, queries, kv_pair, start, start_stats, out, out_stats, keys, values, even, odd):
     half, core, y = info[0], info[1], info[2]
     slot = pl.program_id(0)
     own_pair = (y + slot) & 3
@@ -324,15 +320,17 @@
     @pl.when(slot == 0)
     def _():
         def prepare(block, _):
-            count = jnp.sum(kv[block, 512 : 512 + EXT, :128].astype(F32))
             row = lax.broadcasted_iota(jnp.int32, (512, 128), 0).astype(F32)
             lane = lax.broadcasted_iota(jnp.int32, (512, 128), 1)
-            keys[block, :, :128] = kv[block, :512, :128]
-            keys[block, :, 128:] = jnp.where((lane == 0) & (row >= count), MASKED, 0.0).astype(BF16)
-            values[block] = kv[block, :512, 128:].T
+            for which, kv in enumerate(kv_pair):
+                count = jnp.sum(kv[block, 512 : 512 + EXT, :128].astype(F32))
+                invalid = (lane == 0) & (row >= count)
+                keys[which * 4 + block, :, :128] = kv[block, :512, :128]
+                keys[which * 4 + block, :, 128:] = jnp.where(invalid, MASKED, 0.0).astype(BF16)
+                values[which * 4 + block] = kv[block, :512, 128:].T
             return 0
 
-        lax.fori_loop(0, 8, prepare, 0)
+        lax.fori_loop(0, 4, prepare, 0)
 
     lane = lax.broadcasted_iota(jnp.int32, (512, 128), 1)
     query = jnp.concatenate([queries[0], jnp.where(lane == 0, 1.0, 0.0).astype(BF16)], axis=1)
@@ -381,24 +379,25 @@
         out[0] = (sums / total).T.astype(BF16)
 
 
-def causal_attend(own_part, info, queries, kv, start=None):
+def causal_attend(own_part, info, queries, kv_pair, start=None):
     def by_slot(*shape):
         return pl.BlockSpec((1, *shape), lambda s, info: (s, 0, 0))
 
     sums_shape = jax.ShapeDtypeStruct((4, 128, 512), F32)
     stats_shape = jax.ShapeDtypeStruct((4, 8, 512), F32)
-    in_specs = [by_slot(512, 128), pl.BlockSpec((8, 512 + EXT, 256), lambda s, info: (0, 0, 0))]
-    operands = [queries, kv]
+    whole = pl.BlockSpec((4, 512 + EXT, 256), lambda s, info: (0, 0, 0))
+    in_specs = [by_slot(512, 128), whole, whole]
+    operands = [queries, *kv_pair]
     if own_part:
-        def kernel(info, queries, kv, out, out_stats, *scratch):
-            causal_kernel(True, info, queries, kv, None, None, out, out_stats, *scratch)
+        def kernel(info, queries, kv, other, out, out_stats, *scratch):
+            causal_kernel(True, info, queries, (kv, other), None, None, out, out_stats, *scratch)
 
         out_shape = (sums_shape, stats_shape)
         out_specs = (by_slot(128, 512), by_slot(8, 512))
         tiles = 18
     else:
-        def kernel(info, queries, kv, start, start_stats, out, *scratch):
-            causal_kernel(False, info, queries, kv, start, start_stats, out, None, *scratch)
+        def kernel(info, queries, kv, other, start, start_stats, out, *scratch):
+            causal_kernel(False, info, queries, (kv, other), start, start_stats, out, None, *scratch)
 
         out_shape = jax.ShapeDtypeStruct((4, 512, 128), BF16)
         out_specs = by_slot(512, 128)
@@ -461,8 +460,9 @@
     piece = lax.dynamic_slice(widen, (seq_position * 96, 0), (96, 512))
 
     near, far = gather_blk(prepare(tokens, boundary[None, :]))
-    piece_here = jnp.concatenate(gather_blk(piece), axis=0)
-    piece_across = flip_seq(piece_here, 8)
+    piece = later(jnp.concatenate([piece, flip_seq(piece, 8)], axis=0), near)
+    piece = jnp.concatenate([*gather_blk(piece), jnp.zeros((EXT, 512), BF16)], axis=0)
+    pieces = [piece, turn_y(piece, 3), turn_y(piece, 2), turn_y(piece, 1)]
     marks = jnp.concatenate(
         [part.reshape(4, SENT, D1)[:, rows, :rows] for part in (near, far)], axis=0
     )
@@ -472,10 +472,6 @@
     attended = window_attend(info, qkv, halo, window_attend(info, qkv))
     attn_near = dot(attended[: 4 * rows], heads_out).astype(BF16)
     attn_far = dot(attended[4 * rows :], heads_out).astype(BF16)
-    piece_pair = later(
-        jnp.concatenate([piece_here, piece_across, jnp.zeros((EXT, 512), BF16)], axis=0), attended
-    )
-    pieces = [piece_pair, turn_y(piece_pair, 3), turn_y(piece_pair, 2), turn_y(piece_pair, 1)]
     mid_stream = (tokens.astype(F32) + reduce_blk(attn_near, attn_far)).astype(BF16)
 
     normed_mid = normalize(mid_stream).astype(BF16)
@@ -500,8 +496,9 @@
         + dot(selector[:, :rows], mid_stream)
     ).astype(BF16)
     pooled_own = reduce_blk(placed[:256], placed[256:]).astype(BF16)
-    unread = later(jnp.zeros((EXT, 512), BF16), pooled_own)
-    pieces[1:] = [lax.dynamic_update_slice(part, unread, (1536, 0)) for part in pieces[1:]]
+    for k, value in ((1, mlp_near), (2, pooled_own), (3, mlp_near)):
+        unread = later(jnp.zeros((EXT, 512), BF16), value)
+        pieces[k] = lax.dynamic_update_slice(pieces[k], unread, (1536, 0))
     pieces = [part for own in pieces for part in (own, flip_seq(own, 1))]
     pooled_own = jnp.concatenate(
         [
@@ -518,7 +515,7 @@
 
     far = later(mlp_far, pooled)
     opposite, diagonal = reduce_first(far)
-    level_one = (mid_stream.astype(F32) + reduce_second(mlp_near, opposite, diagonal)).astype(BF16)
+    level_one = mid_stream.astype(F32) + reduce_second(mlp_near, opposite, diagonal)
 
     validity = (jnp.arange(capacity, dtype=jnp.int32) < span_count).astype(F32)
     valid_rows = jnp.pad(
@@ -534,26 +531,27 @@
     first = lax.ppermute(pairs, "seq", [(i, i + 8) for i in range(8)])
     mine = jnp.stack([chunks[0], from_ahead, from_opposite, from_behind])
     queries, own_kv = mine[:, :capacity, :128], mine[:, :, 128:]
-    own_pair = jnp.concatenate([own_kv, flip_seq(own_kv, 1)], axis=0)
+    info_two = jnp.stack([half, core, y]).astype(jnp.int32)
+    running = causal_attend(True, later(info_two, first[0]), queries, (own_kv, flip_seq(own_kv, 1)))
     first_kv = jnp.stack(
         [first[0], turn_y(first[3], 3, 8), turn_y(first[2], 2, 8), turn_y(first[1], 1, 8)]
     )
-    info_two = jnp.stack([half, core, y]).astype(jnp.int32)
-    running = causal_attend(True, later(info_two, opposite), queries, own_pair)
-    unread = jnp.broadcast_to(running[1][0:1, 2:3, :128], (1, EXT, 128)).astype(BF16)
-    first_kv = lax.dynamic_update_slice(first_kv, unread, (0, capacity, 128))
-    first_pair = jnp.concatenate([first_kv, flip_seq(first_kv, 1)], axis=0)
-    mixed = causal_attend(False, later(info_two, level_one), queries, first_pair, running)
+    first_kv = first_kv + running[1][0, 2, 0].astype(BF16)
+    mixed = causal_attend(False, info_two, queries, (first_kv, flip_seq(first_kv, 1)), running)
     back = [mixed[0], turn_y(mixed[3], 3), turn_y(mixed[2], 2), turn_y(mixed[1], 1)]
     heads = jnp.concatenate([back[0], back[1], back[2], back[3]] * 2, axis=1)
     attended_two = lax.dynamic_slice(heads, (0, ((4 - y) & 3) * 128), (capacity, 512))
 
+    level_one = later(level_one, mixed[0]).astype(BF16)
+    column_of = later(block_of, level_one)
+
     def columns(place):
-        part = lax.dynamic_slice(heads_out_two, (0, block_of[place] * 512), (512, 512))
+        part = lax.dynamic_slice(heads_out_two, (0, column_of[place] * 512), (512, 512))
         return dot(attended_two, part).astype(BF16)
 
     out_far = jnp.concatenate([columns(place) for place in range(4, 8)], axis=0)
     out_near = jnp.concatenate([columns(place) for place in range(4)], axis=0)
+    out_near = lax.optimization_barrier(out_near)
     level_two = (
         (wide_cols.astype(F32) + reduce_blk(out_near, out_far)) * validity[:, None]
     ).astype(BF16)

time: 444 us -> 421 us (0.948)
  waiting for transfers between devices: 201 us -> 180 us
  between operations: 6.54 us -> 12.7 us
  starting transfers between devices: 85.1 us -> 79.9 us
    ppermute x12, waiting for transfers between devices: 62.8 us -> 19.4 us  [turn_y(): lax.ppermute(value, 'seq', [(i, i & 9 | i + 2 * steps & 6) for i in range...]
    ppermute x24, waiting for transfers between devices: 60 us -> 86.6 us  [turn_z(): lax.ppermute(value, 'blk', [(i, i & 4 | i + steps & 3) for i in range(8)])]
    ppermute x1, waiting for transfers between devices: 6.51 us -> 25.9 us  [per_device(): first = lax.ppermute(pairs, 'seq', [(i, i + 8) for i in range(8)])]
    ppermute x16, waiting for transfers between devices: 62.2 us -> 48.4 us  [flip_x(): return lax.ppermute(value, 'blk', [(i, i ^ 4) for i in range(8)])]
    ppermute x7, waiting for transfers between devices: 9.4 us -> 0.02 us  [flip_seq(): return lax.ppermute(value, 'seq', [(i, i ^ bit) for i in range(16)])]
    ppermute x12, starting transfers between devices: 28.8 us -> 23.1 us  [turn_y(): lax.ppermute(value, 'seq', [(i, i & 9 | i + 2 * steps & 6) for i in range...]
    unnamed x68 -> x62, local copies, waits for them, and re-layouts: 11.7 us -> 7.31 us
  transfers between devices with their start and end apart: 61 -> 61, of which waited for: 31 -> 28; matrix products, arithmetic and copies ran while one was open for 12% -> 13% of each run, Pallas kernels for 6% -> 12%
where the time goes in v1:
time: 421 us; the launch traced here: 414 us
  waiting for transfers between devices  180 us (43%)
  starting transfers between devices  79.9 us (19%)
  Pallas kernels  71.1 us (17%)
  local copies, waits for them, and re-layouts  34.4 us (8%)
  other arithmetic  18.5 us (4%)
  matrix products  16.9 us (4%)
  between operations  12.7 us (3%)
    ppermute x24, waiting for transfers between devices, turn_z(): lax.ppermute(value, 'blk', [(i, i & 4 | i + steps & 3) for i in range(8)])  86.6 us
    ppermute x16, waiting for transfers between devices, flip_x(): return lax.ppermute(value, 'blk', [(i, i ^ 4) for i in range(8)])  48.4 us
    ppermute x24, starting transfers between devices, turn_z(): lax.ppermute(value, 'blk', [(i, i & 4 | i + steps & 3) for i in range(8)])  36.3 us
    pallas_call x2, Pallas kernels, causal_attend(): pl.pallas_call(kernel, out_shape=out_shape, grid_spec=pltpu.PrefetchScala...  28.8 us
    ppermute x1, waiting for transfers between devices, per_device(): first = lax.ppermute(pairs, 'seq', [(i, i + 8) for i in range(8)])  25.9 us
    ppermute x12, starting transfers between devices, turn_y(): lax.ppermute(value, 'seq', [(i, i & 9 | i + 2 * steps & 6) for i in range...  23.1 us
    pallas_call x1, Pallas kernels, project_two(): pl.pallas_call(project_kernel, out_shape=(jax.ShapeDtypeStruct((4, 512 +...  19.9 us
    ppermute x12, waiting for transfers between devices, turn_y(): lax.ppermute(value, 'seq', [(i, i & 9 | i + 2 * steps & 6) for i in range...  19.4 us
  transfers between devices with their start and end apart: 61, of which 28 were waited for; matrix products, arithmetic and copies ran while one was open for 13% of the time, Pallas kernels for 12%

profile of v1, /device:TPU:6, one launch (start us, length us, event | category | flops | bytes accessed | tf_op | source)
XLA Modules:
  0.0 413.9 jit_solution(17192428697462227102)
XLA Ops:
  3.5 4.0 collective-permute-start.1
  9.3 7.9 %fusion.43 = (bf16[1536,1,512]{2,1,0:T(2,128)(2,1)S(1)}, bf16[1536,1,512]{2,1,0:T(2,128)(2,1)S(1)}) fusion(bf16[1536,2,512]{2,1,0:T(2,128)(2,1)} %param.13), kind=kLoop, calls=%fused_computation.172 | loop fusion | bytes 6291456 | tf_op jit(solution)/shard_map/slice | solution.py:458
  28.3 14.7 %collective-permute-done.3 = bf16[288,1536]{1,0:T(8,128)(2,1)S(1)} collective-permute-done((bf16[288,1536]{1,0:T(8,128)(2,1)S(1)}, bf16[288,1536]{1,0:T(8,128)(2,1)S(1)}, u32[]{:S(2)}, u32[]{:S(2)}) %collective-permute-start.3) | collective-permute-done | bytes 884768 | tf_op jit(solution)/shard_map/ppermute | solution.py:28
  53.5 3.3 collective-permute-done.32
  60.2 4.7 %window_late.1.before = bf16[1024,192]{1,0:T(8,128)(2,1)S(1)} custom-call(s32[9]{0:T(128)S(1)} %add_add_fusion.info, bf16[1152,576]{1,0:T(8,128)(2,1)S(1)} %get-tuple-element.12.qkv), custom_call_target="tpu_custom_call" | custom-call | flops 251658240 | bytes 2097152 | tf_op jit(solution)/shard_map/window_late/pallas_call | solution.py:140
  65.0 5.4 %window_early.1 = bf16[1024,192]{1,0:T(8,128)(2,1)S(1)} custom-call(s32[9]{0:T(128)S(1)} %add_add_fusion.info, bf16[1152,576]{1,0:T(8,128)(2,1)S(1)} %get-tuple-element.12.qkv, bf16[512,384]{1,0:T(8,128)(2,1)} %collective-permute-done.5.halo, bf16[1024,192]{1,0:T(8,128)(2,1)S(1)} %window_late.1.before), custom_call_target="tpu_custom_call" | custom-call | flops 251658240 | bytes 2097152 | tf_op jit(solution)/shard_map/window_early/pallas_call | solution.py:140
  78.4 14.3 %collective-permute-done.6 = bf16[256,1536]{1,0:T(8,128)(2,1)S(1)} collective-permute-done((bf16[256,1536]{1,0:T(8,128)(2,1)S(1)}, bf16[256,1536]{1,0:T(8,128)(2,1)S(1)}, u32[]{:S(2)}, u32[]{:S(2)}) %collective-permute-start.6) | collective-permute-done | bytes 786464 | tf_op jit(solution)/shard_map/ppermute | solution.py:28
  97.4 4.2 %collective-permute-done.36 = bf16[384,512]{1,0:T(8,128)(2,1)S(1)} collective-permute-done((bf16[384,512]{1,0:T(8,128)(2,1)S(1)}, bf16[384,512]{1,0:T(8,128)(2,1)S(1)}, u32[]{:S(2)}, u32[]{:S(2)}) %collective-permute-start.36) | collective-permute-done | bytes 393248 | tf_op jit(solution)/shard_map/ppermute | solution.py:24
  114.8 6.0 %collective-permute-done.11 = bf16[128,1536]{1,0:T(8,128)(2,1)S(1)} collective-permute-done((bf16[128,1536]{1,0:T(8,128)(2,1)S(1)}, bf16[128,1536]{1,0:T(8,128)(2,1)S(1)}, u32[]{:S(2)}, u32[]{:S(2)}) %collective-permute-start.11) | collective-permute-done | bytes 393248 | tf_op jit(solution)/shard_map/ppermute | solution.py:24
  122.7 19.8 %collective-permute-done.13 = bf16[128,1536]{1,0:T(8,128)(2,1)S(1)} collective-permute-done((bf16[128,1536]{1,0:T(8,128)(2,1)S(1)}, bf16[128,1536]{1,0:T(8,128)(2,1)S(1)}, u32[]{:S(2)}, u32[]{:S(2)}) %collective-permute-start.13) | collective-permute-done | bytes 393248 | tf_op jit(solution)/shard_map/ppermute | solution.py:28
  149.4 7.3 %collective-permute-done.15 = bf16[256,1536]{1,0:T(8,128)(2,1)S(1)} collective-permute-done((bf16[256,1536]{1,0:T(8,128)(2,1)S(1)}, bf16[256,1536]{1,0:T(8,128)(2,1)S(1)}, u32[]{:S(2)}, u32[]{:S(2)}) %collective-permute-start.15) | collective-permute-done | bytes 786464 | tf_op jit(solution)/shard_map/ppermute | solution.py:24
  170.4 4.1 collective-permute-done.16
  177.0 3.2 collective-permute-start.20
  188.1 3.3 collective-permute-start.27
  193.0 4.0 collective-permute-done.26
  197.4 8.3 %collective-permute-done.28 = bf16[64,1536]{1,0:T(8,128)(2,1)S(1)} collective-permute-done((bf16[64,1536]{1,0:T(8,128)(2,1)S(1)}, bf16[64,1536]{1,0:T(8,128)(2,1)S(1)}, u32[]{:S(2)}, u32[]{:S(2)}) %collective-permute-start.28) | collective-permute-done | bytes 196640 | tf_op jit(solution)/shard_map/ppermute | solution.py:28
  205.8 12.2 %collective-permute-done.29 = bf16[128,1536]{1,0:T(8,128)(2,1)S(1)} collective-permute-done((bf16[128,1536]{1,0:T(8,128)(2,1)S(1)}, bf16[128,1536]{1,0:T(8,128)(2,1)S(1)}, u32[]{:S(2)}, u32[]{:S(2)}) %collective-permute-start.29) | collective-permute-done | bytes 393248 | tf_op jit(solution)/shard_map/ppermute | solution.py:28
  219.2 8.8 %collective-permute-done.30 = bf16[128,1536]{1,0:T(8,128)(2,1)S(1)} collective-permute-done((bf16[128,1536]{1,0:T(8,128)(2,1)S(1)}, bf16[128,1536]{1,0:T(8,128)(2,1)S(1)}, u32[]{:S(2)}, u32[]{:S(2)}) %collective-permute-start.30) | collective-permute-done | bytes 393248 | tf_op jit(solution)/shard_map/ppermute | solution.py:24
  228.1 19.9 %project_two.1 = (bf16[4,528,384]{2,1,0:T(8,128)(2,1)}, bf16[4,528,256]{2,1,0:T(8,128)(2,1)S(1)}, bf16[512,512]{1,0:T(8,128)(2,1)S(1)}) custom-call(s32[9]{0:T(128)S(1)} %concatenate.89.info, bf16[512,1536]{1,0:T(8,128)(2,1)S(1)} %constant_dynamic-update-slice_fusion.2.pooled, bf16[1552,512]{1,0:T(8,128)(2,1)} %constant_dynamic-update-slice_fusion.8.refs_0_, ...), custom_call_target="tpu_custom_call" | custom-call | flops 12884901888 | bytes 29360128 | tf_op jit(solution)/shard_map/project_two/pallas_call | solution.py:284
  249.8 3.4 collective-permute-start.45
  255.7 6.4 %collective-permute-done.44 = bf16[528,384]{1,0:T(8,128)(2,1)S(1)} collective-permute-done((bf16[528,384]{1,0:T(8,128)(2,1)S(1)}, bf16[528,384]{1,0:T(8,128)(2,1)S(1)}, u32[]{:S(2)}, u32[]{:S(2)}) %collective-permute-start.44) | collective-permute-done | bytes 405536 | tf_op jit(solution)/shard_map/ppermute | solution.py:431
  263.7 5.5 %collective-permute-done.46 = bf16[528,384]{1,0:T(8,128)(2,1)S(1)} collective-permute-done((bf16[528,384]{1,0:T(8,128)(2,1)S(1)}, bf16[528,384]{1,0:T(8,128)(2,1)S(1)}, u32[]{:S(2)}, u32[]{:S(2)}) %collective-permute-start.46) | collective-permute-done | bytes 405536 | tf_op jit(solution)/shard_map/ppermute | solution.py:431
  271.9 25.9 %collective-permute-done.47 = bf16[4,528,256]{2,1,0:T(8,128)(2,1)S(1)} collective-permute-done((bf16[4,528,256]{2,1,0:T(8,128)(2,1)S(1)}, bf16[4,528,256]{2,1,0:T(8,128)(2,1)S(1)}, u32[]{:S(2)}, u32[]{:S(2)}) %collective-permute-start.47) | collective-permute-done | bytes 1081376 | tf_op jit(solution)/shard_map/ppermute | solution.py:531
  299.0 4.2 %collective-permute-start.48 = (bf16[528,256]{1,0:T(8,128)(2,1)S(1)}, bf16[528,256]{1,0:T(8,128)(2,1)S(1)}, u32[]{:S(2)}, u32[]{:S(2)}) collective-permute-start(bf16[528,256]{1,0:T(8,128)(2,1)S(1)} %get-tuple-element.56), channel_id=1, source_target_pairs={{64,112},{72,120},{80,64},{88,72},{96,80},{104,88},{112,96},{120,1... | collective-permute-start | bytes 811016 | tf_op jit(solution)/shard_map/ppermute | solution.py:431
  303.2 3.9 collective-permute-start.49
  309.2 11.0 %causal_own.1 = (f32[4,128,512]{2,1,0:T(8,128)S(1)}, f32[4,8,512]{2,1,0:T(8,128)S(1)}) custom-call(s32[3]{0:T(128)S(1)} %get-tuple-element.22.info, bf16[4,512,128]{2,1,0:T(8,128)(2,1)S(1)} %pad_maximum_fusion.13.queries, bf16[4,528,256]{2,1,0:T(8,128)(2,1)S(1)} %pad_maximum_fusion.4.kv, bf16[4,528,256]{2,1,0:T(8,128)(2,1)S(1)} %collective-permute-done.51.other), custom_call_target="tpu_custom_call" | custom-call | flops 2415919104 | bytes 4194304 | tf_op jit(solution)/shard_map/causal_own/pallas_call | solution.py:407
  326.8 3.2 collective-permute-start.25
  330.1 17.8 %causal_first_half.1 = bf16[4,512,128]{2,1,0:T(8,128)(2,1)S(1)} custom-call(s32[3]{0:T(128)S(1)} %get-tuple-element.23.info, bf16[4,512,128]{2,1,0:T(8,128)(2,1)S(1)} %copy-done.10, bf16[4,528,256]{2,1,0:T(8,128)(2,1)S(1)} %maximum_add_fusion.kv, bf16[4,528,256]{2,1,0:T(8,128)(2,1)} %collective-permute-done.52.other, f32[4,128,512]{2,1,0:T(8,128)S(1)} %copy-done.13, ...), custom_call_target="tpu_custom_call" | custom-call | flops 4294967296 | bytes 4194304 | tf_op jit(solution)/shard_map/causal_first_half/pallas_call | solution.py:407
  362.2 3.7 collective-permute-done.55
  384.4 9.0 %collective-permute-done.56 = bf16[1024,512]{1,0:T(8,128)(2,1)S(1)} collective-permute-done((bf16[1024,512]{1,0:T(8,128)(2,1)S(1)}, bf16[1024,512]{1,0:T(8,128)(2,1)S(1)}, u32[]{:S(2)}, u32[]{:S(2)}) %collective-permute-start.56) | collective-permute-done | bytes 1048608 | tf_op jit(solution)/shard_map/ppermute | solution.py:28
  393.5 3.4 collective-permute-done.58
  403.3 5.6 %collective-permute-done.57 = bf16[512,512]{1,0:T(8,128)(2,1)S(1)} collective-permute-done((bf16[512,512]{1,0:T(8,128)(2,1)S(1)}, bf16[512,512]{1,0:T(8,128)(2,1)S(1)}, u32[]{:S(2)}, u32[]{:S(2)}) %collective-permute-start.57) | collective-permute-done | bytes 524320 | tf_op jit(solution)/shard_map/ppermute | solution.py:24
  (250 shorter events, 142.5 us)
Async XLA Ops:
  2.7 18.1 %collective-permute-start = (bf16[144,1536]{1,0:T(8,128)(2,1)}, bf16[144,1536]{1,0:T(8,128)(2,1)S(1)}, u32[]{:S(2)}, u32[]{:S(2)}) collective-permute-start(bf16[144,1536]{1,0:T(8,128)(2,1)} %prepare.1), channel_id=1, source_target_pairs={{0,4},{1,5},{2,6},{3,7},{4,0},{5,1},{6,2},{7,3},{8,12},{9,13},{10,... | collective-permute-start | bytes 1327112 | tf_op jit(solution)/shard_map/ppermute | solution.py:24
  3.5 19.3 %collective-permute-start.1 = (bf16[144,1536]{1,0:T(8,128)(2,1)}, bf16[144,1536]{1,0:T(8,128)(2,1)S(1)}, u32[]{:S(2)}, u32[]{:S(2)}) collective-permute-start(bf16[144,1536]{1,0:T(8,128)(2,1)} %prepare.1), channel_id=1, source_target_pairs={{0,3},{1,0},{2,1},{3,2},{4,7},{5,4},{6,5},{7,6},{8,11},{9,8},{10,9... | collective-permute-start | bytes 1327112 | tf_op jit(solution)/shard_map/ppermute | solution.py:28
  8.2 39.6 %collective-permute-start.31 = (bf16[96,512]{1,0:T(8,128)(2,1)}, bf16[96,512]{1,0:T(8,128)(2,1)}, u32[]{:S(2)}, u32[]{:S(2)}) collective-permute-start(bf16[96,512]{1,0:T(8,128)(2,1)} %constant_dynamic-slice_fusion.1), channel_id=1, source_target_pairs={{0,64},{8,72},{16,80},{24,88},{32,96},{40,104},{48,112},{56,120},{... | collective-permute-start | bytes 294920 | tf_op jit(solution)/shard_map/ppermute | solution.py:437
  20.9 22.1 %collective-permute-start.3 = (bf16[288,1536]{1,0:T(8,128)(2,1)S(1)}, bf16[288,1536]{1,0:T(8,128)(2,1)S(1)}, u32[]{:S(2)}, u32[]{:S(2)}) collective-permute-start(bf16[288,1536]{1,0:T(8,128)(2,1)S(1)} %pad_maximum_fusion.9), channel_id=1, source_target_pairs={{0,2},{1,3},{2,0},{3,1},{4,6},{5,7},{6,4},{7,5},{8,10},{9,11},{10,... | collective-permute-start | bytes 2654216 | tf_op jit(solution)/shard_map/ppermute | solution.py:28
  22.9 20.2 %collective-permute-start.4 = (bf16[288,1536]{1,0:T(8,128)(2,1)S(1)}, bf16[288,1536]{1,0:T(8,128)(2,1)S(1)}, u32[]{:S(2)}, u32[]{:S(2)}) collective-permute-start(bf16[288,1536]{1,0:T(8,128)(2,1)S(1)} %pad_maximum_fusion.10), channel_id=1, source_target_pairs={{0,4},{1,5},{2,6},{3,7},{4,0},{5,1},{6,2},{7,3},{8,12},{9,13},{10,... | collective-permute-start | bytes 2654216 | tf_op jit(solution)/shard_map/ppermute | solution.py:24
  45.9 19.1 %collective-permute-start.5 = (bf16[512,384]{1,0:T(8,128)(2,1)}, bf16[512,384]{1,0:T(8,128)(2,1)}, u32[]{:S(2)}, u32[]{:S(2)}) collective-permute-start(bf16[512,384]{1,0:T(8,128)(2,1)} %get-tuple-element.13), channel_id=1, source_target_pairs={{0,8},{8,16},{16,24},{24,32},{32,40},{40,48},{48,56},{56,64},{64,7... | collective-permute-start | bytes 1179656 | tf_op jit(solution)/shard_map/ppermute | solution.py:471
  50.6 23.1 %collective-permute-start.33 = (bf16[192,512]{1,0:T(8,128)(2,1)}, bf16[192,512]{1,0:T(8,128)(2,1)S(1)}, u32[]{:S(2)}, u32[]{:S(2)}) collective-permute-start(bf16[192,512]{1,0:T(8,128)(2,1)} %get-tuple-element.25), channel_id=1, source_target_pairs={{0,3},{1,0},{2,1},{3,2},{4,7},{5,4},{6,5},{7,6},{8,11},{9,8},{10,9... | collective-permute-start | bytes 589832 | tf_op jit(solution)/shard_map/ppermute | solution.py:28
  53.5 20.2 %collective-permute-start.34 = (bf16[192,512]{1,0:T(8,128)(2,1)}, bf16[192,512]{1,0:T(8,128)(2,1)S(1)}, u32[]{:S(2)}, u32[]{:S(2)}) collective-permute-start(bf16[192,512]{1,0:T(8,128)(2,1)} %get-tuple-element.25), channel_id=1, source_target_pairs={{0,1},{1,2},{2,3},{3,0},{4,5},{5,6},{6,7},{7,4},{8,9},{9,10},{10,1... | collective-permute-start | bytes 589832 | tf_op jit(solution)/shard_map/ppermute | solution.py:28
  57.8 19.2 %collective-permute-start.35 = (bf16[384,512]{1,0:T(8,128)(2,1)S(1)}, bf16[384,512]{1,0:T(8,128)(2,1)S(1)}, u32[]{:S(2)}, u32[]{:S(2)}) collective-permute-start(bf16[384,512]{1,0:T(8,128)(2,1)S(1)} %pad_maximum_fusion.16), channel_id=1, source_target_pairs={{0,2},{1,3},{2,0},{3,1},{4,6},{5,7},{6,4},{7,5},{8,10},{9,11},{10,... | collective-permute-start | bytes 1179656 | tf_op jit(solution)/shard_map/ppermute | solution.py:28
  71.0 21.6 %collective-permute-start.6 = (bf16[256,1536]{1,0:T(8,128)(2,1)S(1)}, bf16[256,1536]{1,0:T(8,128)(2,1)S(1)}, u32[]{:S(2)}, u32[]{:S(2)}) collective-permute-start(bf16[256,1536]{1,0:T(8,128)(2,1)S(1)} %get-tuple-element.50), channel_id=1, source_target_pairs={{0,2},{1,3},{2,0},{3,1},{4,6},{5,7},{6,4},{7,5},{8,10},{9,11},{10,... | collective-permute-start | bytes 2359304 | tf_op jit(solution)/shard_map/ppermute | solution.py:28
  72.8 20.4 %collective-permute-start.8 = (bf16[256,1536]{1,0:T(8,128)(2,1)S(1)}, bf16[256,1536]{1,0:T(8,128)(2,1)S(1)}, u32[]{:S(2)}, u32[]{:S(2)}) collective-permute-start(bf16[256,1536]{1,0:T(8,128)(2,1)S(1)} %get-tuple-element.51), channel_id=1, source_target_pairs={{0,4},{1,5},{2,6},{3,7},{4,0},{5,1},{6,2},{7,3},{8,12},{9,13},{10,... | collective-permute-start | bytes 2359304 | tf_op jit(solution)/shard_map/ppermute | solution.py:24
  73.7 27.9 %collective-permute-start.36 = (bf16[384,512]{1,0:T(8,128)(2,1)S(1)}, bf16[384,512]{1,0:T(8,128)(2,1)S(1)}, u32[]{:S(2)}, u32[]{:S(2)}) collective-permute-start(bf16[384,512]{1,0:T(8,128)(2,1)S(1)} %pad_maximum_fusion.17), channel_id=1, source_target_pairs={{0,4},{1,5},{2,6},{3,7},{4,0},{5,1},{6,2},{7,3},{8,12},{9,13},{10,... | collective-permute-start | bytes 1179656 | tf_op jit(solution)/shard_map/ppermute | solution.py:24
  103.0 74.1 %collective-permute-start.38 = (bf16[1552,512]{1,0:T(8,128)(2,1)}, bf16[1552,512]{1,0:T(8,128)(2,1)}, u32[]{:S(2)}, u32[]{:S(2)}) collective-permute-start(bf16[1552,512]{1,0:T(8,128)(2,1)} %constant_dynamic-update-slice_fusion.8.refs_0_), channel_id=1, source_target_pairs={{0,48},{8,56},{16,0},{24,8},{32,16},{40,24},{48,32},{56,40},{64,11... | collective-permute-start | bytes 4767752 | tf_op jit(solution)/shard_map/ppermute | solution.py:431
  104.0 76.9 %collective-permute-start.42 = (bf16[1552,512]{1,0:T(8,128)(2,1)}, bf16[1552,512]{1,0:T(8,128)(2,1)}, u32[]{:S(2)}, u32[]{:S(2)}) collective-permute-start(bf16[1552,512]{1,0:T(8,128)(2,1)} %constant_dynamic-update-slice_fusion.8.refs_0_), channel_id=1, source_target_pairs={{0,16},{8,24},{16,32},{24,40},{32,48},{40,56},{48,0},{56,8},{64,80... | collective-permute-start | bytes 4767752 | tf_op jit(solution)/shard_map/ppermute | solution.py:431
  114.3 28.3 %collective-permute-start.13 = (bf16[128,1536]{1,0:T(8,128)(2,1)S(1)}, bf16[128,1536]{1,0:T(8,128)(2,1)S(1)}, u32[]{:S(2)}, u32[]{:S(2)}) collective-permute-start(bf16[128,1536]{1,0:T(8,128)(2,1)S(1)} %fusion.10), channel_id=1, source_target_pairs={{0,1},{1,2},{2,3},{3,0},{4,5},{5,6},{6,7},{7,4},{8,9},{9,10},{10,1... | collective-permute-start | bytes 1179656 | tf_op jit(solution)/shard_map/ppermute | solution.py:28
  120.8 28.5 %collective-permute-start.14 = (bf16[256,1536]{1,0:T(8,128)(2,1)S(1)}, bf16[256,1536]{1,0:T(8,128)(2,1)S(1)}, u32[]{:S(2)}, u32[]{:S(2)}) collective-permute-start(bf16[256,1536]{1,0:T(8,128)(2,1)S(1)} %pad_maximum_fusion.11), channel_id=1, source_target_pairs={{0,2},{1,3},{2,0},{3,1},{4,6},{5,7},{6,4},{7,5},{8,10},{9,11},{10,... | collective-permute-start | bytes 2359304 | tf_op jit(solution)/shard_map/ppermute | solution.py:28
  166.0 25.4 %collective-permute-start.40 = (bf16[1552,512]{1,0:T(8,128)(2,1)}, bf16[1552,512]{1,0:T(8,128)(2,1)}, u32[]{:S(2)}, u32[]{:S(2)}) collective-permute-start(bf16[1552,512]{1,0:T(8,128)(2,1)} %constant_dynamic-update-slice_fusion.8.refs_0_), channel_id=1, source_target_pairs={{0,32},{8,40},{16,48},{24,56},{32,0},{40,8},{48,16},{56,24},{64,96... | collective-permute-start | bytes 4767752 | tf_op jit(solution)/shard_map/ppermute | solution.py:431
  180.9 47.2 %collective-permute-start.37 = (bf16[1552,512]{1,0:T(8,128)(2,1)}, bf16[1552,512]{1,0:T(8,128)(2,1)}, u32[]{:S(2)}, u32[]{:S(2)}) collective-permute-start(bf16[1552,512]{1,0:T(8,128)(2,1)} %constant_dynamic-update-slice_fusion.8.refs_0_), channel_id=1, source_target_pairs={{0,8},{8,0},{16,24},{24,16},{32,40},{40,32},{48,56},{56,48},{64,72... | collective-permute-start | bytes 4767752 | tf_op jit(solution)/shard_map/ppermute | solution.py:437
  181.7 46.4 %collective-permute-start.39 = (bf16[1552,512]{1,0:T(8,128)(2,1)}, bf16[1552,512]{1,0:T(8,128)(2,1)}, u32[]{:S(2)}, u32[]{:S(2)}) collective-permute-start(bf16[1552,512]{1,0:T(8,128)(2,1)} %broadcast_dynamic-update-slice_fusion.2.refs_2_), channel_id=1, source_target_pairs={{0,8},{8,0},{16,24},{24,16},{32,40},{40,32},{48,56},{56,48},{64,72... | collective-permute-start | bytes 4767752 | tf_op jit(solution)/shard_map/ppermute | solution.py:437
  183.9 44.2 %collective-permute-start.43 = (bf16[1552,512]{1,0:T(8,128)(2,1)}, bf16[1552,512]{1,0:T(8,128)(2,1)}, u32[]{:S(2)}, u32[]{:S(2)}) collective-permute-start(bf16[1552,512]{1,0:T(8,128)(2,1)} %broadcast_dynamic-update-slice_fusion.1.refs_6_), channel_id=1, source_target_pairs={{0,8},{8,0},{16,24},{24,16},{32,40},{40,32},{48,56},{56,48},{64,72... | collective-permute-start | bytes 4767752 | tf_op jit(solution)/shard_map/ppermute | solution.py:437
  197.1 31.0 %collective-permute-start.41 = (bf16[1552,512]{1,0:T(8,128)(2,1)}, bf16[1552,512]{1,0:T(8,128)(2,1)S(1)}, u32[]{:S(2)}, u32[]{:S(2)}) collective-permute-start(bf16[1552,512]{1,0:T(8,128)(2,1)} %broadcast_dynamic-update-slice_fusion.refs_4_), channel_id=1, source_target_pairs={{0,8},{8,0},{16,24},{24,16},{32,40},{40,32},{48,56},{56,48},{64,72... | collective-permute-start | bytes 4767752 | tf_op jit(solution)/shard_map/ppermute | solution.py:437
  253.2 16.1 %collective-permute-start.46 = (bf16[528,384]{1,0:T(8,128)(2,1)S(1)}, bf16[528,384]{1,0:T(8,128)(2,1)S(1)}, u32[]{:S(2)}, u32[]{:S(2)}) collective-permute-start(bf16[528,384]{1,0:T(8,128)(2,1)S(1)} %get-tuple-element.40), channel_id=1, source_target_pairs={{0,16},{8,24},{16,32},{24,40},{32,48},{40,56},{48,0},{56,8},{64,80... | collective-permute-start | bytes 1216520 | tf_op jit(solution)/shard_map/ppermute | solution.py:431
  254.4 43.4 %collective-permute-start.47 = (bf16[4,528,256]{2,1,0:T(8,128)(2,1)S(1)}, bf16[4,528,256]{2,1,0:T(8,128)(2,1)S(1)}, u32[]{:S(2)}, u32[]{:S(2)}) collective-permute-start(bf16[4,528,256]{2,1,0:T(8,128)(2,1)S(1)} %get-tuple-element.16), channel_id=1, source_target_pairs={{0,64},{8,72},{16,80},{24,88},{32,96},{40,104},{48,112},{56,120},{... | collective-permute-start | bytes 3244040 | tf_op jit(solution)/shard_map/ppermute | solution.py:531
  269.3 39.8 %collective-permute-start.51 = (bf16[4,528,256]{2,1,0:T(8,128)(2,1)S(1)}, bf16[4,528,256]{2,1,0:T(8,128)(2,1)S(1)}, u32[]{:S(2)}, u32[]{:S(2)}) collective-permute-start(bf16[4,528,256]{2,1,0:T(8,128)(2,1)S(1)} %pad_maximum_fusion.4.kv), channel_id=1, source_target_pairs={{0,8},{8,0},{16,24},{24,16},{32,40},{40,32},{48,56},{56,48},{64,72... | collective-permute-start | bytes 3244040 | tf_op jit(solution)/shard_map/ppermute | solution.py:437
  270.8 51.9 %collective-permute-start.21 = (bf16[256,1536]{1,0:T(8,128)(2,1)}, bf16[256,1536]{1,0:T(8,128)(2,1)}, u32[]{:S(2)}, u32[]{:S(2)}) collective-permute-start(bf16[256,1536]{1,0:T(8,128)(2,1)} %get-tuple-element.44), channel_id=1, source_target_pairs={{0,2},{1,3},{2,0},{3,1},{4,6},{5,7},{6,4},{7,5},{8,10},{9,11},{10,... | collective-permute-start | bytes 2359304 | tf_op jit(solution)/shard_map/ppermute | solution.py:28
  299.0 22.8 %collective-permute-start.48 = (bf16[528,256]{1,0:T(8,128)(2,1)S(1)}, bf16[528,256]{1,0:T(8,128)(2,1)S(1)}, u32[]{:S(2)}, u32[]{:S(2)}) collective-permute-start(bf16[528,256]{1,0:T(8,128)(2,1)S(1)} %get-tuple-element.56), channel_id=1, source_target_pairs={{64,112},{72,120},{80,64},{88,72},{96,80},{104,88},{112,96},{120,1... | collective-permute-start | bytes 811016 | tf_op jit(solution)/shard_map/ppermute | solution.py:431
  303.2 18.6 %collective-permute-start.49 = (bf16[528,256]{1,0:T(8,128)(2,1)S(1)}, bf16[528,256]{1,0:T(8,128)(2,1)S(1)}, u32[]{:S(2)}, u32[]{:S(2)}) collective-permute-start(bf16[528,256]{1,0:T(8,128)(2,1)S(1)} %get-tuple-element.55), channel_id=1, source_target_pairs={{64,96},{72,104},{80,112},{88,120},{96,64},{104,72},{112,80},{120,... | collective-permute-start | bytes 811016 | tf_op jit(solution)/shard_map/ppermute | solution.py:431
  326.4 23.5 %collective-permute-start.22 = (bf16[128,1536]{1,0:T(8,128)(2,1)S(1)}, bf16[128,1536]{1,0:T(8,128)(2,1)S(1)}, u32[]{:S(2)}, u32[]{:S(2)}) collective-permute-start(bf16[128,1536]{1,0:T(8,128)(2,1)S(1)} %get-tuple-element.43), channel_id=1, source_target_pairs={{0,4},{1,5},{2,6},{3,7},{4,0},{5,1},{6,2},{7,3},{8,12},{9,13},{10,... | collective-permute-start | bytes 1179656 | tf_op jit(solution)/shard_map/ppermute | solution.py:24
  326.8 23.0 %collective-permute-start.24 = (bf16[128,1536]{1,0:T(8,128)(2,1)S(1)}, bf16[128,1536]{1,0:T(8,128)(2,1)S(1)}, u32[]{:S(2)}, u32[]{:S(2)}) collective-permute-start(bf16[128,1536]{1,0:T(8,128)(2,1)S(1)} %get-tuple-element.32), channel_id=1, source_target_pairs={{0,1},{1,2},{2,3},{3,0},{4,5},{5,6},{6,7},{7,4},{8,9},{9,10},{10,1... | collective-permute-start | bytes 1179656 | tf_op jit(solution)/shard_map/ppermute | solution.py:28
  326.8 23.0 %collective-permute-start.25 = (bf16[128,1536]{1,0:T(8,128)(2,1)S(1)}, bf16[128,1536]{1,0:T(8,128)(2,1)S(1)}, u32[]{:S(2)}, u32[]{:S(2)}) collective-permute-start(bf16[128,1536]{1,0:T(8,128)(2,1)S(1)} %get-tuple-element.33), channel_id=1, source_target_pairs={{0,3},{1,0},{2,1},{3,2},{4,7},{5,4},{6,5},{7,6},{8,11},{9,8},{10,9... | collective-permute-start | bytes 1179656 | tf_op jit(solution)/shard_map/ppermute | solution.py:28
  369.2 24.3 %collective-permute-start.56 = (bf16[1024,512]{1,0:T(8,128)(2,1)S(1)}, bf16[1024,512]{1,0:T(8,128)(2,1)S(1)}, u32[]{:S(2)}, u32[]{:S(2)}) collective-permute-start(bf16[1024,512]{1,0:T(8,128)(2,1)S(1)} %pad_maximum_fusion.7), channel_id=1, source_target_pairs={{0,2},{1,3},{2,0},{3,1},{4,6},{5,7},{6,4},{7,5},{8,10},{9,11},{10,... | collective-permute-start | bytes 3145736 | tf_op jit(solution)/shard_map/ppermute | solution.py:28
  374.1 22.7 %collective-permute-start.58 = (bf16[1024,512]{1,0:T(8,128)(2,1)}, bf16[1024,512]{1,0:T(8,128)(2,1)}, u32[]{:S(2)}, u32[]{:S(2)}) collective-permute-start(bf16[1024,512]{1,0:T(8,128)(2,1)} %pad_maximum_fusion.8), channel_id=1, source_target_pairs={{0,4},{1,5},{2,6},{3,7},{4,0},{5,1},{6,2},{7,3},{8,12},{9,13},{10,... | collective-permute-start | bytes 3145736 | tf_op jit(solution)/shard_map/ppermute | solution.py:24
  (51 other events, 529.4 us)

commit v2 on v1

--- a/solution.py
+++ b/solution.py
@@ -28,12 +28,18 @@
     return lax.ppermute(value, "blk", [(i, (i & 4) | ((i + steps) & 3)) for i in range(8)])
 
 
-def gather_blk(own):
+def later(array, value):
+    return array + (value[0, 0].astype(F32) * 0.0).astype(array.dtype)
+
+
+def gather_blk(own, between=None):
     across = flip_x(own)
     behind = turn_z(own, 1)
     ahead = turn_z(own, 3)
     first = jnp.concatenate([own, across], axis=0)
     second = jnp.concatenate([ahead, behind], axis=0)
+    if between is not None:
+        first, second = later(first, between), later(second, between)
     opposite = turn_z(first, 2)
     diagonal = flip_x(second)
     near = jnp.concatenate([first, second], axis=0)
@@ -236,8 +242,7 @@
     )(rows, gate, up, down)
 
 
-def project_kernel(info, pooled, *refs):
-    pieces, (weights, valid, chunks, pairs, wide_own, total, squares) = refs[:8], refs[8:]
+def project_kernel(info, pooled, pieces, weights, valid, chunks, wide_own, total, squares):
     step = pl.program_id(0)
     y = info[8]
 
@@ -246,7 +251,7 @@
         total[...] = jnp.zeros_like(total)
         squares[...] = jnp.zeros_like(squares)
 
-    wide = dot(pooled[...], jnp.concatenate([piece[...] for piece in pieces], axis=0)).astype(BF16)
+    wide = dot(pooled[...], pieces[...].reshape(D1, 512)).astype(BF16)
     floats = wide.astype(F32)
     squares[...] += jnp.broadcast_to(
         jnp.sum(floats * floats, axis=-1, keepdims=True), squares.shape
@@ -273,11 +278,7 @@
                 for p in range(8):
                     start = pl.multiple_of(info[p] * 64, 64)
                     chunks[k, pl.ds(start, 64), cut] = part[p * 64 : (p + 1) * 64]
-                    if i > 0:
-                        pairs[k, pl.ds(start, 64), (i - 1) * 128 : i * 128] = part[p * 64 : (p + 1) * 64]
                 chunks[k, 512:, cut] = valid[...]
-                if i > 0:
-                    pairs[k, 512:, (i - 1) * 128 : i * 128] = valid[...]
 
 
 def project_two(info, pooled, pieces, weights, valid):
@@ -285,7 +286,6 @@
         project_kernel,
         out_shape=(
             jax.ShapeDtypeStruct((4, 512 + EXT, 384), BF16),
-            jax.ShapeDtypeStruct((4, 512 + EXT, 256), BF16),
             jax.ShapeDtypeStruct((512, 512), BF16),
         ),
         grid_spec=pltpu.PrefetchScalarGridSpec(
@@ -293,13 +293,12 @@
             grid=(8,),
             in_specs=[
                 pl.BlockSpec((512, D1), lambda s, info: (0, 0)),
-                *[pl.BlockSpec((192, 512), lambda s, info: (s, 0)) for _ in range(8)],
+                pl.BlockSpec((8, 1, 192, 512), lambda s, info: (0, s, 0, 0)),
                 pl.BlockSpec((3, 512, 512), lambda s, info: (0, info[s], 0)),
                 pl.BlockSpec((EXT, 128), lambda s, info: (0, 0)),
             ],
             out_specs=(
                 pl.BlockSpec((4, 512 + EXT, 384), lambda s, info: (0, 0, 0)),
-                pl.BlockSpec((4, 512 + EXT, 256), lambda s, info: (0, 0, 0)),
                 pl.BlockSpec((512, 512), lambda s, info: (0, 0)),
             ),
             scratch_shapes=[pltpu.VMEM((512, 1536), F32), pltpu.VMEM((512, 128), F32)],
@@ -309,7 +308,7 @@
             flops=4 * 512 * 4096 * 1536, bytes_accessed=28 * 2**20, transcendentals=512
         ),
         name="project_two",
-    )(info, pooled, *pieces, weights, valid)
+    )(info, pooled, pieces, weights, valid)
 
 
 def causal_kernel(own_part, info, queries, kv_pair, start, start_stats, out, out_stats, keys, values, even, odd):
@@ -451,28 +450,37 @@
         jnp.where(block_of[None, :] == numbers[:, None], numbers[None, :], 0), axis=1
     )
 
-    def later(number, value):
-        return number + (value[0, 0].astype(F32) * 0.0).astype(number.dtype)
-
     heads_in_flat = heads_in.transpose(1, 2, 0).reshape(3 * width, D1)
-    gate_flat, up_flat = lax.optimization_barrier((gate_up[:, 0, :], gate_up[:, 1, :]))
     core, y, half = seq_position & 1, (seq_position >> 1) & 3, seq_position >> 3
     piece = lax.dynamic_slice(widen, (seq_position * 96, 0), (96, 512))
 
     near, far = gather_blk(prepare(tokens, boundary[None, :]))
-    piece = later(jnp.concatenate([piece, flip_seq(piece, 8)], axis=0), near)
-    piece = jnp.concatenate([*gather_blk(piece), jnp.zeros((EXT, 512), BF16)], axis=0)
-    pieces = [piece, turn_y(piece, 3), turn_y(piece, 2), turn_y(piece, 1)]
+    arrived = near[2 * SENT :]
+    gates = later(gate_up, arrived)
+    gate_flat, up_flat = lax.optimization_barrier((gates[:, 0, :], gates[:, 1, :]))
     marks = jnp.concatenate(
         [part.reshape(4, SENT, D1)[:, rows, :rows] for part in (near, far)], axis=0
     )
     info = later(jnp.concatenate([place_of, seq_position[None]]).astype(jnp.int32), gate_flat)
-    qkv, edge = project_one(far, heads_in_flat, info, project_one(near, heads_in_flat))
+    piece_across = flip_seq(piece, 8)
+    info = later(info, piece_across)
+    qkv_near = project_one(near, heads_in_flat)
+    qkv, edge = project_one(far, heads_in_flat, info, qkv_near)
     halo = lax.ppermute(edge, "seq", [(i, i + 1) for i in range(15)])
     attended = window_attend(info, qkv, halo, window_attend(info, qkv))
     attn_near = dot(attended[: 4 * rows], heads_out).astype(BF16)
     attn_far = dot(attended[4 * rows :], heads_out).astype(BF16)
-    mid_stream = (tokens.astype(F32) + reduce_blk(attn_near, attn_far)).astype(BF16)
+    opposite, diagonal = reduce_first(attn_far)
+
+    piece = later(jnp.concatenate([piece, piece_across], axis=0), qkv_near)
+    pieces = jnp.concatenate(gather_blk(piece, attended), axis=0)
+    pieces = later(later(pieces, opposite), diagonal)
+    pieces = lax.all_gather(
+        pieces, "seq", axis=0, axis_index_groups=[[h * 8 + k for k in range(8)] for h in range(2)]
+    ).reshape(8, 8, 192, 512)
+    mid_stream = (
+        tokens.astype(F32) + reduce_second(attn_near, opposite, diagonal)
+    ).astype(BF16)
 
     normed_mid = normalize(mid_stream).astype(BF16)
 
@@ -496,47 +504,42 @@
         + dot(selector[:, :rows], mid_stream)
     ).astype(BF16)
     pooled_own = reduce_blk(placed[:256], placed[256:]).astype(BF16)
-    for k, value in ((1, mlp_near), (2, pooled_own), (3, mlp_near)):
-        unread = later(jnp.zeros((EXT, 512), BF16), value)
-        pieces[k] = lax.dynamic_update_slice(pieces[k], unread, (1536, 0))
-    pieces = [part for own in pieces for part in (own, flip_seq(own, 1))]
     pooled_own = jnp.concatenate(
         [
             lax.dynamic_slice(
-                pooled_own, (0, 96 * ((half ^ h) * 8 + ((y + k) & 3) * 2 + (core ^ c))), (64, 96)
+                pooled_own, (0, 96 * ((half ^ h) * 8 + k)), (64, 96)
             )
-            for k in range(4)
-            for c in range(2)
+            for k in range(8)
             for h in range(2)
         ],
         axis=1,
     )
     pooled = jnp.concatenate(gather_blk(pooled_own), axis=0)
 
-    far = later(mlp_far, pooled)
-    opposite, diagonal = reduce_first(far)
-    level_one = mid_stream.astype(F32) + reduce_second(mlp_near, opposite, diagonal)
-
     validity = (jnp.arange(capacity, dtype=jnp.int32) < span_count).astype(F32)
     valid_rows = jnp.pad(
         validity.reshape(4, 128).astype(BF16), ((0, EXT - 4), (0, 0))
     )
     info_one = jnp.concatenate([block_of, y[None]]).astype(jnp.int32)
-    chunks, pairs, wide_cols = project_two(
+    chunks, wide_cols = project_two(
         info_one, pooled, pieces, heads_in_two.transpose(1, 0, 2), valid_rows
     )
     from_behind = turn_y(chunks[1], 1)
     from_ahead = turn_y(chunks[3], 3)
     from_opposite = turn_y(chunks[2], 2)
-    first = lax.ppermute(pairs, "seq", [(i, i + 8) for i in range(8)])
+    across = [(i, i + 8) for i in range(8)]
+    first_own = lax.ppermute(chunks[:1, :, 128:], "seq", across)
     mine = jnp.stack([chunks[0], from_ahead, from_opposite, from_behind])
     queries, own_kv = mine[:, :capacity, :128], mine[:, :, 128:]
+    first_rest = lax.ppermute(own_kv[1:], "seq", across)
     info_two = jnp.stack([half, core, y]).astype(jnp.int32)
-    running = causal_attend(True, later(info_two, first[0]), queries, (own_kv, flip_seq(own_kv, 1)))
-    first_kv = jnp.stack(
-        [first[0], turn_y(first[3], 3, 8), turn_y(first[2], 2, 8), turn_y(first[1], 1, 8)]
-    )
+    running = causal_attend(
+        True, later(info_two, first_own[0]), queries, (own_kv, flip_seq(own_kv, 1))
+    )
+    first_kv = jnp.concatenate([first_own, first_rest], axis=0)
     first_kv = first_kv + running[1][0, 2, 0].astype(BF16)
+    opposite, diagonal = reduce_first(later(mlp_far, running[1][0, 2:3]))
+    level_one = mid_stream.astype(F32) + reduce_second(mlp_near, opposite, diagonal)
     mixed = causal_attend(False, info_two, queries, (first_kv, flip_seq(first_kv, 1)), running)
     back = [mixed[0], turn_y(mixed[3], 3), turn_y(mixed[2], 2), turn_y(mixed[1], 1)]
     heads = jnp.concatenate([back[0], back[1], back[2], back[3]] * 2, axis=1)

time: 421 us -> 403 us (0.957)
  between operations: 12.7 us -> 28 us
  starting transfers between devices: 79.9 us -> 67.4 us
  waiting for transfers between devices: 180 us -> 168 us
  local copies, waits for them, and re-layouts: 34.4 us -> 23.4 us
  other arithmetic: 18.5 us -> 23.1 us
    ppermute x24, waiting for transfers between devices: 86.6 us -> 58.3 us  [turn_z(): lax.ppermute(value, 'blk', [(i, i & 4 | i + steps & 3) for i in range(8)])]
    ppermute x16, waiting for transfers between devices: 48.4 us -> 67.1 us  [flip_x(): return lax.ppermute(value, 'blk', [(i, i ^ 4) for i in range(8)])]
    ppermute x7 -> x3, waiting for transfers between devices: 0.02 us -> 11.6 us  [flip_seq(): return lax.ppermute(value, 'seq', [(i, i ^ bit) for i in range(16)])]
    ppermute x12 -> x6, waiting for transfers between devices: 19.4 us -> 9.59 us  [turn_y(): lax.ppermute(value, 'seq', [(i, i & 9 | i + 2 * steps & 6) for i in range...]
    ppermute x24, starting transfers between devices: 36.3 us -> 27.5 us  [turn_z(): lax.ppermute(value, 'blk', [(i, i & 4 | i + steps & 3) for i in range(8)])]
    ppermute x1 -> x2, waiting for transfers between devices: 25.9 us -> 20.1 us  [the longest x1 13.3 us: per_device(): first_own = lax.ppermute(chunks[:1, :, 128:], 'seq', across)]
    ppermute x12 -> x6, starting transfers between devices: 23.1 us -> 17.4 us  [turn_y(): lax.ppermute(value, 'seq', [(i, i & 9 | i + 2 * steps & 6) for i in range...]
    slice x9 -> x12, local copies, waits for them, and re-layouts: 11.8 us -> 6.83 us  [the longest x11 6.08 us: later(): return array + (value[0, 0].astype(F32) * 0.0).astype(array.dtype)]
  transfers between devices with their start and end apart: 61 -> 53, of which waited for: 28 -> 32; matrix products, arithmetic and copies ran while one was open for 13% -> 11% of each run, Pallas kernels for 12% -> 12%
where the time goes in v2:
time: 403 us; the launch traced here: 396 us
  waiting for transfers between devices  168 us (42%)
  Pallas kernels  69.8 us (17%)
  starting transfers between devices  67.4 us (17%)
  between operations  28 us (7%)
  local copies, waits for them, and re-layouts  23.4 us (6%)
  other arithmetic  23.1 us (6%)
  matrix products  16.9 us (4%)
    ppermute x16, waiting for transfers between devices, flip_x(): return lax.ppermute(value, 'blk', [(i, i ^ 4) for i in range(8)])  67.1 us
    ppermute x24, waiting for transfers between devices, turn_z(): lax.ppermute(value, 'blk', [(i, i & 4 | i + steps & 3) for i in range(8)])  58.3 us
    pallas_call x2, Pallas kernels, causal_attend(): pl.pallas_call(kernel, out_shape=out_shape, grid_spec=pltpu.PrefetchScala...  30.4 us
    ppermute x24, starting transfers between devices, turn_z(): lax.ppermute(value, 'blk', [(i, i & 4 | i + steps & 3) for i in range(8)])  27.5 us
    pallas_call x1, Pallas kernels, project_two(): pl.pallas_call(project_kernel, out_shape=(jax.ShapeDtypeStruct((4, 512 +...  18.1 us
    ppermute x6, starting transfers between devices, turn_y(): lax.ppermute(value, 'seq', [(i, i & 9 | i + 2 * steps & 6) for i in range...  17.4 us
    dot_general x14, matrix products, dot(): return jnp.dot(left, right, preferred_element_type=F32)  16.9 us
    ppermute x16, starting transfers between devices, flip_x(): return lax.ppermute(value, 'blk', [(i, i ^ 4) for i in range(8)])  16.6 us
  transfers between devices with their start and end apart: 53, of which 32 were waited for; matrix products, arithmetic and copies ran while one was open for 11% of the time, Pallas kernels for 12%

profile of v2, /device:TPU:6, one launch (start us, length us, event | category | flops | bytes accessed | tf_op | source)
XLA Modules:
  0.0 396.5 jit_solution(4444370663886405197)
XLA Ops:
  9.3 4.0 %collective-permute-start = (bf16[144,1536]{1,0:T(8,128)(2,1)}, bf16[144,1536]{1,0:T(8,128)(2,1)S(1)}, u32[]{:S(2)}, u32[]{:S(2)}) collective-permute-start(bf16[144,1536]{1,0:T(8,128)(2,1)} %prepare.1), channel_id=1, source_target_pairs={{0,3},{1,0},{2,1},{3,2},{4,7},{5,4},{6,5},{7,6},{8,11},{9,8},{10,9... | collective-permute-start | bytes 1327112 | tf_op jit(solution)/shard_map/ppermute | solution.py:28
  15.6 11.6 %collective-permute-done.1 = bf16[96,512]{1,0:T(8,128)(2,1)S(1)} collective-permute-done((bf16[96,512]{1,0:T(8,128)(2,1)S(1)}, bf16[96,512]{1,0:T(8,128)(2,1)S(1)}, u32[]{:S(2)}, u32[]{:S(2)}) %collective-permute-start.1) | collective-permute-done | bytes 98336 | tf_op jit(solution)/shard_map/ppermute | solution.py:436
  39.4 12.9 %collective-permute-done.4 = bf16[288,1536]{1,0:T(8,128)(2,1)S(1)} collective-permute-done((bf16[288,1536]{1,0:T(8,128)(2,1)S(1)}, bf16[288,1536]{1,0:T(8,128)(2,1)S(1)}, u32[]{:S(2)}, u32[]{:S(2)}) %collective-permute-start.4) | collective-permute-done | bytes 884768 | tf_op jit(solution)/shard_map/ppermute | solution.py:28
  57.9 3.5 collective-permute-start.28
  61.4 4.7 %window_late.1.before = bf16[1024,192]{1,0:T(8,128)(2,1)S(1)} custom-call(s32[9]{0:T(128)S(1)} %fusion.43.info, bf16[1152,576]{1,0:T(8,128)(2,1)S(1)} %get-tuple-element.11.qkv), custom_call_target="tpu_custom_call" | custom-call | flops 251658240 | bytes 2097152 | tf_op jit(solution)/shard_map/window_late/pallas_call | solution.py:146
  67.3 4.8 %window_early.1 = bf16[1024,192]{1,0:T(8,128)(2,1)S(1)} custom-call(s32[9]{0:T(128)S(1)} %fusion.43.info, bf16[1152,576]{1,0:T(8,128)(2,1)S(1)} %get-tuple-element.11.qkv, bf16[512,384]{1,0:T(8,128)(2,1)S(1)} %collective-permute-done.6.halo, bf16[1024,192]{1,0:T(8,128)(2,1)S(1)} %window_late.1.before), custom_call_target="tpu_custom_call" | custom-call | flops 251658240 | bytes 2097152 | tf_op jit(solution)/shard_map/window_early/pallas_call | solution.py:146
  79.3 18.2 %collective-permute-done.27 = bf16[192,512]{1,0:T(8,128)(2,1)S(1)} collective-permute-done((bf16[192,512]{1,0:T(8,128)(2,1)S(1)}, bf16[192,512]{1,0:T(8,128)(2,1)S(1)}, u32[]{:S(2)}, u32[]{:S(2)}) %collective-permute-start.27) | collective-permute-done | bytes 196640 | tf_op jit(solution)/shard_map/ppermute | solution.py:24
  102.1 2.9 collective-permute-done.31
  105.0 3.3 collective-permute-done.30
  118.2 4.3 %collective-permute-done.11 = bf16[128,1536]{1,0:T(8,128)(2,1)} collective-permute-done((bf16[128,1536]{1,0:T(8,128)(2,1)}, bf16[128,1536]{1,0:T(8,128)(2,1)}, u32[]{:S(2)}, u32[]{:S(2)}) %collective-permute-start.11) | collective-permute-done | bytes 393248 | tf_op jit(solution)/shard_map/ppermute | solution.py:28
  126.7 3.5 collective-permute-start.13
  132.1 3.4 collective-permute-done.14
  136.9 5.5 %collective-permute-done.12 = bf16[128,1536]{1,0:T(8,128)(2,1)S(1)} collective-permute-done((bf16[128,1536]{1,0:T(8,128)(2,1)S(1)}, bf16[128,1536]{1,0:T(8,128)(2,1)S(1)}, u32[]{:S(2)}, u32[]{:S(2)}) %collective-permute-start.12) | collective-permute-done | bytes 393248 | tf_op jit(solution)/shard_map/ppermute | solution.py:24
  145.2 3.0 mlp.2
  148.2 6.3 %collective-permute-done.16 = bf16[256,1536]{1,0:T(8,128)(2,1)S(1)} collective-permute-done((bf16[256,1536]{1,0:T(8,128)(2,1)S(1)}, bf16[256,1536]{1,0:T(8,128)(2,1)S(1)}, u32[]{:S(2)}, u32[]{:S(2)}) %collective-permute-start.16) | collective-permute-done | bytes 786464 | tf_op jit(solution)/shard_map/ppermute | solution.py:24
  156.2 3.0 mlp.3
  162.4 6.6 %collective-permute-done.19 = bf16[128,1536]{1,0:T(8,128)(2,1)S(1)} collective-permute-done((bf16[128,1536]{1,0:T(8,128)(2,1)S(1)}, bf16[128,1536]{1,0:T(8,128)(2,1)S(1)}, u32[]{:S(2)}, u32[]{:S(2)}) %collective-permute-start.19) | collective-permute-done | bytes 393248 | tf_op jit(solution)/shard_map/ppermute | solution.py:24
  169.0 4.5 %collective-permute-done.17 = bf16[128,1536]{1,0:T(8,128)(2,1)S(1)} collective-permute-done((bf16[128,1536]{1,0:T(8,128)(2,1)S(1)}, bf16[128,1536]{1,0:T(8,128)(2,1)S(1)}, u32[]{:S(2)}, u32[]{:S(2)}) %collective-permute-start.17) | collective-permute-done | bytes 393248 | tf_op jit(solution)/shard_map/ppermute | solution.py:28
  190.4 3.3 collective-permute-done.22
  197.2 5.8 %collective-permute-done.25 = bf16[128,1536]{1,0:T(8,128)(2,1)S(1)} collective-permute-done((bf16[128,1536]{1,0:T(8,128)(2,1)S(1)}, bf16[128,1536]{1,0:T(8,128)(2,1)S(1)}, u32[]{:S(2)}, u32[]{:S(2)}) %collective-permute-start.25) | collective-permute-done | bytes 393248 | tf_op jit(solution)/shard_map/ppermute | solution.py:28
  206.3 18.1 %project_two.1 = (bf16[4,528,384]{2,1,0:T(8,128)(2,1)S(1)}, bf16[512,512]{1,0:T(8,128)(2,1)S(1)}) custom-call(s32[9]{0:T(128)S(1)} %concatenate.118.info, bf16[512,1536]{1,0:T(8,128)(2,1)S(1)} %copy-done.12, bf16[8,8,192,512]{3,2,1,0:T(8,128)(2,1)} %bitcast.103, bf16[3,4096,512]{2,1,0:T(8,128)(2,1)} %bitcast.102, bf16[16,128]{1,0:T(8,128)(2,1)S(1)} %pad.4.valid), custom_call_target="tpu_custom_call" | custom-call | flops 12884901888 | bytes 29360128 | tf_op jit(solution)/shard_map/project_two/pallas_call | solution.py:285
  224.6 8.6 %collective-permute-start.35 = (bf16[528,384]{1,0:T(8,128)(2,1)S(1)}, bf16[528,384]{1,0:T(8,128)(2,1)S(1)}, u32[]{:S(2)}, u32[]{:S(2)}) collective-permute-start(bf16[528,384]{1,0:T(8,128)(2,1)S(1)} %get-tuple-element.36), channel_id=1, source_target_pairs={{0,16},{8,24},{16,32},{24,40},{32,48},{40,56},{48,0},{56,8},{64,80... | collective-permute-start | bytes 1216520 | tf_op jit(solution)/shard_map/ppermute | solution.py:430
  236.3 3.8 collective-permute-done.35
  240.1 5.8 %collective-permute-done.34 = bf16[528,384]{1,0:T(8,128)(2,1)S(1)} collective-permute-done((bf16[528,384]{1,0:T(8,128)(2,1)S(1)}, bf16[528,384]{1,0:T(8,128)(2,1)S(1)}, u32[]{:S(2)}, u32[]{:S(2)}) %collective-permute-start.34) | collective-permute-done | bytes 405536 | tf_op jit(solution)/shard_map/ppermute | solution.py:430
  249.3 13.3 %collective-permute-done.32 = bf16[1,528,256]{2,1,0:T(8,128)(2,1)S(1)} collective-permute-done((bf16[1,528,256]{2,1,0:T(8,128)(2,1)}, bf16[1,528,256]{2,1,0:T(8,128)(2,1)S(1)}, u32[]{:S(2)}, u32[]{:S(2)}) %collective-permute-start.32) | collective-permute-done | bytes 270368 | tf_op jit(solution)/shard_map/ppermute | solution.py:531
  266.6 12.6 %causal_own.1 = (f32[4,128,512]{2,1,0:T(8,128)S(1)}, f32[4,8,512]{2,1,0:T(8,128)S(1)}) custom-call(s32[3]{0:T(128)S(1)} %get-tuple-element.20.info, bf16[4,512,128]{2,1,0:T(8,128)(2,1)S(1)} %pad_maximum_fusion.15.queries, bf16[4,528,256]{2,1,0:T(8,128)(2,1)} %pad_maximum_fusion.4.kv, bf16[4,528,256]{2,1,0:T(8,128)(2,1)} %collective-permute-done.36.other), custom_call_target="tpu_custom_call" | custom-call | flops 2415919104 | bytes 4194304 | tf_op jit(solution)/shard_map/causal_own/pallas_call | solution.py:406
  282.6 6.9 %collective-permute-done.42 = bf16[3,528,256]{2,1,0:T(8,128)(2,1)S(1)} collective-permute-done((bf16[3,528,256]{2,1,0:T(8,128)(2,1)S(1)}, bf16[3,528,256]{2,1,0:T(8,128)(2,1)S(1)}, u32[]{:S(2)}, u32[]{:S(2)}) %collective-permute-start.42) | collective-permute-done | bytes 811040 | tf_op jit(solution)/shard_map/ppermute | solution.py:534
  290.4 11.3 %collective-permute-done.39 = bf16[256,1536]{1,0:T(8,128)(2,1)} collective-permute-done((bf16[256,1536]{1,0:T(8,128)(2,1)}, bf16[256,1536]{1,0:T(8,128)(2,1)}, u32[]{:S(2)}, u32[]{:S(2)}) %collective-permute-start.39) | collective-permute-done | bytes 786464 | tf_op jit(solution)/shard_map/ppermute | solution.py:24
  308.6 17.8 %causal_first_half.1 = bf16[4,512,128]{2,1,0:T(8,128)(2,1)S(1)} custom-call(s32[3]{0:T(128)S(1)} %get-tuple-element.21.info, bf16[4,512,128]{2,1,0:T(8,128)(2,1)S(1)} %copy-done.10, bf16[4,528,256]{2,1,0:T(8,128)(2,1)S(1)} %maximum_add_fusion.1.kv, bf16[4,528,256]{2,1,0:T(8,128)(2,1)} %collective-permute-done.43.other, f32[4,128,512]{2,1,0:T(8,128)S(1)} %copy-done.15, ...), custom_call_target="tpu_custom_call" | custom-call | flops 4294967296 | bytes 4194304 | tf_op jit(solution)/shard_map/causal_first_half/pallas_call | solution.py:406
  357.0 9.1 %collective-permute-done.49 = bf16[1024,512]{1,0:T(8,128)(2,1)} collective-permute-done((bf16[1024,512]{1,0:T(8,128)(2,1)S(1)}, bf16[1024,512]{1,0:T(8,128)(2,1)}, u32[]{:S(2)}, u32[]{:S(2)}) %collective-permute-start.49) | collective-permute-done | bytes 1048608 | tf_op jit(solution)/shard_map/ppermute | solution.py:24
  366.1 6.0 %collective-permute-done.47 = bf16[1024,512]{1,0:T(8,128)(2,1)S(1)} collective-permute-done((bf16[1024,512]{1,0:T(8,128)(2,1)}, bf16[1024,512]{1,0:T(8,128)(2,1)S(1)}, u32[]{:S(2)}, u32[]{:S(2)}) %collective-permute-start.47) | collective-permute-done | bytes 1048608 | tf_op jit(solution)/shard_map/ppermute | solution.py:28
  377.6 6.7 %collective-permute-done.51 = bf16[512,512]{1,0:T(8,128)(2,1)S(1)} collective-permute-done((bf16[512,512]{1,0:T(8,128)(2,1)S(1)}, bf16[512,512]{1,0:T(8,128)(2,1)S(1)}, u32[]{:S(2)}, u32[]{:S(2)}) %collective-permute-start.51) | collective-permute-done | bytes 524320 | tf_op jit(solution)/shard_map/ppermute | solution.py:28
  (271 shorter events, 133.5 us)
Async XLA Ops:
  7.2 197.7 %all-gather.2.cloned.1.call-start = ((), (), s32[]{:S(2)}) async-start(), calls=%async_computation | async-start | bytes 14155776 | tf_op jit(solution)/shard_map/all_gather | solution.py:478
  9.3 19.0 %collective-permute-start = (bf16[144,1536]{1,0:T(8,128)(2,1)}, bf16[144,1536]{1,0:T(8,128)(2,1)S(1)}, u32[]{:S(2)}, u32[]{:S(2)}) collective-permute-start(bf16[144,1536]{1,0:T(8,128)(2,1)} %prepare.1), channel_id=1, source_target_pairs={{0,3},{1,0},{2,1},{3,2},{4,7},{5,4},{6,5},{7,6},{8,11},{9,8},{10,9... | collective-permute-start | bytes 1327112 | tf_op jit(solution)/shard_map/ppermute | solution.py:28
  13.3 16.3 %collective-permute-start.2 = (bf16[144,1536]{1,0:T(8,128)(2,1)}, bf16[144,1536]{1,0:T(8,128)(2,1)S(1)}, u32[]{:S(2)}, u32[]{:S(2)}) collective-permute-start(bf16[144,1536]{1,0:T(8,128)(2,1)} %prepare.1), channel_id=1, source_target_pairs={{0,4},{1,5},{2,6},{3,7},{4,0},{5,1},{6,2},{7,3},{8,12},{9,13},{10,... | collective-permute-start | bytes 1327112 | tf_op jit(solution)/shard_map/ppermute | solution.py:24
  14.1 16.9 %collective-permute-start.3 = (bf16[144,1536]{1,0:T(8,128)(2,1)}, bf16[144,1536]{1,0:T(8,128)(2,1)S(1)}, u32[]{:S(2)}, u32[]{:S(2)}) collective-permute-start(bf16[144,1536]{1,0:T(8,128)(2,1)} %prepare.1), channel_id=1, source_target_pairs={{0,1},{1,2},{2,3},{3,0},{4,5},{5,6},{6,7},{7,4},{8,9},{9,10},{10,1... | collective-permute-start | bytes 1327112 | tf_op jit(solution)/shard_map/ppermute | solution.py:28
  14.2 13.0 %collective-permute-start.1 = (bf16[96,512]{1,0:T(8,128)(2,1)S(1)}, bf16[96,512]{1,0:T(8,128)(2,1)S(1)}, u32[]{:S(2)}, u32[]{:S(2)}) collective-permute-start(bf16[96,512]{1,0:T(8,128)(2,1)S(1)} %constant_dynamic-slice_fusion.16), channel_id=1, source_target_pairs={{0,64},{8,72},{16,80},{24,88},{32,96},{40,104},{48,112},{56,120},{... | collective-permute-start | bytes 294920 | tf_op jit(solution)/shard_map/ppermute | solution.py:436
  30.8 21.5 %collective-permute-start.4 = (bf16[288,1536]{1,0:T(8,128)(2,1)S(1)}, bf16[288,1536]{1,0:T(8,128)(2,1)S(1)}, u32[]{:S(2)}, u32[]{:S(2)}) collective-permute-start(bf16[288,1536]{1,0:T(8,128)(2,1)S(1)} %pad_maximum_fusion.9), channel_id=1, source_target_pairs={{0,2},{1,3},{2,0},{3,1},{4,6},{5,7},{6,4},{7,5},{8,10},{9,11},{10,... | collective-permute-start | bytes 2654216 | tf_op jit(solution)/shard_map/ppermute | solution.py:28
  31.1 21.3 %collective-permute-start.5 = (bf16[288,1536]{1,0:T(8,128)(2,1)S(1)}, bf16[288,1536]{1,0:T(8,128)(2,1)S(1)}, u32[]{:S(2)}, u32[]{:S(2)}) collective-permute-start(bf16[288,1536]{1,0:T(8,128)(2,1)S(1)} %pad_maximum_fusion.10), channel_id=1, source_target_pairs={{0,4},{1,5},{2,6},{3,7},{4,0},{5,1},{6,2},{7,3},{8,12},{9,13},{10,... | collective-permute-start | bytes 2654216 | tf_op jit(solution)/shard_map/ppermute | solution.py:24
  54.6 12.7 %collective-permute-start.6 = (bf16[512,384]{1,0:T(8,128)(2,1)S(1)}, bf16[512,384]{1,0:T(8,128)(2,1)S(1)}, u32[]{:S(2)}, u32[]{:S(2)}) collective-permute-start(bf16[512,384]{1,0:T(8,128)(2,1)S(1)} %get-tuple-element.12), channel_id=1, source_target_pairs={{0,8},{8,16},{16,24},{24,32},{32,40},{40,48},{48,56},{56,64},{64,7... | collective-permute-start | bytes 1179656 | tf_op jit(solution)/shard_map/ppermute | solution.py:469
  57.8 20.2 %collective-permute-start.29 = (bf16[192,512]{1,0:T(8,128)(2,1)S(1)}, bf16[192,512]{1,0:T(8,128)(2,1)S(1)}, u32[]{:S(2)}, u32[]{:S(2)}) collective-permute-start(bf16[192,512]{1,0:T(8,128)(2,1)S(1)} %maximum_add_fusion.4), channel_id=1, source_target_pairs={{0,1},{1,2},{2,3},{3,0},{4,5},{5,6},{6,7},{7,4},{8,9},{9,10},{10,1... | collective-permute-start | bytes 589832 | tf_op jit(solution)/shard_map/ppermute | solution.py:28
  57.9 20.1 %collective-permute-start.28 = (bf16[192,512]{1,0:T(8,128)(2,1)S(1)}, bf16[192,512]{1,0:T(8,128)(2,1)S(1)}, u32[]{:S(2)}, u32[]{:S(2)}) collective-permute-start(bf16[192,512]{1,0:T(8,128)(2,1)S(1)} %maximum_add_fusion.4), channel_id=1, source_target_pairs={{0,3},{1,0},{2,1},{3,2},{4,7},{5,4},{6,5},{7,6},{8,11},{9,8},{10,9... | collective-permute-start | bytes 589832 | tf_op jit(solution)/shard_map/ppermute | solution.py:28
  72.9 26.8 %collective-permute-start.9 = (bf16[256,1536]{1,0:T(8,128)(2,1)S(1)}, bf16[256,1536]{1,0:T(8,128)(2,1)S(1)}, u32[]{:S(2)}, u32[]{:S(2)}) collective-permute-start(bf16[256,1536]{1,0:T(8,128)(2,1)S(1)} %get-tuple-element.47), channel_id=1, source_target_pairs={{0,4},{1,5},{2,6},{3,7},{4,0},{5,1},{6,2},{7,3},{8,12},{9,13},{10,... | collective-permute-start | bytes 2359304 | tf_op jit(solution)/shard_map/ppermute | solution.py:24
  74.1 26.7 %collective-permute-start.7 = (bf16[256,1536]{1,0:T(8,128)(2,1)S(1)}, bf16[256,1536]{1,0:T(8,128)(2,1)S(1)}, u32[]{:S(2)}, u32[]{:S(2)}) collective-permute-start(bf16[256,1536]{1,0:T(8,128)(2,1)S(1)} %get-tuple-element.46), channel_id=1, source_target_pairs={{0,2},{1,3},{2,0},{3,1},{4,6},{5,7},{6,4},{7,5},{8,10},{9,11},{10,... | collective-permute-start | bytes 2359304 | tf_op jit(solution)/shard_map/ppermute | solution.py:28
  76.0 21.6 %collective-permute-start.27 = (bf16[192,512]{1,0:T(8,128)(2,1)S(1)}, bf16[192,512]{1,0:T(8,128)(2,1)S(1)}, u32[]{:S(2)}, u32[]{:S(2)}) collective-permute-start(bf16[192,512]{1,0:T(8,128)(2,1)S(1)} %maximum_add_fusion.4), channel_id=1, source_target_pairs={{0,4},{1,5},{2,6},{3,7},{4,0},{5,1},{6,2},{7,3},{8,12},{9,13},{10,... | collective-permute-start | bytes 589832 | tf_op jit(solution)/shard_map/ppermute | solution.py:24
  78.1 26.9 %collective-permute-start.31 = (bf16[384,512]{1,0:T(8,128)(2,1)S(1)}, bf16[384,512]{1,0:T(8,128)(2,1)S(1)}, u32[]{:S(2)}, u32[]{:S(2)}) collective-permute-start(bf16[384,512]{1,0:T(8,128)(2,1)S(1)} %maximum_add_fusion.3), channel_id=1, source_target_pairs={{0,4},{1,5},{2,6},{3,7},{4,0},{5,1},{6,2},{7,3},{8,12},{9,13},{10,... | collective-permute-start | bytes 1179656 | tf_op jit(solution)/shard_map/ppermute | solution.py:24
  130.5 12.0 %collective-permute-start.12 = (bf16[128,1536]{1,0:T(8,128)(2,1)S(1)}, bf16[128,1536]{1,0:T(8,128)(2,1)S(1)}, u32[]{:S(2)}, u32[]{:S(2)}) collective-permute-start(bf16[128,1536]{1,0:T(8,128)(2,1)S(1)} %fusion.11), channel_id=1, source_target_pairs={{0,4},{1,5},{2,6},{3,7},{4,0},{5,1},{6,2},{7,3},{8,12},{9,13},{10,... | collective-permute-start | bytes 1179656 | tf_op jit(solution)/shard_map/ppermute | solution.py:24
  135.5 19.0 %collective-permute-start.16 = (bf16[256,1536]{1,0:T(8,128)(2,1)S(1)}, bf16[256,1536]{1,0:T(8,128)(2,1)S(1)}, u32[]{:S(2)}, u32[]{:S(2)}) collective-permute-start(bf16[256,1536]{1,0:T(8,128)(2,1)S(1)} %pad_maximum_fusion.14), channel_id=1, source_target_pairs={{0,4},{1,5},{2,6},{3,7},{4,0},{5,1},{6,2},{7,3},{8,12},{9,13},{10,... | collective-permute-start | bytes 2359304 | tf_op jit(solution)/shard_map/ppermute | solution.py:24
  142.5 13.6 %collective-permute-start.15 = (bf16[256,1536]{1,0:T(8,128)(2,1)S(1)}, bf16[256,1536]{1,0:T(8,128)(2,1)S(1)}, u32[]{:S(2)}, u32[]{:S(2)}) collective-permute-start(bf16[256,1536]{1,0:T(8,128)(2,1)S(1)} %pad_maximum_fusion.13), channel_id=1, source_target_pairs={{0,2},{1,3},{2,0},{3,1},{4,6},{5,7},{6,4},{7,5},{8,10},{9,11},{10,... | collective-permute-start | bytes 2359304 | tf_op jit(solution)/shard_map/ppermute | solution.py:28
  224.6 15.5 %collective-permute-start.35 = (bf16[528,384]{1,0:T(8,128)(2,1)S(1)}, bf16[528,384]{1,0:T(8,128)(2,1)S(1)}, u32[]{:S(2)}, u32[]{:S(2)}) collective-permute-start(bf16[528,384]{1,0:T(8,128)(2,1)S(1)} %get-tuple-element.36), channel_id=1, source_target_pairs={{0,16},{8,24},{16,32},{24,40},{32,48},{40,56},{48,0},{56,8},{64,80... | collective-permute-start | bytes 1216520 | tf_op jit(solution)/shard_map/ppermute | solution.py:430
  233.2 12.7 %collective-permute-start.34 = (bf16[528,384]{1,0:T(8,128)(2,1)S(1)}, bf16[528,384]{1,0:T(8,128)(2,1)S(1)}, u32[]{:S(2)}, u32[]{:S(2)}) collective-permute-start(bf16[528,384]{1,0:T(8,128)(2,1)S(1)} %get-tuple-element.37), channel_id=1, source_target_pairs={{0,32},{8,40},{16,48},{24,56},{32,0},{40,8},{48,16},{56,24},{64,96... | collective-permute-start | bytes 1216520 | tf_op jit(solution)/shard_map/ppermute | solution.py:430
  247.2 19.4 %collective-permute-start.36 = (bf16[4,528,256]{2,1,0:T(8,128)(2,1)}, bf16[4,528,256]{2,1,0:T(8,128)(2,1)}, u32[]{:S(2)}, u32[]{:S(2)}) collective-permute-start(bf16[4,528,256]{2,1,0:T(8,128)(2,1)} %pad_maximum_fusion.4.kv), channel_id=1, source_target_pairs={{0,8},{8,0},{16,24},{24,16},{32,40},{40,32},{48,56},{56,48},{64,72... | collective-permute-start | bytes 3244040 | tf_op jit(solution)/shard_map/ppermute | solution.py:436
  247.9 14.6 %collective-permute-start.32 = (bf16[1,528,256]{2,1,0:T(8,128)(2,1)}, bf16[1,528,256]{2,1,0:T(8,128)(2,1)S(1)}, u32[]{:S(2)}, u32[]{:S(2)}) collective-permute-start(bf16[1,528,256]{2,1,0:T(8,128)(2,1)} %slice.294), channel_id=1, source_target_pairs={{0,64},{8,72},{16,80},{24,88},{32,96},{40,104},{48,112},{56,120},{... | collective-permute-start | bytes 811016 | tf_op jit(solution)/shard_map/ppermute | solution.py:531
  265.1 24.3 %collective-permute-start.42 = (bf16[3,528,256]{2,1,0:T(8,128)(2,1)S(1)}, bf16[3,528,256]{2,1,0:T(8,128)(2,1)S(1)}, u32[]{:S(2)}, u32[]{:S(2)}) collective-permute-start(bf16[3,528,256]{2,1,0:T(8,128)(2,1)S(1)} %pad_maximum_fusion.11), channel_id=1, source_target_pairs={{0,64},{8,72},{16,80},{24,88},{32,96},{40,104},{48,112},{56,120},{... | collective-permute-start | bytes 2433032 | tf_op jit(solution)/shard_map/ppermute | solution.py:534
  282.0 19.7 %collective-permute-start.39 = (bf16[256,1536]{1,0:T(8,128)(2,1)}, bf16[256,1536]{1,0:T(8,128)(2,1)}, u32[]{:S(2)}, u32[]{:S(2)}) collective-permute-start(bf16[256,1536]{1,0:T(8,128)(2,1)} %get-tuple-element.41), channel_id=1, source_target_pairs={{0,4},{1,5},{2,6},{3,7},{4,0},{5,1},{6,2},{7,3},{8,12},{9,13},{10,... | collective-permute-start | bytes 2359304 | tf_op jit(solution)/shard_map/ppermute | solution.py:24
  282.0 21.2 %collective-permute-start.37 = (bf16[256,1536]{1,0:T(8,128)(2,1)}, bf16[256,1536]{1,0:T(8,128)(2,1)}, u32[]{:S(2)}, u32[]{:S(2)}) collective-permute-start(bf16[256,1536]{1,0:T(8,128)(2,1)} %get-tuple-element.40), channel_id=1, source_target_pairs={{0,2},{1,3},{2,0},{3,1},{4,6},{5,7},{6,4},{7,5},{8,10},{9,11},{10,... | collective-permute-start | bytes 2359304 | tf_op jit(solution)/shard_map/ppermute | solution.py:28
  290.2 18.3 %collective-permute-start.43 = (bf16[4,528,256]{2,1,0:T(8,128)(2,1)S(1)}, bf16[4,528,256]{2,1,0:T(8,128)(2,1)}, u32[]{:S(2)}, u32[]{:S(2)}) collective-permute-start(bf16[4,528,256]{2,1,0:T(8,128)(2,1)S(1)} %maximum_add_fusion.1.kv), channel_id=1, source_target_pairs={{0,8},{8,0},{16,24},{24,16},{32,40},{40,32},{48,56},{56,48},{64,72... | collective-permute-start | bytes 3244040 | tf_op jit(solution)/shard_map/ppermute | solution.py:436
  304.7 27.7 %collective-permute-start.41 = (bf16[128,1536]{1,0:T(8,128)(2,1)S(1)}, bf16[128,1536]{1,0:T(8,128)(2,1)S(1)}, u32[]{:S(2)}, u32[]{:S(2)}) collective-permute-start(bf16[128,1536]{1,0:T(8,128)(2,1)S(1)} %get-tuple-element.29), channel_id=1, source_target_pairs={{0,3},{1,0},{2,1},{3,2},{4,7},{5,4},{6,5},{7,6},{8,11},{9,8},{10,9... | collective-permute-start | bytes 1179656 | tf_op jit(solution)/shard_map/ppermute | solution.py:28
  304.8 29.3 %collective-permute-start.40 = (bf16[128,1536]{1,0:T(8,128)(2,1)S(1)}, bf16[128,1536]{1,0:T(8,128)(2,1)S(1)}, u32[]{:S(2)}, u32[]{:S(2)}) collective-permute-start(bf16[128,1536]{1,0:T(8,128)(2,1)S(1)} %get-tuple-element.28), channel_id=1, source_target_pairs={{0,1},{1,2},{2,3},{3,0},{4,5},{5,6},{6,7},{7,4},{8,9},{9,10},{10,1... | collective-permute-start | bytes 1179656 | tf_op jit(solution)/shard_map/ppermute | solution.py:28
  306.8 27.3 %collective-permute-start.38 = (bf16[128,1536]{1,0:T(8,128)(2,1)S(1)}, bf16[128,1536]{1,0:T(8,128)(2,1)S(1)}, u32[]{:S(2)}, u32[]{:S(2)}) collective-permute-start(bf16[128,1536]{1,0:T(8,128)(2,1)S(1)} %get-tuple-element.39), channel_id=1, source_target_pairs={{0,4},{1,5},{2,6},{3,7},{4,0},{5,1},{6,2},{7,3},{8,12},{9,13},{10,... | collective-permute-start | bytes 1179656 | tf_op jit(solution)/shard_map/ppermute | solution.py:24
  328.3 12.1 %collective-permute-start.44 = (bf16[512,128]{1,0:T(8,128)(2,1)}, bf16[512,128]{1,0:T(8,128)(2,1)S(1)}, u32[]{:S(2)}, u32[]{:S(2)}) collective-permute-start(bf16[512,128]{1,0:T(8,128)(2,1)} %get-tuple-element.50), channel_id=1, source_target_pairs={{0,48},{8,56},{16,0},{24,8},{32,16},{40,24},{48,32},{56,40},{64,11... | collective-permute-start | bytes 393224 | tf_op jit(solution)/shard_map/ppermute | solution.py:430
  343.7 22.3 %collective-permute-start.49 = (bf16[1024,512]{1,0:T(8,128)(2,1)S(1)}, bf16[1024,512]{1,0:T(8,128)(2,1)}, u32[]{:S(2)}, u32[]{:S(2)}) collective-permute-start(bf16[1024,512]{1,0:T(8,128)(2,1)S(1)} %pad_maximum_fusion.8), channel_id=1, source_target_pairs={{0,4},{1,5},{2,6},{3,7},{4,0},{5,1},{6,2},{7,3},{8,12},{9,13},{10,... | collective-permute-start | bytes 3145736 | tf_op jit(solution)/shard_map/ppermute | solution.py:24
  348.1 23.9 %collective-permute-start.47 = (bf16[1024,512]{1,0:T(8,128)(2,1)}, bf16[1024,512]{1,0:T(8,128)(2,1)S(1)}, u32[]{:S(2)}, u32[]{:S(2)}) collective-permute-start(bf16[1024,512]{1,0:T(8,128)(2,1)} %pad_maximum_fusion.7), channel_id=1, source_target_pairs={{0,2},{1,3},{2,0},{3,1},{4,6},{5,7},{6,4},{7,5},{8,10},{9,11},{10,... | collective-permute-start | bytes 3145736 | tf_op jit(solution)/shard_map/ppermute | solution.py:28
  375.7 11.3 %collective-permute-start.50 = (bf16[512,512]{1,0:T(8,128)(2,1)S(1)}, bf16[512,512]{1,0:T(8,128)(2,1)S(1)}, u32[]{:S(2)}, u32[]{:S(2)}) collective-permute-start(bf16[512,512]{1,0:T(8,128)(2,1)S(1)} %get-tuple-element.24), channel_id=1, source_target_pairs={{0,1},{1,2},{2,3},{3,0},{4,5},{5,6},{6,7},{7,4},{8,9},{9,10},{10,1... | collective-permute-start | bytes 1572872 | tf_op jit(solution)/shard_map/ppermute | solution.py:28
  (62 other events, 537.3 us)
Sparse Core Ops, SparseCore 0:
  110.0 67.1 all-gather.1

commit v3 on v2

--- a/solution.py
+++ b/solution.py
@@ -456,14 +456,13 @@
 
     near, far = gather_blk(prepare(tokens, boundary[None, :]))
     arrived = near[2 * SENT :]
+    piece_across = flip_seq(piece, 8)
     gates = later(gate_up, arrived)
     gate_flat, up_flat = lax.optimization_barrier((gates[:, 0, :], gates[:, 1, :]))
     marks = jnp.concatenate(
         [part.reshape(4, SENT, D1)[:, rows, :rows] for part in (near, far)], axis=0
     )
     info = later(jnp.concatenate([place_of, seq_position[None]]).astype(jnp.int32), gate_flat)
-    piece_across = flip_seq(piece, 8)
-    info = later(info, piece_across)
     qkv_near = project_one(near, heads_in_flat)
     qkv, edge = project_one(far, heads_in_flat, info, qkv_near)
     halo = lax.ppermute(edge, "seq", [(i, i + 1) for i in range(15)])
@@ -472,8 +471,8 @@
     attn_far = dot(attended[4 * rows :], heads_out).astype(BF16)
     opposite, diagonal = reduce_first(attn_far)
 
-    piece = later(jnp.concatenate([piece, piece_across], axis=0), qkv_near)
-    pieces = jnp.concatenate(gather_blk(piece, attended), axis=0)
+    piece = later(jnp.concatenate([piece, piece_across], axis=0), qkv)
+    pieces = jnp.concatenate(gather_blk(piece, halo), axis=0)
     pieces = later(later(pieces, opposite), diagonal)
     pieces = lax.all_gather(
         pieces, "seq", axis=0, axis_index_groups=[[h * 8 + k for k in range(8)] for h in range(2)]
@@ -524,26 +523,24 @@
     chunks, wide_cols = project_two(
         info_one, pooled, pieces, heads_in_two.transpose(1, 0, 2), valid_rows
     )
+    opposite, diagonal = reduce_first(later(mlp_far, chunks[0]))
     from_behind = turn_y(chunks[1], 1)
     from_ahead = turn_y(chunks[3], 3)
     from_opposite = turn_y(chunks[2], 2)
-    across = [(i, i + 8) for i in range(8)]
-    first_own = lax.ppermute(chunks[:1, :, 128:], "seq", across)
     mine = jnp.stack([chunks[0], from_ahead, from_opposite, from_behind])
     queries, own_kv = mine[:, :capacity, :128], mine[:, :, 128:]
-    first_rest = lax.ppermute(own_kv[1:], "seq", across)
+    first_kv = lax.ppermute(own_kv, "seq", [(i, i + 8) for i in range(8)])
     info_two = jnp.stack([half, core, y]).astype(jnp.int32)
-    running = causal_attend(
-        True, later(info_two, first_own[0]), queries, (own_kv, flip_seq(own_kv, 1))
-    )
-    first_kv = jnp.concatenate([first_own, first_rest], axis=0)
+    running = causal_attend(True, info_two, queries, (own_kv, flip_seq(own_kv, 1)))
     first_kv = first_kv + running[1][0, 2, 0].astype(BF16)
-    opposite, diagonal = reduce_first(later(mlp_far, running[1][0, 2:3]))
-    level_one = mid_stream.astype(F32) + reduce_second(mlp_near, opposite, diagonal)
+    level_one = mid_stream.astype(F32) + reduce_second(
+        later(mlp_near, running[1][0, 2:3]), opposite, diagonal
+    )
     mixed = causal_attend(False, info_two, queries, (first_kv, flip_seq(first_kv, 1)), running)
     back = [mixed[0], turn_y(mixed[3], 3), turn_y(mixed[2], 2), turn_y(mixed[1], 1)]
     heads = jnp.concatenate([back[0], back[1], back[2], back[3]] * 2, axis=1)
     attended_two = lax.dynamic_slice(heads, (0, ((4 - y) & 3) * 128), (capacity, 512))
+
 
     level_one = later(level_one, mixed[0]).astype(BF16)
     column_of = later(block_of, level_one)

time: 403 us -> 412 us (1.022)
  the two profiles are of different devices: /device:TPU:6 before, /device:TPU:0 now
where the time goes in v3:
time: 412 us; the launch traced here: 406 us
  waiting for transfers between devices  188 us (46%)
  starting transfers between devices  71.6 us (17%)
  Pallas kernels  54.9 us (13%)
  between operations  27.1 us (7%)
  local copies, waits for them, and re-layouts  26.6 us (6%)
  other arithmetic  22.3 us (5%)
  matrix products  15.7 us (4%)
    ppermute x16, waiting for transfers between devices, flip_x(): return lax.ppermute(value, 'blk', [(i, i ^ 4) for i in range(8)])  82.1 us
    ppermute x24, waiting for transfers between devices, turn_z(): lax.ppermute(value, 'blk', [(i, i & 4 | i + steps & 3) for i in range(8)])  79.8 us
    ppermute x24, starting transfers between devices, turn_z(): lax.ppermute(value, 'blk', [(i, i & 4 | i + steps & 3) for i in range(8)])  30.9 us
    pallas_call x1, Pallas kernels, project_two(): pl.pallas_call(project_kernel, out_shape=(jax.ShapeDtypeStruct((4, 512 +...  18.1 us
    dot_general x14, matrix products, dot(): return jnp.dot(left, right, preferred_element_type=F32)  15.7 us
    ppermute x6, starting transfers between devices, turn_y(): lax.ppermute(value, 'seq', [(i, i & 9 | i + 2 * steps & 6) for i in range...  15 us
    ppermute x16, starting transfers between devices, flip_x(): return lax.ppermute(value, 'blk', [(i, i ^ 4) for i in range(8)])  14.9 us
    pallas_call x2, Pallas kernels, causal_attend(): pl.pallas_call(kernel, out_shape=out_shape, grid_spec=pltpu.PrefetchScala...  14.5 us
  transfers between devices with their start and end apart: 52, of which 33 were waited for; matrix products, arithmetic and copies ran while one was open for 10% of the time, Pallas kernels for 8%

profile of v3, /device:TPU:0, one launch (start us, length us, event | category | flops | bytes accessed | tf_op | source)
XLA Modules:
  0.0 405.7 jit_solution(4953017198779289520)
XLA Ops:
  10.8 4.0 collective-permute-start
  15.1 6.1 %collective-permute-done.1 = bf16[144,1536]{1,0:T(8,128)(2,1)S(1)} collective-permute-done((bf16[144,1536]{1,0:T(8,128)(2,1)}, bf16[144,1536]{1,0:T(8,128)(2,1)S(1)}, u32[]{:S(2)}, u32[]{:S(2)}) %collective-permute-start.1) | collective-permute-done | bytes 442400 | tf_op jit(solution)/shard_map/ppermute | solution.py:24
  22.4 4.2 %collective-permute-start.3 = (bf16[288,1536]{1,0:T(8,128)(2,1)S(1)}, bf16[288,1536]{1,0:T(8,128)(2,1)S(1)}, u32[]{:S(2)}, u32[]{:S(2)}) collective-permute-start(bf16[288,1536]{1,0:T(8,128)(2,1)S(1)} %pad_maximum_fusion.9), channel_id=1, source_target_pairs={{0,2},{1,3},{2,0},{3,1},{4,6},{5,7},{6,4},{7,5},{8,10},{9,11},{10,... | collective-permute-start | bytes 2654216 | tf_op jit(solution)/shard_map/ppermute | solution.py:28
  26.7 19.9 %collective-permute-done.2 = bf16[144,1536]{1,0:T(8,128)(2,1)S(1)} collective-permute-done((bf16[144,1536]{1,0:T(8,128)(2,1)}, bf16[144,1536]{1,0:T(8,128)(2,1)S(1)}, u32[]{:S(2)}, u32[]{:S(2)}) %collective-permute-start.2) | collective-permute-done | bytes 442400 | tf_op jit(solution)/shard_map/ppermute | solution.py:28
  56.1 3.7 collective-permute-done.4
  72.6 3.5 collective-permute-start.28
  77.5 4.8 %window_late.1.before = bf16[1024,192]{1,0:T(8,128)(2,1)S(1)} custom-call(s32[9]{0:T(128)S(1)} %add_add_fusion.info, bf16[1152,576]{1,0:T(8,128)(2,1)S(1)} %copy-done.4), custom_call_target="tpu_custom_call" | custom-call | flops 251658240 | bytes 2097152 | tf_op jit(solution)/shard_map/window_late/pallas_call | solution.py:146
  82.3 5.3 %window_early.1 = bf16[1024,192]{1,0:T(8,128)(2,1)S(1)} custom-call(s32[9]{0:T(128)S(1)} %add_add_fusion.info, bf16[1152,576]{1,0:T(8,128)(2,1)S(1)} %copy-done.4, bf16[512,384]{1,0:T(8,128)(2,1)} %collective-permute-done.5.halo, bf16[1024,192]{1,0:T(8,128)(2,1)S(1)} %window_late.1.before), custom_call_target="tpu_custom_call" | custom-call | flops 251658240 | bytes 2097152 | tf_op jit(solution)/shard_map/window_early/pallas_call | solution.py:146
  93.0 20.1 %collective-permute-done.27 = bf16[192,512]{1,0:T(8,128)(2,1)S(1)} collective-permute-done((bf16[192,512]{1,0:T(8,128)(2,1)S(1)}, bf16[192,512]{1,0:T(8,128)(2,1)S(1)}, u32[]{:S(2)}, u32[]{:S(2)}) %collective-permute-start.27) | collective-permute-done | bytes 196640 | tf_op jit(solution)/shard_map/ppermute | solution.py:24
  115.6 4.7 %collective-permute-done.31 = bf16[384,512]{1,0:T(8,128)(2,1)S(1)} collective-permute-done((bf16[384,512]{1,0:T(8,128)(2,1)S(1)}, bf16[384,512]{1,0:T(8,128)(2,1)S(1)}, u32[]{:S(2)}, u32[]{:S(2)}) %collective-permute-start.31) | collective-permute-done | bytes 393248 | tf_op jit(solution)/shard_map/ppermute | solution.py:24
  132.0 4.1 collective-permute-done.10
  140.3 3.7 collective-permute-start.12
  145.6 3.7 collective-permute-done.13
  150.4 6.0 %collective-permute-done.11 = bf16[128,1536]{1,0:T(8,128)(2,1)S(1)} collective-permute-done((bf16[128,1536]{1,0:T(8,128)(2,1)S(1)}, bf16[128,1536]{1,0:T(8,128)(2,1)S(1)}, u32[]{:S(2)}, u32[]{:S(2)}) %collective-permute-start.11) | collective-permute-done | bytes 393248 | tf_op jit(solution)/shard_map/ppermute | solution.py:24
  162.2 6.5 %collective-permute-done.15 = bf16[256,1536]{1,0:T(8,128)(2,1)S(1)} collective-permute-done((bf16[256,1536]{1,0:T(8,128)(2,1)S(1)}, bf16[256,1536]{1,0:T(8,128)(2,1)S(1)}, u32[]{:S(2)}, u32[]{:S(2)}) %collective-permute-start.15) | collective-permute-done | bytes 786464 | tf_op jit(solution)/shard_map/ppermute | solution.py:24
  176.2 6.9 %collective-permute-done.18 = bf16[128,1536]{1,0:T(8,128)(2,1)S(1)} collective-permute-done((bf16[128,1536]{1,0:T(8,128)(2,1)S(1)}, bf16[128,1536]{1,0:T(8,128)(2,1)S(1)}, u32[]{:S(2)}, u32[]{:S(2)}) %collective-permute-start.18) | collective-permute-done | bytes 393248 | tf_op jit(solution)/shard_map/ppermute | solution.py:24
  183.1 4.5 %collective-permute-done.16 = bf16[128,1536]{1,0:T(8,128)(2,1)S(1)} collective-permute-done((bf16[128,1536]{1,0:T(8,128)(2,1)S(1)}, bf16[128,1536]{1,0:T(8,128)(2,1)S(1)}, u32[]{:S(2)}, u32[]{:S(2)}) %collective-permute-start.16) | collective-permute-done | bytes 393248 | tf_op jit(solution)/shard_map/ppermute | solution.py:28
  188.6 6.4 %collective-permute-start.20 = (bf16[64,1536]{1,0:T(8,128)(2,1)}, bf16[64,1536]{1,0:T(8,128)(2,1)}, u32[]{:S(2)}, u32[]{:S(2)}) collective-permute-start(bf16[64,1536]{1,0:T(8,128)(2,1)} %get-tuple-element.32), channel_id=1, source_target_pairs={{0,3},{1,0},{2,1},{3,2},{4,7},{5,4},{6,5},{7,6},{8,11},{9,8},{10,9... | collective-permute-start | bytes 589832 | tf_op jit(solution)/shard_map/ppermute | solution.py:28
  196.2 4.0 collective-permute-done.20
  200.2 7.6 %collective-permute-done.19 = bf16[64,1536]{1,0:T(8,128)(2,1)} collective-permute-done((bf16[64,1536]{1,0:T(8,128)(2,1)}, bf16[64,1536]{1,0:T(8,128)(2,1)}, u32[]{:S(2)}, u32[]{:S(2)}) %collective-permute-start.19) | collective-permute-done | bytes 196640 | tf_op jit(solution)/shard_map/ppermute | solution.py:28
  221.3 6.7 %collective-permute-done.24 = bf16[128,1536]{1,0:T(8,128)(2,1)S(1)} collective-permute-done((bf16[128,1536]{1,0:T(8,128)(2,1)S(1)}, bf16[128,1536]{1,0:T(8,128)(2,1)S(1)}, u32[]{:S(2)}, u32[]{:S(2)}) %collective-permute-start.24) | collective-permute-done | bytes 393248 | tf_op jit(solution)/shard_map/ppermute | solution.py:28
  230.7 18.1 %project_two.1 = (bf16[4,528,384]{2,1,0:T(8,128)(2,1)S(1)}, bf16[512,512]{1,0:T(8,128)(2,1)S(1)}) custom-call(s32[9]{0:T(128)S(1)} %concatenate.111.info, bf16[512,1536]{1,0:T(8,128)(2,1)S(1)} %copy-done.14, bf16[8,8,192,512]{3,2,1,0:T(8,128)(2,1)} %bitcast.93, bf16[3,4096,512]{2,1,0:T(8,128)(2,1)} %bitcast.92, bf16[16,128]{1,0:T(8,128)(2,1)S(1)} %pad.4.valid), custom_call_target="tpu_custom_call" | custom-call | flops 12884901888 | bytes 29360128 | tf_op jit(solution)/shard_map/project_two/pallas_call | solution.py:285
  252.3 9.6 %collective-permute-start.33 = (bf16[528,384]{1,0:T(8,128)(2,1)}, bf16[528,384]{1,0:T(8,128)(2,1)}, u32[]{:S(2)}, u32[]{:S(2)}) collective-permute-start(bf16[528,384]{1,0:T(8,128)(2,1)} %get-tuple-element.36), channel_id=1, source_target_pairs={{0,32},{8,40},{16,48},{24,56},{32,0},{40,8},{48,16},{56,24},{64,96... | collective-permute-start | bytes 1216520 | tf_op jit(solution)/shard_map/ppermute | solution.py:430
  266.6 5.8 %collective-permute-done.33 = bf16[528,384]{1,0:T(8,128)(2,1)} collective-permute-done((bf16[528,384]{1,0:T(8,128)(2,1)}, bf16[528,384]{1,0:T(8,128)(2,1)}, u32[]{:S(2)}, u32[]{:S(2)}) %collective-permute-start.33) | collective-permute-done | bytes 405536 | tf_op jit(solution)/shard_map/ppermute | solution.py:430
  273.9 5.9 %collective-permute-start.41 = (bf16[4,528,256]{2,1,0:T(8,128)(2,1)S(1)}, bf16[4,528,256]{2,1,0:T(8,128)(2,1)S(1)}, u32[]{:S(2)}, u32[]{:S(2)}) collective-permute-start(bf16[4,528,256]{2,1,0:T(8,128)(2,1)S(1)} %pad_maximum_fusion.4.kv), channel_id=1, source_target_pairs={{0,64},{8,72},{16,80},{24,88},{32,96},{40,104},{48,112},{56,120},{... | collective-permute-start | bytes 3244040 | tf_op jit(solution)/shard_map/ppermute | solution.py:532
  281.5 11.1 %causal_own.1 = (f32[4,128,512]{2,1,0:T(8,128)S(1)}, f32[4,8,512]{2,1,0:T(8,128)S(1)}) custom-call(s32[3]{0:T(128)S(1)} %pad_add_fusion.info, bf16[4,512,128]{2,1,0:T(8,128)(2,1)S(1)} %pad_maximum_fusion.13.queries, bf16[4,528,256]{2,1,0:T(8,128)(2,1)S(1)} %pad_maximum_fusion.4.kv, bf16[4,528,256]{2,1,0:T(8,128)(2,1)S(1)} %collective-permute-done.35.other), custom_call_target="tpu_custom_call" | custom-call | flops 2415919104 | bytes 4194304 | tf_op jit(solution)/shard_map/causal_own/pallas_call | solution.py:406
  294.3 9.7 %collective-permute-done.41 = bf16[4,528,256]{2,1,0:T(8,128)(2,1)S(1)} collective-permute-done((bf16[4,528,256]{2,1,0:T(8,128)(2,1)S(1)}, bf16[4,528,256]{2,1,0:T(8,128)(2,1)S(1)}, u32[]{:S(2)}, u32[]{:S(2)}) %collective-permute-start.41) | collective-permute-done | bytes 1081376 | tf_op jit(solution)/shard_map/ppermute | solution.py:532
  304.8 16.4 %collective-permute-done.38 = bf16[256,1536]{1,0:T(8,128)(2,1)S(1)} collective-permute-done((bf16[256,1536]{1,0:T(8,128)(2,1)S(1)}, bf16[256,1536]{1,0:T(8,128)(2,1)S(1)}, u32[]{:S(2)}, u32[]{:S(2)}) %collective-permute-start.38) | collective-permute-done | bytes 786464 | tf_op jit(solution)/shard_map/ppermute | solution.py:24
  325.3 3.4 causal_first_half.1
  366.2 9.2 %collective-permute-done.48 = bf16[1024,512]{1,0:T(8,128)(2,1)} collective-permute-done((bf16[1024,512]{1,0:T(8,128)(2,1)}, bf16[1024,512]{1,0:T(8,128)(2,1)}, u32[]{:S(2)}, u32[]{:S(2)}) %collective-permute-start.48) | collective-permute-done | bytes 1048608 | tf_op jit(solution)/shard_map/ppermute | solution.py:24
  375.4 6.6 %collective-permute-done.46 = bf16[1024,512]{1,0:T(8,128)(2,1)S(1)} collective-permute-done((bf16[1024,512]{1,0:T(8,128)(2,1)}, bf16[1024,512]{1,0:T(8,128)(2,1)S(1)}, u32[]{:S(2)}, u32[]{:S(2)}) %collective-permute-start.46) | collective-permute-done | bytes 1048608 | tf_op jit(solution)/shard_map/ppermute | solution.py:28
  386.3 8.2 %collective-permute-done.50 = bf16[512,512]{1,0:T(8,128)(2,1)S(1)} collective-permute-done((bf16[512,512]{1,0:T(8,128)(2,1)S(1)}, bf16[512,512]{1,0:T(8,128)(2,1)S(1)}, u32[]{:S(2)}, u32[]{:S(2)}) %collective-permute-start.50) | collective-permute-done | bytes 524320 | tf_op jit(solution)/shard_map/ppermute | solution.py:28
  (255 shorter events, 138.1 us)
Async XLA Ops:
  7.2 222.1 %all-gather.2.cloned.1.call-start = ((), (), s32[]{:S(2)}) async-start(), calls=%async_computation | async-start | bytes 14155776 | tf_op jit(solution)/shard_map/all_gather | solution.py:477
  9.3 11.9 %collective-permute-start.1 = (bf16[144,1536]{1,0:T(8,128)(2,1)}, bf16[144,1536]{1,0:T(8,128)(2,1)S(1)}, u32[]{:S(2)}, u32[]{:S(2)}) collective-permute-start(bf16[144,1536]{1,0:T(8,128)(2,1)} %prepare.1), channel_id=1, source_target_pairs={{0,4},{1,5},{2,6},{3,7},{4,0},{5,1},{6,2},{7,3},{8,12},{9,13},{10,... | collective-permute-start | bytes 1327112 | tf_op jit(solution)/shard_map/ppermute | solution.py:24
  10.8 15.8 %collective-permute-start = (bf16[144,1536]{1,0:T(8,128)(2,1)}, bf16[144,1536]{1,0:T(8,128)(2,1)S(1)}, u32[]{:S(2)}, u32[]{:S(2)}) collective-permute-start(bf16[144,1536]{1,0:T(8,128)(2,1)} %prepare.1), channel_id=1, source_target_pairs={{0,3},{1,0},{2,1},{3,2},{4,7},{5,4},{6,5},{7,6},{8,11},{9,8},{10,9... | collective-permute-start | bytes 1327112 | tf_op jit(solution)/shard_map/ppermute | solution.py:28
  14.9 31.7 %collective-permute-start.2 = (bf16[144,1536]{1,0:T(8,128)(2,1)}, bf16[144,1536]{1,0:T(8,128)(2,1)S(1)}, u32[]{:S(2)}, u32[]{:S(2)}) collective-permute-start(bf16[144,1536]{1,0:T(8,128)(2,1)} %prepare.1), channel_id=1, source_target_pairs={{0,1},{1,2},{2,3},{3,0},{4,5},{5,6},{6,7},{7,4},{8,9},{9,10},{10,1... | collective-permute-start | bytes 1327112 | tf_op jit(solution)/shard_map/ppermute | solution.py:28
  22.4 33.6 %collective-permute-start.3 = (bf16[288,1536]{1,0:T(8,128)(2,1)S(1)}, bf16[288,1536]{1,0:T(8,128)(2,1)S(1)}, u32[]{:S(2)}, u32[]{:S(2)}) collective-permute-start(bf16[288,1536]{1,0:T(8,128)(2,1)S(1)} %pad_maximum_fusion.9), channel_id=1, source_target_pairs={{0,2},{1,3},{2,0},{3,1},{4,6},{5,7},{6,4},{7,5},{8,10},{9,11},{10,... | collective-permute-start | bytes 2654216 | tf_op jit(solution)/shard_map/ppermute | solution.py:28
  46.7 13.1 %collective-permute-start.4 = (bf16[288,1536]{1,0:T(8,128)(2,1)S(1)}, bf16[288,1536]{1,0:T(8,128)(2,1)S(1)}, u32[]{:S(2)}, u32[]{:S(2)}) collective-permute-start(bf16[288,1536]{1,0:T(8,128)(2,1)S(1)} %pad_maximum_fusion.10), channel_id=1, source_target_pairs={{0,4},{1,5},{2,6},{3,7},{4,0},{5,1},{6,2},{7,3},{8,12},{9,13},{10,... | collective-permute-start | bytes 2654216 | tf_op jit(solution)/shard_map/ppermute | solution.py:24
  63.7 18.5 %collective-permute-start.5 = (bf16[512,384]{1,0:T(8,128)(2,1)}, bf16[512,384]{1,0:T(8,128)(2,1)}, u32[]{:S(2)}, u32[]{:S(2)}) collective-permute-start(bf16[512,384]{1,0:T(8,128)(2,1)} %get-tuple-element.12), channel_id=1, source_target_pairs={{0,8},{8,16},{16,24},{24,32},{32,40},{40,48},{48,56},{56,64},{64,7... | collective-permute-start | bytes 1179656 | tf_op jit(solution)/shard_map/ppermute | solution.py:468
  72.5 19.8 %collective-permute-start.29 = (bf16[192,512]{1,0:T(8,128)(2,1)S(1)}, bf16[192,512]{1,0:T(8,128)(2,1)S(1)}, u32[]{:S(2)}, u32[]{:S(2)}) collective-permute-start(bf16[192,512]{1,0:T(8,128)(2,1)S(1)} %maximum_add_fusion.3), channel_id=1, source_target_pairs={{0,1},{1,2},{2,3},{3,0},{4,5},{5,6},{6,7},{7,4},{8,9},{9,10},{10,1... | collective-permute-start | bytes 589832 | tf_op jit(solution)/shard_map/ppermute | solution.py:28
  72.6 19.7 %collective-permute-start.28 = (bf16[192,512]{1,0:T(8,128)(2,1)S(1)}, bf16[192,512]{1,0:T(8,128)(2,1)S(1)}, u32[]{:S(2)}, u32[]{:S(2)}) collective-permute-start(bf16[192,512]{1,0:T(8,128)(2,1)S(1)} %maximum_add_fusion.3), channel_id=1, source_target_pairs={{0,3},{1,0},{2,1},{3,2},{4,7},{5,4},{6,5},{7,6},{8,11},{9,8},{10,9... | collective-permute-start | bytes 589832 | tf_op jit(solution)/shard_map/ppermute | solution.py:28
  88.4 24.8 %collective-permute-start.8 = (bf16[256,1536]{1,0:T(8,128)(2,1)S(1)}, bf16[256,1536]{1,0:T(8,128)(2,1)S(1)}, u32[]{:S(2)}, u32[]{:S(2)}) collective-permute-start(bf16[256,1536]{1,0:T(8,128)(2,1)S(1)} %get-tuple-element.46), channel_id=1, source_target_pairs={{0,4},{1,5},{2,6},{3,7},{4,0},{5,1},{6,2},{7,3},{8,12},{9,13},{10,... | collective-permute-start | bytes 2359304 | tf_op jit(solution)/shard_map/ppermute | solution.py:24
  88.9 25.5 %collective-permute-start.6 = (bf16[256,1536]{1,0:T(8,128)(2,1)S(1)}, bf16[256,1536]{1,0:T(8,128)(2,1)S(1)}, u32[]{:S(2)}, u32[]{:S(2)}) collective-permute-start(bf16[256,1536]{1,0:T(8,128)(2,1)S(1)} %get-tuple-element.45), channel_id=1, source_target_pairs={{0,2},{1,3},{2,0},{3,1},{4,6},{5,7},{6,4},{7,5},{8,10},{9,11},{10,... | collective-permute-start | bytes 2359304 | tf_op jit(solution)/shard_map/ppermute | solution.py:28
  88.9 24.1 %collective-permute-start.27 = (bf16[192,512]{1,0:T(8,128)(2,1)S(1)}, bf16[192,512]{1,0:T(8,128)(2,1)S(1)}, u32[]{:S(2)}, u32[]{:S(2)}) collective-permute-start(bf16[192,512]{1,0:T(8,128)(2,1)S(1)} %maximum_add_fusion.3), channel_id=1, source_target_pairs={{0,4},{1,5},{2,6},{3,7},{4,0},{5,1},{6,2},{7,3},{8,12},{9,13},{10,... | collective-permute-start | bytes 589832 | tf_op jit(solution)/shard_map/ppermute | solution.py:24
  92.4 27.9 %collective-permute-start.31 = (bf16[384,512]{1,0:T(8,128)(2,1)S(1)}, bf16[384,512]{1,0:T(8,128)(2,1)S(1)}, u32[]{:S(2)}, u32[]{:S(2)}) collective-permute-start(bf16[384,512]{1,0:T(8,128)(2,1)S(1)} %maximum_add_fusion.2), channel_id=1, source_target_pairs={{0,4},{1,5},{2,6},{3,7},{4,0},{5,1},{6,2},{7,3},{8,12},{9,13},{10,... | collective-permute-start | bytes 1179656 | tf_op jit(solution)/shard_map/ppermute | solution.py:24
  144.3 12.0 %collective-permute-start.11 = (bf16[128,1536]{1,0:T(8,128)(2,1)S(1)}, bf16[128,1536]{1,0:T(8,128)(2,1)S(1)}, u32[]{:S(2)}, u32[]{:S(2)}) collective-permute-start(bf16[128,1536]{1,0:T(8,128)(2,1)S(1)} %fusion.11), channel_id=1, source_target_pairs={{0,4},{1,5},{2,6},{3,7},{4,0},{5,1},{6,2},{7,3},{8,12},{9,13},{10,... | collective-permute-start | bytes 1179656 | tf_op jit(solution)/shard_map/ppermute | solution.py:24
  149.5 19.2 %collective-permute-start.15 = (bf16[256,1536]{1,0:T(8,128)(2,1)S(1)}, bf16[256,1536]{1,0:T(8,128)(2,1)S(1)}, u32[]{:S(2)}, u32[]{:S(2)}) collective-permute-start(bf16[256,1536]{1,0:T(8,128)(2,1)S(1)} %pad_maximum_fusion.12), channel_id=1, source_target_pairs={{0,4},{1,5},{2,6},{3,7},{4,0},{5,1},{6,2},{7,3},{8,12},{9,13},{10,... | collective-permute-start | bytes 2359304 | tf_op jit(solution)/shard_map/ppermute | solution.py:24
  156.4 13.6 %collective-permute-start.14 = (bf16[256,1536]{1,0:T(8,128)(2,1)S(1)}, bf16[256,1536]{1,0:T(8,128)(2,1)S(1)}, u32[]{:S(2)}, u32[]{:S(2)}) collective-permute-start(bf16[256,1536]{1,0:T(8,128)(2,1)S(1)} %pad_maximum_fusion.11), channel_id=1, source_target_pairs={{0,2},{1,3},{2,0},{3,1},{4,6},{5,7},{6,4},{7,5},{8,10},{9,11},{10,... | collective-permute-start | bytes 2359304 | tf_op jit(solution)/shard_map/ppermute | solution.py:28
  176.1 11.5 %collective-permute-start.16 = (bf16[128,1536]{1,0:T(8,128)(2,1)S(1)}, bf16[128,1536]{1,0:T(8,128)(2,1)S(1)}, u32[]{:S(2)}, u32[]{:S(2)}) collective-permute-start(bf16[128,1536]{1,0:T(8,128)(2,1)S(1)} %get-tuple-element.42), channel_id=1, source_target_pairs={{0,2},{1,3},{2,0},{3,1},{4,6},{5,7},{6,4},{7,5},{8,10},{9,11},{10,... | collective-permute-start | bytes 1179656 | tf_op jit(solution)/shard_map/ppermute | solution.py:28
  188.6 11.6 %collective-permute-start.20 = (bf16[64,1536]{1,0:T(8,128)(2,1)}, bf16[64,1536]{1,0:T(8,128)(2,1)}, u32[]{:S(2)}, u32[]{:S(2)}) collective-permute-start(bf16[64,1536]{1,0:T(8,128)(2,1)} %get-tuple-element.32), channel_id=1, source_target_pairs={{0,3},{1,0},{2,1},{3,2},{4,7},{5,4},{6,5},{7,6},{8,11},{9,8},{10,9... | collective-permute-start | bytes 589832 | tf_op jit(solution)/shard_map/ppermute | solution.py:28
  195.0 12.8 %collective-permute-start.19 = (bf16[64,1536]{1,0:T(8,128)(2,1)}, bf16[64,1536]{1,0:T(8,128)(2,1)}, u32[]{:S(2)}, u32[]{:S(2)}) collective-permute-start(bf16[64,1536]{1,0:T(8,128)(2,1)} %get-tuple-element.31), channel_id=1, source_target_pairs={{0,1},{1,2},{2,3},{3,0},{4,5},{5,6},{6,7},{7,4},{8,9},{9,10},{10,1... | collective-permute-start | bytes 589832 | tf_op jit(solution)/shard_map/ppermute | solution.py:28
  195.0 12.8 %collective-permute-start.17 = (bf16[64,1536]{1,0:T(8,128)(2,1)}, bf16[64,1536]{1,0:T(8,128)(2,1)}, u32[]{:S(2)}, u32[]{:S(2)}) collective-permute-start(bf16[64,1536]{1,0:T(8,128)(2,1)} %get-tuple-element.41), channel_id=1, source_target_pairs={{0,4},{1,5},{2,6},{3,7},{4,0},{5,1},{6,2},{7,3},{8,12},{9,13},{10,... | collective-permute-start | bytes 589832 | tf_op jit(solution)/shard_map/ppermute | solution.py:24
  250.3 16.3 %collective-permute-start.34 = (bf16[528,384]{1,0:T(8,128)(2,1)}, bf16[528,384]{1,0:T(8,128)(2,1)}, u32[]{:S(2)}, u32[]{:S(2)}) collective-permute-start(bf16[528,384]{1,0:T(8,128)(2,1)} %get-tuple-element.35), channel_id=1, source_target_pairs={{0,16},{8,24},{16,32},{24,40},{32,48},{40,56},{48,0},{56,8},{64,80... | collective-permute-start | bytes 1216520 | tf_op jit(solution)/shard_map/ppermute | solution.py:430
  252.3 20.1 %collective-permute-start.33 = (bf16[528,384]{1,0:T(8,128)(2,1)}, bf16[528,384]{1,0:T(8,128)(2,1)}, u32[]{:S(2)}, u32[]{:S(2)}) collective-permute-start(bf16[528,384]{1,0:T(8,128)(2,1)} %get-tuple-element.36), channel_id=1, source_target_pairs={{0,32},{8,40},{16,48},{24,56},{32,0},{40,8},{48,16},{56,24},{64,96... | collective-permute-start | bytes 1216520 | tf_op jit(solution)/shard_map/ppermute | solution.py:430
  273.9 30.0 %collective-permute-start.41 = (bf16[4,528,256]{2,1,0:T(8,128)(2,1)S(1)}, bf16[4,528,256]{2,1,0:T(8,128)(2,1)S(1)}, u32[]{:S(2)}, u32[]{:S(2)}) collective-permute-start(bf16[4,528,256]{2,1,0:T(8,128)(2,1)S(1)} %pad_maximum_fusion.4.kv), channel_id=1, source_target_pairs={{0,64},{8,72},{16,80},{24,88},{32,96},{40,104},{48,112},{56,120},{... | collective-permute-start | bytes 3244040 | tf_op jit(solution)/shard_map/ppermute | solution.py:532
  280.0 41.2 %collective-permute-start.38 = (bf16[256,1536]{1,0:T(8,128)(2,1)S(1)}, bf16[256,1536]{1,0:T(8,128)(2,1)S(1)}, u32[]{:S(2)}, u32[]{:S(2)}) collective-permute-start(bf16[256,1536]{1,0:T(8,128)(2,1)S(1)} %get-tuple-element.40), channel_id=1, source_target_pairs={{0,4},{1,5},{2,6},{3,7},{4,0},{5,1},{6,2},{7,3},{8,12},{9,13},{10,... | collective-permute-start | bytes 2359304 | tf_op jit(solution)/shard_map/ppermute | solution.py:24
  280.4 40.8 %collective-permute-start.36 = (bf16[256,1536]{1,0:T(8,128)(2,1)S(1)}, bf16[256,1536]{1,0:T(8,128)(2,1)S(1)}, u32[]{:S(2)}, u32[]{:S(2)}) collective-permute-start(bf16[256,1536]{1,0:T(8,128)(2,1)S(1)} %get-tuple-element.39), channel_id=1, source_target_pairs={{0,2},{1,3},{2,0},{3,1},{4,6},{5,7},{6,4},{7,5},{8,10},{9,11},{10,... | collective-permute-start | bytes 2359304 | tf_op jit(solution)/shard_map/ppermute | solution.py:28
  304.6 20.7 %collective-permute-start.42 = (bf16[4,528,256]{2,1,0:T(8,128)(2,1)S(1)}, bf16[4,528,256]{2,1,0:T(8,128)(2,1)S(1)}, u32[]{:S(2)}, u32[]{:S(2)}) collective-permute-start(bf16[4,528,256]{2,1,0:T(8,128)(2,1)S(1)} %broadcast_add_fusion.2.kv), channel_id=1, source_target_pairs={{0,8},{8,0},{16,24},{24,16},{32,40},{40,32},{48,56},{56,48},{64,72... | collective-permute-start | bytes 3244040 | tf_op jit(solution)/shard_map/ppermute | solution.py:436
  322.7 11.7 %collective-permute-start.39 = (bf16[128,1536]{1,0:T(8,128)(2,1)S(1)}, bf16[128,1536]{1,0:T(8,128)(2,1)S(1)}, u32[]{:S(2)}, u32[]{:S(2)}) collective-permute-start(bf16[128,1536]{1,0:T(8,128)(2,1)S(1)} %get-tuple-element.26), channel_id=1, source_target_pairs={{0,1},{1,2},{2,3},{3,0},{4,5},{5,6},{6,7},{7,4},{8,9},{9,10},{10,1... | collective-permute-start | bytes 1179656 | tf_op jit(solution)/shard_map/ppermute | solution.py:28
  351.8 23.6 %collective-permute-start.48 = (bf16[1024,512]{1,0:T(8,128)(2,1)}, bf16[1024,512]{1,0:T(8,128)(2,1)}, u32[]{:S(2)}, u32[]{:S(2)}) collective-permute-start(bf16[1024,512]{1,0:T(8,128)(2,1)} %pad_maximum_fusion.8), channel_id=1, source_target_pairs={{0,4},{1,5},{2,6},{3,7},{4,0},{5,1},{6,2},{7,3},{8,12},{9,13},{10,... | collective-permute-start | bytes 3145736 | tf_op jit(solution)/shard_map/ppermute | solution.py:24
  357.3 24.7 %collective-permute-start.46 = (bf16[1024,512]{1,0:T(8,128)(2,1)}, bf16[1024,512]{1,0:T(8,128)(2,1)S(1)}, u32[]{:S(2)}, u32[]{:S(2)}) collective-permute-start(bf16[1024,512]{1,0:T(8,128)(2,1)} %pad_maximum_fusion.7), channel_id=1, source_target_pairs={{0,2},{1,3},{2,0},{3,1},{4,6},{5,7},{6,4},{7,5},{8,10},{9,11},{10,... | collective-permute-start | bytes 3145736 | tf_op jit(solution)/shard_map/ppermute | solution.py:28
  383.6 10.9 %collective-permute-start.50 = (bf16[512,512]{1,0:T(8,128)(2,1)S(1)}, bf16[512,512]{1,0:T(8,128)(2,1)S(1)}, u32[]{:S(2)}, u32[]{:S(2)}) collective-permute-start(bf16[512,512]{1,0:T(8,128)(2,1)S(1)} %get-tuple-element.23), channel_id=1, source_target_pairs={{0,3},{1,0},{2,1},{3,2},{4,7},{5,4},{6,5},{7,6},{8,11},{9,8},{10,9... | collective-permute-start | bytes 1572872 | tf_op jit(solution)/shard_map/ppermute | solution.py:28
  385.5 11.7 %collective-permute-start.49 = (bf16[512,512]{1,0:T(8,128)(2,1)S(1)}, bf16[512,512]{1,0:T(8,128)(2,1)S(1)}, u32[]{:S(2)}, u32[]{:S(2)}) collective-permute-start(bf16[512,512]{1,0:T(8,128)(2,1)S(1)} %get-tuple-element.22), channel_id=1, source_target_pairs={{0,1},{1,2},{2,3},{3,0},{4,5},{5,6},{6,7},{7,4},{8,9},{9,10},{10,1... | collective-permute-start | bytes 1572872 | tf_op jit(solution)/shard_map/ppermute | solution.py:28
  385.7 11.5 %collective-permute-start.47 = (bf16[512,512]{1,0:T(8,128)(2,1)S(1)}, bf16[512,512]{1,0:T(8,128)(2,1)S(1)}, u32[]{:S(2)}, u32[]{:S(2)}) collective-permute-start(bf16[512,512]{1,0:T(8,128)(2,1)S(1)} %get-tuple-element.30), channel_id=1, source_target_pairs={{0,4},{1,5},{2,6},{3,7},{4,0},{5,1},{6,2},{7,3},{8,12},{9,13},{10,... | collective-permute-start | bytes 1572872 | tf_op jit(solution)/shard_map/ppermute | solution.py:24
  (55 other events, 458.1 us)
Sparse Core Ops, SparseCore 0:
  125.2 67.1 all-gather.1

commit v4 on v3

--- a/solution.py
+++ b/solution.py
@@ -452,11 +452,10 @@
 
     heads_in_flat = heads_in.transpose(1, 2, 0).reshape(3 * width, D1)
     core, y, half = seq_position & 1, (seq_position >> 1) & 3, seq_position >> 3
-    piece = lax.dynamic_slice(widen, (seq_position * 96, 0), (96, 512))
+    piece = lax.dynamic_slice(widen, ((seq_position & 7) * 192, 0), (192, 512))
 
     near, far = gather_blk(prepare(tokens, boundary[None, :]))
     arrived = near[2 * SENT :]
-    piece_across = flip_seq(piece, 8)
     gates = later(gate_up, arrived)
     gate_flat, up_flat = lax.optimization_barrier((gates[:, 0, :], gates[:, 1, :]))
     marks = jnp.concatenate(
@@ -471,9 +470,8 @@
     attn_far = dot(attended[4 * rows :], heads_out).astype(BF16)
     opposite, diagonal = reduce_first(attn_far)
 
-    piece = later(jnp.concatenate([piece, piece_across], axis=0), qkv)
-    pieces = jnp.concatenate(gather_blk(piece, halo), axis=0)
-    pieces = later(later(pieces, opposite), diagonal)
+    pieces = jnp.concatenate(gather_blk(piece, qkv), axis=0)
+    pieces = later(pieces, attended)
     pieces = lax.all_gather(
         pieces, "seq", axis=0, axis_index_groups=[[h * 8 + k for k in range(8)] for h in range(2)]
     ).reshape(8, 8, 192, 512)
@@ -503,16 +501,6 @@
         + dot(selector[:, :rows], mid_stream)
     ).astype(BF16)
     pooled_own = reduce_blk(placed[:256], placed[256:]).astype(BF16)
-    pooled_own = jnp.concatenate(
-        [
-            lax.dynamic_slice(
-                pooled_own, (0, 96 * ((half ^ h) * 8 + k)), (64, 96)
-            )
-            for k in range(8)
-            for h in range(2)
-        ],
-        axis=1,
-    )
     pooled = jnp.concatenate(gather_blk(pooled_own), axis=0)
 
     validity = (jnp.arange(capacity, dtype=jnp.int32) < span_count).astype(F32)
@@ -533,16 +521,16 @@
     info_two = jnp.stack([half, core, y]).astype(jnp.int32)
     running = causal_attend(True, info_two, queries, (own_kv, flip_seq(own_kv, 1)))
     first_kv = first_kv + running[1][0, 2, 0].astype(BF16)
-    level_one = mid_stream.astype(F32) + reduce_second(
-        later(mlp_near, running[1][0, 2:3]), opposite, diagonal
-    )
     mixed = causal_attend(False, info_two, queries, (first_kv, flip_seq(first_kv, 1)), running)
     back = [mixed[0], turn_y(mixed[3], 3), turn_y(mixed[2], 2), turn_y(mixed[1], 1)]
     heads = jnp.concatenate([back[0], back[1], back[2], back[3]] * 2, axis=1)
     attended_two = lax.dynamic_slice(heads, (0, ((4 - y) & 3) * 128), (capacity, 512))
 
 
-    level_one = later(level_one, mixed[0]).astype(BF16)
+    level_one = (
+        mid_stream.astype(F32)
+        + reduce_second(later(mlp_near, mixed[0]), opposite, diagonal)
+    ).astype(BF16)
     column_of = later(block_of, level_one)
 
     def columns(place):

time: 412 us -> 369 us (0.90)
  the two profiles are of different devices: /device:TPU:0 before, /device:TPU:6 now
where the time goes in v4:
time: 369 us; the launch traced here: 362 us
  waiting for transfers between devices  132 us (36%)
  starting transfers between devices  73.4 us (20%)
  Pallas kernels  69.3 us (19%)
  between operations  25.3 us (7%)
  other arithmetic  22.9 us (6%)
  local copies, waits for them, and re-layouts  21.1 us (6%)
  matrix products  17.7 us (5%)
    ppermute x24, waiting for transfers between devices, turn_z(): lax.ppermute(value, 'blk', [(i, i & 4 | i + steps & 3) for i in range(8)])  56.9 us
    ppermute x16, waiting for transfers between devices, flip_x(): return lax.ppermute(value, 'blk', [(i, i ^ 4) for i in range(8)])  46.6 us
    ppermute x24, starting transfers between devices, turn_z(): lax.ppermute(value, 'blk', [(i, i & 4 | i + steps & 3) for i in range(8)])  31.6 us
    pallas_call x2, Pallas kernels, causal_attend(): pl.pallas_call(kernel, out_shape=out_shape, grid_spec=pltpu.PrefetchScala...  29.2 us
    ppermute x16, starting transfers between devices, flip_x(): return lax.ppermute(value, 'blk', [(i, i ^ 4) for i in range(8)])  22.8 us
    pallas_call x1, Pallas kernels, project_two(): pl.pallas_call(project_kernel, out_shape=(jax.ShapeDtypeStruct((4, 512 +...  18.1 us
    dot_general x14, matrix products, dot(): return jnp.dot(left, right, preferred_element_type=F32)  17.7 us
    ppermute x6, starting transfers between devices, turn_y(): lax.ppermute(value, 'seq', [(i, i & 9 | i + 2 * steps & 6) for i in range...  15.5 us
  transfers between devices with their start and end apart: 51, of which 34 were waited for; matrix products, arithmetic and copies ran while one was open for 11% of the time, Pallas kernels for 14%

profile of v4, /device:TPU:6, one launch (start us, length us, event | category | flops | bytes accessed | tf_op | source)
XLA Modules:
  0.0 362.2 jit_solution(7607221444276785683)
XLA Ops:
  10.1 4.0 %collective-permute-start = (bf16[144,1536]{1,0:T(8,128)(2,1)}, bf16[144,1536]{1,0:T(8,128)(2,1)S(1)}, u32[]{:S(2)}, u32[]{:S(2)}) collective-permute-start(bf16[144,1536]{1,0:T(8,128)(2,1)} %prepare.1), channel_id=1, source_target_pairs={{0,3},{1,0},{2,1},{3,2},{4,7},{5,4},{6,5},{7,6},{8,11},{9,8},{10,9... | collective-permute-start | bytes 1327112 | tf_op jit(solution)/shard_map/ppermute | solution.py:28
  14.8 3.2 collective-permute-start.27
  18.3 3.1 collective-permute-done.1
  39.2 9.6 %collective-permute-done.3 = bf16[288,1536]{1,0:T(8,128)(2,1)S(1)} collective-permute-done((bf16[288,1536]{1,0:T(8,128)(2,1)S(1)}, bf16[288,1536]{1,0:T(8,128)(2,1)S(1)}, u32[]{:S(2)}, u32[]{:S(2)}) %collective-permute-start.3) | collective-permute-done | bytes 884768 | tf_op jit(solution)/shard_map/ppermute | solution.py:28
  59.7 4.7 %window_late.1.before = bf16[1024,192]{1,0:T(8,128)(2,1)S(1)} custom-call(s32[9]{0:T(128)S(1)} %add_add_fusion.info, bf16[1152,576]{1,0:T(8,128)(2,1)S(1)} %get-tuple-element.11.qkv), custom_call_target="tpu_custom_call" | custom-call | flops 251658240 | bytes 2097152 | tf_op jit(solution)/shard_map/window_late/pallas_call | solution.py:146
  65.6 5.6 %window_early.1 = bf16[1024,192]{1,0:T(8,128)(2,1)} custom-call(s32[9]{0:T(128)S(1)} %add_add_fusion.info, bf16[1152,576]{1,0:T(8,128)(2,1)S(1)} %get-tuple-element.11.qkv, bf16[512,384]{1,0:T(8,128)(2,1)S(1)} %collective-permute-done.5.halo, bf16[1024,192]{1,0:T(8,128)(2,1)S(1)} %window_late.1.before), custom_call_target="tpu_custom_call" | custom-call | flops 251658240 | bytes 2097152 | tf_op jit(solution)/shard_map/window_early/pallas_call | solution.py:146
  76.4 2.6 collective-permute-start.8
  82.4 13.6 %collective-permute-done.8 = bf16[256,1536]{1,0:T(8,128)(2,1)S(1)} collective-permute-done((bf16[256,1536]{1,0:T(8,128)(2,1)S(1)}, bf16[256,1536]{1,0:T(8,128)(2,1)S(1)}, u32[]{:S(2)}, u32[]{:S(2)}) %collective-permute-start.8) | collective-permute-done | bytes 786464 | tf_op jit(solution)/shard_map/ppermute | solution.py:24
  103.4 4.5 %collective-permute-done.10 = bf16[128,1536]{1,0:T(8,128)(2,1)} collective-permute-done((bf16[128,1536]{1,0:T(8,128)(2,1)}, bf16[128,1536]{1,0:T(8,128)(2,1)}, u32[]{:S(2)}, u32[]{:S(2)}) %collective-permute-start.10) | collective-permute-done | bytes 393248 | tf_op jit(solution)/shard_map/ppermute | solution.py:28
  113.1 2.2 collective-permute-start.12
  117.8 3.3 collective-permute-done.13
  123.1 3.3 collective-permute-done.11
  129.6 2.9 mlp.2
  132.6 7.7 %collective-permute-done.15 = bf16[256,1536]{1,0:T(8,128)(2,1)S(1)} collective-permute-done((bf16[256,1536]{1,0:T(8,128)(2,1)S(1)}, bf16[256,1536]{1,0:T(8,128)(2,1)S(1)}, u32[]{:S(2)}, u32[]{:S(2)}) %collective-permute-start.15) | collective-permute-done | bytes 786464 | tf_op jit(solution)/shard_map/ppermute | solution.py:24
  140.8 3.0 mlp.3
  148.5 5.1 %collective-permute-done.18 = bf16[128,1536]{1,0:T(8,128)(2,1)S(1)} collective-permute-done((bf16[128,1536]{1,0:T(8,128)(2,1)S(1)}, bf16[128,1536]{1,0:T(8,128)(2,1)S(1)}, u32[]{:S(2)}, u32[]{:S(2)}) %collective-permute-start.18) | collective-permute-done | bytes 393248 | tf_op jit(solution)/shard_map/ppermute | solution.py:24
  153.6 3.9 %collective-permute-done.16 = bf16[128,1536]{1,0:T(8,128)(2,1)S(1)} collective-permute-done((bf16[128,1536]{1,0:T(8,128)(2,1)S(1)}, bf16[128,1536]{1,0:T(8,128)(2,1)S(1)}, u32[]{:S(2)}, u32[]{:S(2)}) %collective-permute-start.16) | collective-permute-done | bytes 393248 | tf_op jit(solution)/shard_map/ppermute | solution.py:28
  167.6 2.8 collective-permute-start.21
  173.2 3.3 collective-permute-done.21
  182.8 4.0 %collective-permute-done.24 = bf16[128,1536]{1,0:T(8,128)(2,1)S(1)} collective-permute-done((bf16[128,1536]{1,0:T(8,128)(2,1)S(1)}, bf16[128,1536]{1,0:T(8,128)(2,1)S(1)}, u32[]{:S(2)}, u32[]{:S(2)}) %collective-permute-start.24) | collective-permute-done | bytes 393248 | tf_op jit(solution)/shard_map/ppermute | solution.py:28
  189.9 18.1 %project_two.1 = (bf16[4,528,384]{2,1,0:T(8,128)(2,1)S(1)}, bf16[512,512]{1,0:T(8,128)(2,1)S(1)}) custom-call(s32[9]{0:T(128)S(1)} %concatenate.105.info, bf16[512,1536]{1,0:T(8,128)(2,1)S(1)} %copy-done.8, bf16[8,8,192,512]{3,2,1,0:T(8,128)(2,1)} %bitcast.94, bf16[3,4096,512]{2,1,0:T(8,128)(2,1)} %bitcast.93, bf16[16,128]{1,0:T(8,128)(2,1)S(1)} %pad.4.valid), custom_call_target="tpu_custom_call" | custom-call | flops 12884901888 | bytes 29360128 | tf_op jit(solution)/shard_map/project_two/pallas_call | solution.py:285
  209.0 7.6 %collective-permute-start.33 = (bf16[528,384]{1,0:T(8,128)(2,1)S(1)}, bf16[528,384]{1,0:T(8,128)(2,1)S(1)}, u32[]{:S(2)}, u32[]{:S(2)}) collective-permute-start(bf16[528,384]{1,0:T(8,128)(2,1)S(1)} %get-tuple-element.37), channel_id=1, source_target_pairs={{0,16},{8,24},{16,32},{24,40},{32,48},{40,56},{48,0},{56,8},{64,80... | collective-permute-start | bytes 1216520 | tf_op jit(solution)/shard_map/ppermute | solution.py:430
  219.6 3.4 collective-permute-done.33
  223.1 5.8 %collective-permute-done.32 = bf16[528,384]{1,0:T(8,128)(2,1)S(1)} collective-permute-done((bf16[528,384]{1,0:T(8,128)(2,1)S(1)}, bf16[528,384]{1,0:T(8,128)(2,1)S(1)}, u32[]{:S(2)}, u32[]{:S(2)}) %collective-permute-start.32) | collective-permute-done | bytes 405536 | tf_op jit(solution)/shard_map/ppermute | solution.py:430
  234.7 12.6 %causal_own.1 = (f32[4,128,512]{2,1,0:T(8,128)S(1)}, f32[4,8,512]{2,1,0:T(8,128)S(1)}) custom-call(s32[3]{0:T(128)S(1)} %pad_add_fusion.info, bf16[4,512,128]{2,1,0:T(8,128)(2,1)S(1)} %pad_maximum_fusion.13.queries, bf16[4,528,256]{2,1,0:T(8,128)(2,1)} %pad_maximum_fusion.4.kv, bf16[4,528,256]{2,1,0:T(8,128)(2,1)} %collective-permute-done.35.other), custom_call_target="tpu_custom_call" | custom-call | flops 2415919104 | bytes 4194304 | tf_op jit(solution)/shard_map/causal_own/pallas_call | solution.py:406
  247.9 12.4 %collective-permute-done.34 = bf16[4,528,256]{2,1,0:T(8,128)(2,1)} collective-permute-done((bf16[4,528,256]{2,1,0:T(8,128)(2,1)}, bf16[4,528,256]{2,1,0:T(8,128)(2,1)}, u32[]{:S(2)}, u32[]{:S(2)}) %collective-permute-start.34) | collective-permute-done | bytes 1081376 | tf_op jit(solution)/shard_map/ppermute | solution.py:520
  265.1 16.5 %causal_first_half.1 = bf16[4,512,128]{2,1,0:T(8,128)(2,1)S(1)} custom-call(s32[3]{0:T(128)S(1)} %pad_add_fusion.info, bf16[4,512,128]{2,1,0:T(8,128)(2,1)S(1)} %pad_maximum_fusion.13.queries, bf16[4,528,256]{2,1,0:T(8,128)(2,1)S(1)} %broadcast_add_fusion.2.kv, bf16[4,528,256]{2,1,0:T(8,128)(2,1)S(1)} %collective-permute-done.36.other, ...), custom_call_target="tpu_custom_call" | custom-call | flops 4294967296 | bytes 4194304 | tf_op jit(solution)/shard_map/causal_first_half/pallas_call | solution.py:406
  285.0 2.4 collective-permute-start.43
  291.8 5.7 %collective-permute-done.44 = bf16[512,128]{1,0:T(8,128)(2,1)S(1)} collective-permute-done((bf16[512,128]{1,0:T(8,128)(2,1)S(1)}, bf16[512,128]{1,0:T(8,128)(2,1)S(1)}, u32[]{:S(2)}, u32[]{:S(2)}) %collective-permute-start.44) | collective-permute-done | bytes 131104 | tf_op jit(solution)/shard_map/ppermute | solution.py:430
  324.0 8.4 %collective-permute-done.47 = bf16[1024,512]{1,0:T(8,128)(2,1)} collective-permute-done((bf16[1024,512]{1,0:T(8,128)(2,1)}, bf16[1024,512]{1,0:T(8,128)(2,1)}, u32[]{:S(2)}, u32[]{:S(2)}) %collective-permute-start.47) | collective-permute-done | bytes 1048608 | tf_op jit(solution)/shard_map/ppermute | solution.py:24
  332.4 6.5 %collective-permute-done.45 = bf16[1024,512]{1,0:T(8,128)(2,1)S(1)} collective-permute-done((bf16[1024,512]{1,0:T(8,128)(2,1)}, bf16[1024,512]{1,0:T(8,128)(2,1)S(1)}, u32[]{:S(2)}, u32[]{:S(2)}) %collective-permute-start.45) | collective-permute-done | bytes 1048608 | tf_op jit(solution)/shard_map/ppermute | solution.py:28
  343.3 8.2 %collective-permute-done.49 = bf16[512,512]{1,0:T(8,128)(2,1)S(1)} collective-permute-done((bf16[512,512]{1,0:T(8,128)(2,1)S(1)}, bf16[512,512]{1,0:T(8,128)(2,1)S(1)}, u32[]{:S(2)}, u32[]{:S(2)}) %collective-permute-start.49) | collective-permute-done | bytes 524320 | tf_op jit(solution)/shard_map/ppermute | solution.py:28
  (215 shorter events, 136.6 us)
Async XLA Ops:
  7.2 181.3 %all-gather.2.cloned.1.call-start = ((), (), s32[]{:S(2)}) async-start(), calls=%async_computation | async-start | bytes 14155776 | tf_op jit(solution)/shard_map/all_gather | solution.py:475
  9.3 12.1 %collective-permute-start.1 = (bf16[144,1536]{1,0:T(8,128)(2,1)}, bf16[144,1536]{1,0:T(8,128)(2,1)S(1)}, u32[]{:S(2)}, u32[]{:S(2)}) collective-permute-start(bf16[144,1536]{1,0:T(8,128)(2,1)} %prepare.1), channel_id=1, source_target_pairs={{0,4},{1,5},{2,6},{3,7},{4,0},{5,1},{6,2},{7,3},{8,12},{9,13},{10,... | collective-permute-start | bytes 1327112 | tf_op jit(solution)/shard_map/ppermute | solution.py:24
  10.1 15.0 %collective-permute-start = (bf16[144,1536]{1,0:T(8,128)(2,1)}, bf16[144,1536]{1,0:T(8,128)(2,1)S(1)}, u32[]{:S(2)}, u32[]{:S(2)}) collective-permute-start(bf16[144,1536]{1,0:T(8,128)(2,1)} %prepare.1), channel_id=1, source_target_pairs={{0,3},{1,0},{2,1},{3,2},{4,7},{5,4},{6,5},{7,6},{8,11},{9,8},{10,9... | collective-permute-start | bytes 1327112 | tf_op jit(solution)/shard_map/ppermute | solution.py:28
  14.1 15.2 %collective-permute-start.2 = (bf16[144,1536]{1,0:T(8,128)(2,1)}, bf16[144,1536]{1,0:T(8,128)(2,1)S(1)}, u32[]{:S(2)}, u32[]{:S(2)}) collective-permute-start(bf16[144,1536]{1,0:T(8,128)(2,1)} %prepare.1), channel_id=1, source_target_pairs={{0,1},{1,2},{2,3},{3,0},{4,5},{5,6},{6,7},{7,4},{8,9},{9,10},{10,1... | collective-permute-start | bytes 1327112 | tf_op jit(solution)/shard_map/ppermute | solution.py:28
  14.8 39.4 %collective-permute-start.28 = (bf16[192,512]{1,0:T(8,128)(2,1)}, bf16[192,512]{1,0:T(8,128)(2,1)}, u32[]{:S(2)}, u32[]{:S(2)}) collective-permute-start(bf16[192,512]{1,0:T(8,128)(2,1)} %constant_dynamic-slice_fusion), channel_id=1, source_target_pairs={{0,1},{1,2},{2,3},{3,0},{4,5},{5,6},{6,7},{7,4},{8,9},{9,10},{10,1... | collective-permute-start | bytes 589832 | tf_op jit(solution)/shard_map/ppermute | solution.py:28
  14.8 39.4 %collective-permute-start.27 = (bf16[192,512]{1,0:T(8,128)(2,1)}, bf16[192,512]{1,0:T(8,128)(2,1)}, u32[]{:S(2)}, u32[]{:S(2)}) collective-permute-start(bf16[192,512]{1,0:T(8,128)(2,1)} %constant_dynamic-slice_fusion), channel_id=1, source_target_pairs={{0,3},{1,0},{2,1},{3,2},{4,7},{5,4},{6,5},{7,6},{8,11},{9,8},{10,9... | collective-permute-start | bytes 589832 | tf_op jit(solution)/shard_map/ppermute | solution.py:28
  21.4 35.2 %collective-permute-start.26 = (bf16[192,512]{1,0:T(8,128)(2,1)}, bf16[192,512]{1,0:T(8,128)(2,1)S(1)}, u32[]{:S(2)}, u32[]{:S(2)}) collective-permute-start(bf16[192,512]{1,0:T(8,128)(2,1)} %constant_dynamic-slice_fusion), channel_id=1, source_target_pairs={{0,4},{1,5},{2,6},{3,7},{4,0},{5,1},{6,2},{7,3},{8,12},{9,13},{10,... | collective-permute-start | bytes 589832 | tf_op jit(solution)/shard_map/ppermute | solution.py:24
  25.1 23.7 %collective-permute-start.3 = (bf16[288,1536]{1,0:T(8,128)(2,1)S(1)}, bf16[288,1536]{1,0:T(8,128)(2,1)S(1)}, u32[]{:S(2)}, u32[]{:S(2)}) collective-permute-start(bf16[288,1536]{1,0:T(8,128)(2,1)S(1)} %pad_maximum_fusion.9), channel_id=1, source_target_pairs={{0,2},{1,3},{2,0},{3,1},{4,6},{5,7},{6,4},{7,5},{8,10},{9,11},{10,... | collective-permute-start | bytes 2654216 | tf_op jit(solution)/shard_map/ppermute | solution.py:28
  29.4 19.5 %collective-permute-start.4 = (bf16[288,1536]{1,0:T(8,128)(2,1)S(1)}, bf16[288,1536]{1,0:T(8,128)(2,1)S(1)}, u32[]{:S(2)}, u32[]{:S(2)}) collective-permute-start(bf16[288,1536]{1,0:T(8,128)(2,1)S(1)} %pad_maximum_fusion.10), channel_id=1, source_target_pairs={{0,4},{1,5},{2,6},{3,7},{4,0},{5,1},{6,2},{7,3},{8,12},{9,13},{10,... | collective-permute-start | bytes 2654216 | tf_op jit(solution)/shard_map/ppermute | solution.py:24
  51.1 14.5 %collective-permute-start.5 = (bf16[512,384]{1,0:T(8,128)(2,1)S(1)}, bf16[512,384]{1,0:T(8,128)(2,1)S(1)}, u32[]{:S(2)}, u32[]{:S(2)}) collective-permute-start(bf16[512,384]{1,0:T(8,128)(2,1)S(1)} %get-tuple-element.12), channel_id=1, source_target_pairs={{0,8},{8,16},{16,24},{24,32},{32,40},{40,48},{48,56},{56,64},{64,7... | collective-permute-start | bytes 1179656 | tf_op jit(solution)/shard_map/ppermute | solution.py:467
  55.3 17.7 %collective-permute-start.30 = (bf16[384,512]{1,0:T(8,128)(2,1)S(1)}, bf16[384,512]{1,0:T(8,128)(2,1)S(1)}, u32[]{:S(2)}, u32[]{:S(2)}) collective-permute-start(bf16[384,512]{1,0:T(8,128)(2,1)S(1)} %maximum_add_fusion.2), channel_id=1, source_target_pairs={{0,4},{1,5},{2,6},{3,7},{4,0},{5,1},{6,2},{7,3},{8,12},{9,13},{10,... | collective-permute-start | bytes 1179656 | tf_op jit(solution)/shard_map/ppermute | solution.py:24
  57.6 15.5 %collective-permute-start.29 = (bf16[384,512]{1,0:T(8,128)(2,1)S(1)}, bf16[384,512]{1,0:T(8,128)(2,1)S(1)}, u32[]{:S(2)}, u32[]{:S(2)}) collective-permute-start(bf16[384,512]{1,0:T(8,128)(2,1)S(1)} %maximum_add_fusion.1), channel_id=1, source_target_pairs={{0,2},{1,3},{2,0},{3,1},{4,6},{5,7},{6,4},{7,5},{8,10},{9,11},{10,... | collective-permute-start | bytes 1179656 | tf_op jit(solution)/shard_map/ppermute | solution.py:28
  76.4 19.6 %collective-permute-start.8 = (bf16[256,1536]{1,0:T(8,128)(2,1)S(1)}, bf16[256,1536]{1,0:T(8,128)(2,1)S(1)}, u32[]{:S(2)}, u32[]{:S(2)}) collective-permute-start(bf16[256,1536]{1,0:T(8,128)(2,1)S(1)} %get-tuple-element.48), channel_id=1, source_target_pairs={{0,4},{1,5},{2,6},{3,7},{4,0},{5,1},{6,2},{7,3},{8,12},{9,13},{10,... | collective-permute-start | bytes 2359304 | tf_op jit(solution)/shard_map/ppermute | solution.py:24
  79.0 19.0 %collective-permute-start.6 = (bf16[256,1536]{1,0:T(8,128)(2,1)S(1)}, bf16[256,1536]{1,0:T(8,128)(2,1)S(1)}, u32[]{:S(2)}, u32[]{:S(2)}) collective-permute-start(bf16[256,1536]{1,0:T(8,128)(2,1)S(1)} %get-tuple-element.47), channel_id=1, source_target_pairs={{0,2},{1,3},{2,0},{3,1},{4,6},{5,7},{6,4},{7,5},{8,10},{9,11},{10,... | collective-permute-start | bytes 2359304 | tf_op jit(solution)/shard_map/ppermute | solution.py:28
  115.6 10.9 %collective-permute-start.11 = (bf16[128,1536]{1,0:T(8,128)(2,1)S(1)}, bf16[128,1536]{1,0:T(8,128)(2,1)S(1)}, u32[]{:S(2)}, u32[]{:S(2)}) collective-permute-start(bf16[128,1536]{1,0:T(8,128)(2,1)S(1)} %fusion.10), channel_id=1, source_target_pairs={{0,4},{1,5},{2,6},{3,7},{4,0},{5,1},{6,2},{7,3},{8,12},{9,13},{10,... | collective-permute-start | bytes 1179656 | tf_op jit(solution)/shard_map/ppermute | solution.py:24
  121.1 19.1 %collective-permute-start.15 = (bf16[256,1536]{1,0:T(8,128)(2,1)S(1)}, bf16[256,1536]{1,0:T(8,128)(2,1)S(1)}, u32[]{:S(2)}, u32[]{:S(2)}) collective-permute-start(bf16[256,1536]{1,0:T(8,128)(2,1)S(1)} %pad_maximum_fusion.12), channel_id=1, source_target_pairs={{0,4},{1,5},{2,6},{3,7},{4,0},{5,1},{6,2},{7,3},{8,12},{9,13},{10,... | collective-permute-start | bytes 2359304 | tf_op jit(solution)/shard_map/ppermute | solution.py:24
  126.5 14.2 %collective-permute-start.14 = (bf16[256,1536]{1,0:T(8,128)(2,1)S(1)}, bf16[256,1536]{1,0:T(8,128)(2,1)S(1)}, u32[]{:S(2)}, u32[]{:S(2)}) collective-permute-start(bf16[256,1536]{1,0:T(8,128)(2,1)S(1)} %pad_maximum_fusion.11), channel_id=1, source_target_pairs={{0,2},{1,3},{2,0},{3,1},{4,6},{5,7},{6,4},{7,5},{8,10},{9,11},{10,... | collective-permute-start | bytes 2359304 | tf_op jit(solution)/shard_map/ppermute | solution.py:28
  147.6 9.9 %collective-permute-start.16 = (bf16[128,1536]{1,0:T(8,128)(2,1)S(1)}, bf16[128,1536]{1,0:T(8,128)(2,1)S(1)}, u32[]{:S(2)}, u32[]{:S(2)}) collective-permute-start(bf16[128,1536]{1,0:T(8,128)(2,1)S(1)} %get-tuple-element.44), channel_id=1, source_target_pairs={{0,2},{1,3},{2,0},{3,1},{4,6},{5,7},{6,4},{7,5},{8,10},{9,11},{10,... | collective-permute-start | bytes 1179656 | tf_op jit(solution)/shard_map/ppermute | solution.py:28
  209.0 14.1 %collective-permute-start.33 = (bf16[528,384]{1,0:T(8,128)(2,1)S(1)}, bf16[528,384]{1,0:T(8,128)(2,1)S(1)}, u32[]{:S(2)}, u32[]{:S(2)}) collective-permute-start(bf16[528,384]{1,0:T(8,128)(2,1)S(1)} %get-tuple-element.37), channel_id=1, source_target_pairs={{0,16},{8,24},{16,32},{24,40},{32,48},{40,56},{48,0},{56,8},{64,80... | collective-permute-start | bytes 1216520 | tf_op jit(solution)/shard_map/ppermute | solution.py:430
  216.6 12.3 %collective-permute-start.32 = (bf16[528,384]{1,0:T(8,128)(2,1)S(1)}, bf16[528,384]{1,0:T(8,128)(2,1)S(1)}, u32[]{:S(2)}, u32[]{:S(2)}) collective-permute-start(bf16[528,384]{1,0:T(8,128)(2,1)S(1)} %get-tuple-element.38), channel_id=1, source_target_pairs={{0,32},{8,40},{16,48},{24,56},{32,0},{40,8},{48,16},{56,24},{64,96... | collective-permute-start | bytes 1216520 | tf_op jit(solution)/shard_map/ppermute | solution.py:430
  218.7 10.2 %collective-permute-start.31 = (bf16[528,384]{1,0:T(8,128)(2,1)S(1)}, bf16[528,384]{1,0:T(8,128)(2,1)S(1)}, u32[]{:S(2)}, u32[]{:S(2)}) collective-permute-start(bf16[528,384]{1,0:T(8,128)(2,1)S(1)} %get-tuple-element.39), channel_id=1, source_target_pairs={{0,48},{8,56},{16,0},{24,8},{32,16},{40,24},{48,32},{56,40},{64,11... | collective-permute-start | bytes 1216520 | tf_op jit(solution)/shard_map/ppermute | solution.py:430
  230.3 30.0 %collective-permute-start.34 = (bf16[4,528,256]{2,1,0:T(8,128)(2,1)}, bf16[4,528,256]{2,1,0:T(8,128)(2,1)}, u32[]{:S(2)}, u32[]{:S(2)}) collective-permute-start(bf16[4,528,256]{2,1,0:T(8,128)(2,1)} %pad_maximum_fusion.4.kv), channel_id=1, source_target_pairs={{0,64},{8,72},{16,80},{24,88},{32,96},{40,104},{48,112},{56,120},{... | collective-permute-start | bytes 3244040 | tf_op jit(solution)/shard_map/ppermute | solution.py:520
  262.6 24.9 %collective-permute-start.39 = (bf16[256,1536]{1,0:T(8,128)(2,1)S(1)}, bf16[256,1536]{1,0:T(8,128)(2,1)S(1)}, u32[]{:S(2)}, u32[]{:S(2)}) collective-permute-start(bf16[256,1536]{1,0:T(8,128)(2,1)S(1)} %get-tuple-element.42), channel_id=1, source_target_pairs={{0,4},{1,5},{2,6},{3,7},{4,0},{5,1},{6,2},{7,3},{8,12},{9,13},{10,... | collective-permute-start | bytes 2359304 | tf_op jit(solution)/shard_map/ppermute | solution.py:24
  263.6 23.8 %collective-permute-start.37 = (bf16[256,1536]{1,0:T(8,128)(2,1)S(1)}, bf16[256,1536]{1,0:T(8,128)(2,1)S(1)}, u32[]{:S(2)}, u32[]{:S(2)}) collective-permute-start(bf16[256,1536]{1,0:T(8,128)(2,1)S(1)} %get-tuple-element.41), channel_id=1, source_target_pairs={{0,2},{1,3},{2,0},{3,1},{4,6},{5,7},{6,4},{7,5},{8,10},{9,11},{10,... | collective-permute-start | bytes 2359304 | tf_op jit(solution)/shard_map/ppermute | solution.py:28
  287.8 10.5 %collective-permute-start.41 = (bf16[128,1536]{1,0:T(8,128)(2,1)S(1)}, bf16[128,1536]{1,0:T(8,128)(2,1)S(1)}, u32[]{:S(2)}, u32[]{:S(2)}) collective-permute-start(bf16[128,1536]{1,0:T(8,128)(2,1)S(1)} %get-tuple-element.29), channel_id=1, source_target_pairs={{0,3},{1,0},{2,1},{3,2},{4,7},{5,4},{6,5},{7,6},{8,11},{9,8},{10,9... | collective-permute-start | bytes 1179656 | tf_op jit(solution)/shard_map/ppermute | solution.py:28
  288.6 11.3 %collective-permute-start.40 = (bf16[128,1536]{1,0:T(8,128)(2,1)S(1)}, bf16[128,1536]{1,0:T(8,128)(2,1)S(1)}, u32[]{:S(2)}, u32[]{:S(2)}) collective-permute-start(bf16[128,1536]{1,0:T(8,128)(2,1)S(1)} %get-tuple-element.28), channel_id=1, source_target_pairs={{0,1},{1,2},{2,3},{3,0},{4,5},{5,6},{6,7},{7,4},{8,9},{9,10},{10,1... | collective-permute-start | bytes 1179656 | tf_op jit(solution)/shard_map/ppermute | solution.py:28
  289.9 10.0 %collective-permute-start.38 = (bf16[128,1536]{1,0:T(8,128)(2,1)S(1)}, bf16[128,1536]{1,0:T(8,128)(2,1)S(1)}, u32[]{:S(2)}, u32[]{:S(2)}) collective-permute-start(bf16[128,1536]{1,0:T(8,128)(2,1)S(1)} %get-tuple-element.40), channel_id=1, source_target_pairs={{0,4},{1,5},{2,6},{3,7},{4,0},{5,1},{6,2},{7,3},{8,12},{9,13},{10,... | collective-permute-start | bytes 1179656 | tf_op jit(solution)/shard_map/ppermute | solution.py:24
  308.9 23.5 %collective-permute-start.47 = (bf16[1024,512]{1,0:T(8,128)(2,1)}, bf16[1024,512]{1,0:T(8,128)(2,1)}, u32[]{:S(2)}, u32[]{:S(2)}) collective-permute-start(bf16[1024,512]{1,0:T(8,128)(2,1)} %pad_maximum_fusion.8), channel_id=1, source_target_pairs={{0,4},{1,5},{2,6},{3,7},{4,0},{5,1},{6,2},{7,3},{8,12},{9,13},{10,... | collective-permute-start | bytes 3145736 | tf_op jit(solution)/shard_map/ppermute | solution.py:24
  314.0 24.9 %collective-permute-start.45 = (bf16[1024,512]{1,0:T(8,128)(2,1)}, bf16[1024,512]{1,0:T(8,128)(2,1)S(1)}, u32[]{:S(2)}, u32[]{:S(2)}) collective-permute-start(bf16[1024,512]{1,0:T(8,128)(2,1)} %pad_maximum_fusion.7), channel_id=1, source_target_pairs={{0,2},{1,3},{2,0},{3,1},{4,6},{5,7},{6,4},{7,5},{8,10},{9,11},{10,... | collective-permute-start | bytes 3145736 | tf_op jit(solution)/shard_map/ppermute | solution.py:28
  340.5 11.0 %collective-permute-start.49 = (bf16[512,512]{1,0:T(8,128)(2,1)S(1)}, bf16[512,512]{1,0:T(8,128)(2,1)S(1)}, u32[]{:S(2)}, u32[]{:S(2)}) collective-permute-start(bf16[512,512]{1,0:T(8,128)(2,1)S(1)} %get-tuple-element.25), channel_id=1, source_target_pairs={{0,3},{1,0},{2,1},{3,2},{4,7},{5,4},{6,5},{7,6},{8,11},{9,8},{10,9... | collective-permute-start | bytes 1572872 | tf_op jit(solution)/shard_map/ppermute | solution.py:28
  342.0 11.7 %collective-permute-start.48 = (bf16[512,512]{1,0:T(8,128)(2,1)S(1)}, bf16[512,512]{1,0:T(8,128)(2,1)S(1)}, u32[]{:S(2)}, u32[]{:S(2)}) collective-permute-start(bf16[512,512]{1,0:T(8,128)(2,1)S(1)} %get-tuple-element.24), channel_id=1, source_target_pairs={{0,1},{1,2},{2,3},{3,0},{4,5},{5,6},{6,7},{7,4},{8,9},{9,10},{10,1... | collective-permute-start | bytes 1572872 | tf_op jit(solution)/shard_map/ppermute | solution.py:28
  342.6 11.1 %collective-permute-start.46 = (bf16[512,512]{1,0:T(8,128)(2,1)S(1)}, bf16[512,512]{1,0:T(8,128)(2,1)S(1)}, u32[]{:S(2)}, u32[]{:S(2)}) collective-permute-start(bf16[512,512]{1,0:T(8,128)(2,1)S(1)} %get-tuple-element.32), channel_id=1, source_target_pairs={{0,4},{1,5},{2,6},{3,7},{4,0},{5,1},{6,2},{7,3},{8,12},{9,13},{10,... | collective-permute-start | bytes 1572872 | tf_op jit(solution)/shard_map/ppermute | solution.py:24
  (39 other events, 265.9 us)
Sparse Core Ops, SparseCore 0:
  74.7 66.6 all-gather.1
